TPU v7x, 32 devices: a whole 2x2x4 slice. The times are simulated.
32 devices in a mesh: dp: 8 (over y, x, core), fsdp: 4 (over z).
Axes of the slice: x: 2, y: 2, z: 4, core: 2. Of those that a mesh axis runs over, the one named last changes fastest.
Arguments:
- tokens: bfloat16 [32, 512, 1024], P(('dp', 'fsdp')), may hold values from -6 to 6
- lengths: int32 [32], P(('dp', 'fsdp')), may hold values from 128 to 512, as said below
- span_starts: int32 [32, 5], P(('dp', 'fsdp')), may hold values from 0 to 502
- mask_embed: bfloat16 [1024], P('fsdp'), may hold values from -6 to 6
- norm_gains: bfloat16 [5, 1024], P(None, 'fsdp'), may hold values from 0.099609375 to 1.8984375
- ffn1_in: bfloat16 [1024, 4096], P('fsdp'), may hold values from -0.1875 to 0.1875
- ffn1_out: bfloat16 [4096, 1024], P('fsdp'), may hold values from -0.09375 to 0.09375
- attn_in: bfloat16 [1024, 3072], P('fsdp'), may hold values from -0.1875 to 0.1875
- attn_out: bfloat16 [1024, 1024], P('fsdp'), may hold values from -0.75 to 0.75
- conv_in: bfloat16 [1024, 2048], P('fsdp'), may hold values from -0.1875 to 0.1875
- conv_out: bfloat16 [1024, 1024], P('fsdp'), may hold values from -0.1875 to 0.1875
- depth: bfloat16 [5, 1024], P(None, 'fsdp'), may hold values from -2.5 to 2.5
- bn_affine: bfloat16 [2, 1024], P(None, 'fsdp'), may hold values from 0.5 to 1.5
- ffn2_in: bfloat16 [1024, 4096], P('fsdp'), may hold values from -0.1875 to 0.1875
- ffn2_out: bfloat16 [4096, 1024], P('fsdp'), may hold values from -0.09375 to 0.09375
- cotangent: bfloat16 [32, 512, 1024], P(('dp', 'fsdp')), may hold values from -6 to 6
Outputs:
- output: bfloat16 [32, 512, 1024], P(('dp', 'fsdp'))
- input_grad: bfloat16 [32, 512, 1024], P(('dp', 'fsdp'))
- mask_embed_grad: float32 [1024], P('fsdp')
- norm_gains_grad: float32 [5, 1024], P(None, 'fsdp')
- ffn1_in_grad: float32 [1024, 4096], P('fsdp')
- ffn1_out_grad: float32 [4096, 1024], P('fsdp')
- attn_in_grad: float32 [1024, 3072], P('fsdp')
- attn_out_grad: float32 [1024, 1024], P('fsdp')
- conv_in_grad: float32 [1024, 2048], P('fsdp')
- conv_out_grad: float32 [1024, 1024], P('fsdp')
- depth_grad: float32 [5, 1024], P(None, 'fsdp')
- bn_affine_grad: float32 [2, 1024], P(None, 'fsdp')
- ffn2_in_grad: float32 [1024, 4096], P('fsdp')
- ffn2_out_grad: float32 [4096, 1024], P('fsdp')
Inputs may be any that keep to these rules, and one draw needn't show every extreme that they name: `lengths`: some utterance fills all 512 slots in every draw.
All inputs are finite; a program needn't handle non-finite values.
Results may differ from a plain program's by a relative error of at most 0.02.
Values may be sent and summed in bfloat16 or wider, within the bound.
A program may use at most 256 MiB of HBM per device.

v0:
```python
import jax
import jax.numpy as jnp
from jax import lax
from jax.sharding import PartitionSpec as P

HEAD = 128
KER = 5
SPAN_LEN = 10


EPSILON = 1e-05
NEGATIVE = -1000000000.0


def product(left_side, right_side):
    return jnp.dot(left_side, right_side, preferred_element_type=jnp.float32)


def product_tn(left_side, right_side):
    return lax.dot_general(
        left_side, right_side, (((0,), (0,)), ((), ())), preferred_element_type=jnp.float32
    )


def product_nt(left_side, right_side):
    return lax.dot_general(
        left_side, right_side, (((1,), (1,)), ((), ())), preferred_element_type=jnp.float32
    )


def layer_norm(inputs, layer_gain):
    average = jnp.mean(inputs, axis=-1, keepdims=True)
    centered = inputs - average
    inverse = lax.rsqrt(jnp.mean(centered * centered, axis=-1, keepdims=True) + EPSILON)
    normed = centered * inverse
    return (normed * layer_gain, normed, inverse)


def norm_back(upstream, layer_gain, normed, inverse):
    scaled = upstream * layer_gain
    first_mean = jnp.mean(scaled, axis=-1, keepdims=True)
    second_mean = jnp.mean(scaled * normed, axis=-1, keepdims=True)
    return (
        inverse * (scaled - first_mean - normed * second_mean),
        jnp.sum(upstream * normed, axis=0),
    )


def swish_slope(inputs):
    sigmoid_part = jax.nn.sigmoid(inputs)
    return sigmoid_part * (1.0 + inputs * (1.0 - sigmoid_part))


def rotation(frame_count):
    half_size = HEAD // 2
    position = jnp.arange(frame_count, dtype=jnp.float32)
    frequency = 10000.0 ** (-jnp.arange(half_size, dtype=jnp.float32) / half_size)
    angles = position[:, None] * frequency[None, :]
    return (jnp.cos(angles)[:, None, :], jnp.sin(angles)[:, None, :])


def rotate(inputs, cosine, sine):
    half_size = HEAD // 2
    front = inputs[..., :half_size]
    back_half = inputs[..., half_size:]
    return jnp.concatenate(
        [front * cosine - back_half * sine, front * sine + back_half * cosine], axis=-1
    )


def unrotate(inputs, cosine, sine):
    half_size = HEAD // 2
    front = inputs[..., :half_size]
    back_half = inputs[..., half_size:]
    return jnp.concatenate(
        [front * cosine + back_half * sine, back_half * cosine - front * sine], axis=-1
    )


def fetch(weight_in, weight_out, small_part):
    return (
        lax.all_gather(weight_in, "fsdp", axis=0, tiled=True),
        lax.all_gather(weight_out, "fsdp", axis=0, tiled=True),
        lax.all_gather(small_part, "fsdp", axis=1, tiled=True),
    )


def fetch_again(weight_in, weight_out, small_part):
    return (
        lax.all_gather(weight_in, "fsdp", axis=0, tiled=True),
        lax.all_gather(weight_out, "fsdp", axis=0, tiled=True),
        lax.all_gather(small_part, "fsdp", axis=1, tiled=True),
    )


def reduce_grads(grad_in, grad_out, small_grad):
    shards = (
        lax.psum_scatter(
            grad_in.astype(jnp.bfloat16), "fsdp", scatter_dimension=0, tiled=True
        ).astype(jnp.float32),
        lax.psum_scatter(
            grad_out.astype(jnp.bfloat16), "fsdp", scatter_dimension=0, tiled=True
        ).astype(jnp.float32),
        lax.psum_scatter(
            small_grad.astype(jnp.bfloat16), "fsdp", scatter_dimension=1, tiled=True
        ).astype(jnp.float32),
    )
    return (
        lax.psum(shards[0].astype(jnp.bfloat16), "dp").astype(jnp.float32),
        lax.psum(shards[1].astype(jnp.bfloat16), "dp").astype(jnp.float32),
        lax.psum(shards[2].astype(jnp.bfloat16), "dp").astype(jnp.float32),
    )


def ffn_forward(inputs, layer_gain, weight_in, weight_out):
    out_norm, normed, inverse = layer_norm(inputs, layer_gain)
    hidden = out_norm.astype(jnp.bfloat16)
    inner = product(hidden, weight_in)
    active = jax.nn.silu(inner).astype(jnp.bfloat16)
    return (product(active, weight_out), (hidden, normed, inverse, inner, active))


def ffn_backward(upstream, stored, layer_gain, weight_in, weight_out):
    hidden, normed, inverse, inner, active = stored
    branch_grad = (0.5 * upstream).astype(jnp.bfloat16)
    grad_out = product_tn(active, branch_grad)
    active_grad = product_nt(branch_grad, weight_out)
    inner_grad = (active_grad * swish_slope(inner)).astype(jnp.bfloat16)
    grad_in = product_tn(hidden, inner_grad)
    norm_grad, gain_grad = norm_back(product_nt(inner_grad, weight_in), layer_gain, normed, inverse)
    return (upstream + norm_grad, grad_in, grad_out, gain_grad)


def attention_scores(queries, keys_rot, key_live):
    raw_scores = jnp.einsum(
        "uqhd,ukhd->uhqk", queries, keys_rot, preferred_element_type=jnp.float32
    )
    return jnp.where(key_live[:, None, None, :], raw_scores * HEAD ** (-0.5), NEGATIVE)


def attention_forward(inputs, layer_gain, weight_in, weight_out, key_live, tables, units):
    row_count, model_width = inputs.shape
    shape_heads = (units, row_count // units, model_width // HEAD, HEAD)
    out_norm, normed, inverse = layer_norm(inputs, layer_gain)
    hidden = out_norm.astype(jnp.bfloat16)
    joined = product(hidden, weight_in)
    queries = rotate(joined[:, :model_width].reshape(shape_heads), tables[0], tables[1]).astype(
        jnp.bfloat16
    )
    keys_rot = rotate(
        joined[:, model_width : 2 * model_width].reshape(shape_heads), tables[0], tables[1]
    ).astype(jnp.bfloat16)
    values_low = joined[:, 2 * model_width :].reshape(shape_heads).astype(jnp.bfloat16)
    scores = attention_scores(queries, keys_rot, key_live)
    top_score = jnp.max(scores, axis=-1, keepdims=True)
    log_total = top_score + jnp.log(jnp.sum(jnp.exp(scores - top_score), axis=-1, keepdims=True))
    probs_low = jnp.exp(scores - log_total).astype(jnp.bfloat16)
    heads_out = jnp.einsum(
        "uhqk,ukhd->uqhd", probs_low, values_low, preferred_element_type=jnp.float32
    )
    merged = heads_out.reshape(row_count, model_width).astype(jnp.bfloat16)
    return (
        product(merged, weight_out),
        (hidden, normed, inverse, queries, keys_rot, values_low, log_total, merged),
    )


def attention_backward(upstream, stored, layer_gain, weight_in, weight_out, key_live, tables):
    hidden, normed, inverse, queries, keys_rot, values_low, log_total, merged = stored
    row_count, model_width = upstream.shape
    branch_grad = upstream.astype(jnp.bfloat16)
    grad_out = product_tn(merged, branch_grad)
    merged_grad = product_nt(branch_grad, weight_out).astype(jnp.bfloat16).reshape(queries.shape)
    probs = jnp.exp(attention_scores(queries, keys_rot, key_live) - log_total)
    prob_grad = jnp.einsum(
        "uqhd,ukhd->uhqk", merged_grad, values_low, preferred_element_type=jnp.float32
    )
    value_grad = jnp.einsum(
        "uhqk,uqhd->ukhd",
        probs.astype(jnp.bfloat16),
        merged_grad,
        preferred_element_type=jnp.float32,
    )
    row_term = jnp.sum(probs * prob_grad, axis=-1, keepdims=True)
    score_grad = (probs * (prob_grad - row_term) * HEAD ** (-0.5)).astype(jnp.bfloat16)
    query_grad = unrotate(
        jnp.einsum("uhqk,ukhd->uqhd", score_grad, keys_rot, preferred_element_type=jnp.float32),
        tables[0],
        tables[1],
    )
    key_grad = unrotate(
        jnp.einsum("uhqk,uqhd->ukhd", score_grad, queries, preferred_element_type=jnp.float32),
        tables[0],
        tables[1],
    )
    joined_grad = jnp.concatenate(
        [
            query_grad.reshape(row_count, model_width),
            key_grad.reshape(row_count, model_width),
            value_grad.reshape(row_count, model_width),
        ],
        axis=1,
    ).astype(jnp.bfloat16)
    grad_in = product_tn(hidden, joined_grad)
    norm_grad, gain_grad = norm_back(
        product_nt(joined_grad, weight_in), layer_gain, normed, inverse
    )
    return (upstream + norm_grad, grad_in, grad_out, gain_grad)


def conv_forward(inputs, layer_gain, weight_in, weight_out, small_low, live, units):
    row_count, model_width = inputs.shape
    frame_count = row_count // units
    out_norm, normed, inverse = layer_norm(inputs, layer_gain)
    hidden = out_norm.astype(jnp.bfloat16)
    proj = product(hidden, weight_in)
    linear_part = proj[:, :model_width]
    gate_part = jax.nn.sigmoid(proj[:, model_width:])
    glu = (linear_part * gate_part * live).reshape(units, frame_count, model_width)
    side = KER // 2
    padded = jnp.pad(glu, ((0, 0), (side, side), (0, 0)))
    kernel = small_low[1 : KER + 1].astype(jnp.float32)
    mixed = kernel[0] * padded[:, 0:frame_count]
    for offset in range(1, KER):
        mixed = mixed + kernel[offset] * padded[:, offset : offset + frame_count]
    mixed = mixed.reshape(row_count, model_width)
    local_sum = jnp.sum(mixed * live, axis=0)
    local_count = jnp.sum(live)
    total_sum, count = lax.psum((local_sum, local_count), ("dp", "fsdp"))
    bmean = total_sum / count
    deviation = mixed - bmean
    bvar = lax.psum(jnp.sum(deviation * deviation * live, axis=0), ("dp", "fsdp")) / count
    bn_inverse = lax.rsqrt(bvar + EPSILON)
    bn_normed = (mixed - bmean) * bn_inverse
    pre_act = small_low[KER + 1].astype(jnp.float32) * bn_normed + small_low[KER + 2].astype(
        jnp.float32
    )
    active = jax.nn.silu(pre_act).astype(jnp.bfloat16)
    stored = (
        hidden,
        normed,
        inverse,
        linear_part,
        gate_part,
        padded,
        bn_normed,
        bn_inverse,
        count,
        pre_act,
        active,
    )
    return (product(active, weight_out), stored)


def conv_backward(upstream, stored, layer_gain, weight_in, weight_out, small_low, live, units):
    (
        hidden,
        normed,
        inverse,
        linear_part,
        gate_part,
        padded,
        bn_normed,
        bn_inverse,
        count,
        pre_act,
        active,
    ) = stored
    row_count, model_width = upstream.shape
    frame_count = row_count // units
    kernel = small_low[1 : KER + 1].astype(jnp.float32)
    bn_scale = small_low[KER + 1].astype(jnp.float32)
    branch_grad = upstream.astype(jnp.bfloat16)
    grad_out = product_tn(active, branch_grad)
    pre_grad = product_nt(branch_grad, weight_out) * swish_slope(pre_act)
    shift_total, scale_total = lax.psum(
        (jnp.sum(pre_grad, axis=0), jnp.sum(pre_grad * bn_normed, axis=0)), ("dp", "fsdp")
    )
    mixed_grad = bn_inverse * (
        bn_scale * pre_grad
        - live * (bn_scale * shift_total) / count
        - live * bn_normed * (bn_scale * scale_total) / count
    )
    side = KER // 2
    grid_grad = mixed_grad.reshape(units, frame_count, model_width)
    grad_padded = jnp.pad(grid_grad, ((0, 0), (side, side), (0, 0)))
    last_tap = KER - 1
    glu_grad = kernel[0] * grad_padded[:, last_tap : last_tap + frame_count]
    for offset in range(1, KER):
        glu_grad = (
            glu_grad
            + kernel[offset] * grad_padded[:, last_tap - offset : last_tap - offset + frame_count]
        )
    kernel_grad = jnp.stack(
        [
            jnp.sum(padded[:, offset : offset + frame_count] * grid_grad, axis=(0, 1))
            for offset in range(KER)
        ]
    )
    glu_grad = glu_grad.reshape(row_count, model_width) * live
    proj_grad = jnp.concatenate(
        [glu_grad * gate_part, glu_grad * linear_part * gate_part * (1.0 - gate_part)], axis=1
    ).astype(jnp.bfloat16)
    grad_in = product_tn(hidden, proj_grad)
    norm_grad, gain_grad = norm_back(product_nt(proj_grad, weight_in), layer_gain, normed, inverse)
    return (
        upstream + norm_grad,
        grad_in,
        grad_out,
        gain_grad,
        kernel_grad,
        jnp.stack([scale_total, shift_total]),
    )


def local(
    tokens,
    lengths,
    span_starts,
    mask_embed,
    norm_gains,
    ffn1_in,
    ffn1_out,
    attn_in,
    attn_out,
    conv_in,
    conv_out,
    depth,
    bn_affine,
    ffn2_in,
    ffn2_out,
    cotangent,
):
    units, frame_count, model_width = tokens.shape
    row_count = units * frame_count
    position = jnp.arange(frame_count, dtype=jnp.int32)
    valid = position[None, :] < lengths[:, None]
    inside = (position[None, None, :] >= span_starts[:, :, None]) & (
        position[None, None, :] < span_starts[:, :, None] + SPAN_LEN
    )
    masked = jnp.any(inside, axis=1) & valid
    live = valid.reshape(row_count, 1).astype(jnp.float32)
    masked_col = masked.reshape(row_count, 1)
    tables = rotation(frame_count)
    first_small = jnp.concatenate([norm_gains[0:1], mask_embed[None, :]], axis=0)
    second_small = norm_gains[1:2]
    third_small = jnp.concatenate([norm_gains[2:3], depth, bn_affine], axis=0)
    fourth_small = norm_gains[3:5]
    first_weights = fetch(ffn1_in, ffn1_out, first_small)
    gain_one = first_weights[2][0].astype(jnp.float32)
    embed = first_weights[2][1].astype(jnp.float32)
    start = jnp.where(masked_col, embed, tokens.reshape(row_count, model_width).astype(jnp.float32))
    branch, first_stored = ffn_forward(start, gain_one, first_weights[0], first_weights[1])
    first = start + 0.5 * branch
    second_weights = fetch(attn_in, attn_out, second_small)
    gain_two = second_weights[2][0].astype(jnp.float32)
    branch, second_stored = attention_forward(
        first, gain_two, second_weights[0], second_weights[1], valid, tables, units
    )
    second = first + branch
    third_weights = fetch(conv_in, conv_out, third_small)
    gain_three = third_weights[2][0].astype(jnp.float32)
    branch, third_stored = conv_forward(
        second, gain_three, third_weights[0], third_weights[1], third_weights[2], live, units
    )
    third = second + branch
    fourth_weights = fetch(ffn2_in, ffn2_out, fourth_small)
    gain_four = fourth_weights[2][0].astype(jnp.float32)
    gain_five = fourth_weights[2][1].astype(jnp.float32)
    branch, fourth_stored = ffn_forward(third, gain_four, fourth_weights[0], fourth_weights[1])
    fourth = third + 0.5 * branch
    out_norm, final_normed, final_inverse = layer_norm(fourth, gain_five)
    output = out_norm.astype(jnp.bfloat16).reshape(units, frame_count, model_width)
    upstream = cotangent.reshape(row_count, model_width).astype(jnp.float32)
    grad_four, gain_five_grad = norm_back(upstream, gain_five, final_normed, final_inverse)
    fourth_back = fetch_again(ffn2_in, ffn2_out, fourth_small)
    grad_three, grad_in, grad_out, gain_four_grad = ffn_backward(
        grad_four, fourth_stored, gain_four, fourth_back[0], fourth_back[1]
    )
    fourth_red = reduce_grads(grad_in, grad_out, jnp.stack([gain_four_grad, gain_five_grad]))
    third_back = fetch_again(conv_in, conv_out, third_small)
    grad_two, grad_in, grad_out, gain_three_grad, kernel_grad, affine_full = conv_backward(
        grad_three,
        third_stored,
        gain_three,
        third_back[0],
        third_back[1],
        third_weights[2],
        live,
        units,
    )
    third_red = reduce_grads(
        grad_in, grad_out, jnp.concatenate([gain_three_grad[None, :], kernel_grad], axis=0)
    )
    second_back = fetch_again(attn_in, attn_out, second_small)
    grad_one, grad_in, grad_out, gain_two_grad = attention_backward(
        grad_two, second_stored, gain_two, second_back[0], second_back[1], valid, tables
    )
    second_red = reduce_grads(grad_in, grad_out, gain_two_grad[None, :])
    first_back = fetch_again(ffn1_in, ffn1_out, first_small)
    grad_zero, grad_in, grad_out, gain_one_grad = ffn_backward(
        grad_one, first_stored, gain_one, first_back[0], first_back[1]
    )
    masked_float = masked_col.astype(jnp.float32)
    embed_grad = jnp.sum(grad_zero * masked_float, axis=0)
    input_grad = (
        (grad_zero * (1.0 - masked_float))
        .astype(jnp.bfloat16)
        .reshape(units, frame_count, model_width)
    )
    first_red = reduce_grads(grad_in, grad_out, jnp.stack([gain_one_grad, embed_grad]))
    column_width = norm_gains.shape[1]
    affine_grad = lax.dynamic_slice_in_dim(
        affine_full, lax.axis_index("fsdp") * column_width, column_width, 1
    )
    gains_grad = jnp.concatenate(
        [first_red[2][0:1], second_red[2], third_red[2][0:1], fourth_red[2]], axis=0
    )
    return (
        output,
        input_grad,
        first_red[2][1],
        gains_grad,
        first_red[0],
        first_red[1],
        second_red[0],
        second_red[1],
        third_red[0],
        third_red[1],
        third_red[2][1:],
        affine_grad,
        fourth_red[0],
        fourth_red[1],
    )


def solution(mesh):
    in_specs = (
        P(("dp", "fsdp"), None, None),
        P(("dp", "fsdp")),
        P(("dp", "fsdp"), None),
        P("fsdp"),
        P(None, "fsdp"),
        P("fsdp", None),
        P("fsdp", None),
        P("fsdp", None),
        P("fsdp", None),
        P("fsdp", None),
        P("fsdp", None),
        P(None, "fsdp"),
        P(None, "fsdp"),
        P("fsdp", None),
        P("fsdp", None),
        P(("dp", "fsdp"), None, None),
    )
    out_specs = (
        P(("dp", "fsdp"), None, None),
        P(("dp", "fsdp"), None, None),
        P("fsdp"),
        P(None, "fsdp"),
        P("fsdp", None),
        P("fsdp", None),
        P("fsdp", None),
        P("fsdp", None),
        P("fsdp", None),
        P("fsdp", None),
        P(None, "fsdp"),
        P(None, "fsdp"),
        P("fsdp", None),
        P("fsdp", None),
    )
    return jax.shard_map(local, mesh=mesh, in_specs=in_specs, out_specs=out_specs, check_vma=False)
```

profile of v0, /device:TPU:0, one launch (start us, length us, event | category | flops | bytes accessed | tf_op | source)
XLA Modules:
  0.0 2153.4 jit_solution(11857282383305734538)
XLA Ops:
  12.8 14.9 all_gather.50
  53.4 20.1 all_gather.53
  73.5 88.7 %all-gather.9.cloned.1.call-done = bf16[1024,4096]{1,0:T(8,128)(2,1)} async-done(((bf16[256,4096]{1,0:T(8,128)(2,1)}), bf16[1024,4096]{1,0:T(8,128)(2,1)}) %all-gather.9.cloned.1.call-update) | async-done | bytes 8388624 | tf_op jit(solution)/shard_map/all_gather | solution.py:82
  172.6 139.0 %all-gather.11.cloned.1.call-done = bf16[4096,1024]{1,0:T(8,128)(2,1)} async-done(((bf16[1024,1024]{1,0:T(8,128)(2,1)}), bf16[4096,1024]{1,0:T(8,128)(2,1)}) %all-gather.11.cloned.1.call-update) | async-done | bytes 8388624 | tf_op jit(solution)/shard_map/all_gather | solution.py:83
  321.7 105.1 %all-gather.13.cloned.1.call-done = bf16[1024,3072]{1,0:T(8,128)(2,1)} async-done(((bf16[256,3072]{1,0:T(8,128)(2,1)}), bf16[1024,3072]{1,0:T(8,128)(2,1)}) %all-gather.13.cloned.1.call-update) | async-done | bytes 6291472 | tf_op jit(solution)/shard_map/all_gather | solution.py:82
  446.1 26.3 %all-gather.15.cloned.1.call-done = bf16[1024,1024]{1,0:T(8,128)(2,1)} async-done(((bf16[256,1024]{1,0:T(8,128)(2,1)}), bf16[1024,1024]{1,0:T(8,128)(2,1)}) %all-gather.15.cloned.1.call-update) | async-done | bytes 2097168 | tf_op jit(solution)/shard_map/all_gather | solution.py:83
  477.0 76.3 %all-gather.17.cloned.1.call-done = bf16[1024,2048]{1,0:T(8,128)(2,1)} async-done(((bf16[256,2048]{1,0:T(8,128)(2,1)}), bf16[1024,2048]{1,0:T(8,128)(2,1)}) %all-gather.17.cloned.1.call-update) | async-done | bytes 4194320 | tf_op jit(solution)/shard_map/all_gather | solution.py:82
  562.6 42.2 %all-reduce.3 = (f32[1024]{0:T(1024)S(1)}, f32[]{:T(128)}) all-reduce(f32[1024]{0:T(1024)S(1)} %get-tuple-element.59, f32[]{:T(128)} %fusion.89), channel_id=1, replica_groups=mesh['dp'=8,'fsdp'=4] {'dp','fsdp'}, use_global_device_ids=true, to_apply=%region_10.11 | all-reduce | flops 1025 | bytes 8200 | tf_op jit(solution)/shard_map/psum | solution.py:229
  605.7 48.0 %psum.121 = f32[1024]{0:T(1024)S(1)} all-reduce(f32[1024]{0:T(1024)S(1)} %multiply_reduce_fusion.16), channel_id=1, replica_groups=mesh['dp'=8,'fsdp'=4] {'dp','fsdp'}, use_global_device_ids=true, to_apply=%region_14.15 | all-reduce | flops 1024 | bytes 8192 | tf_op jit(solution)/shard_map/psum | solution.py:232
  659.9 91.4 %all-gather.21.cloned.1.call-done = bf16[1024,4096]{1,0:T(8,128)(2,1)} async-done(((bf16[256,4096]{1,0:T(8,128)(2,1)}), bf16[1024,4096]{1,0:T(8,128)(2,1)}) %all-gather.21.cloned.1.call-update) | async-done | bytes 8388624 | tf_op jit(solution)/shard_map/all_gather | solution.py:82
  763.5 137.2 %all-gather.23.cloned.1.call-done = bf16[4096,1024]{1,0:T(8,128)(2,1)} async-done(((bf16[1024,1024]{1,0:T(8,128)(2,1)}), bf16[4096,1024]{1,0:T(8,128)(2,1)}) %all-gather.23.cloned.1.call-update) | async-done | bytes 8388624 | tf_op jit(solution)/shard_map/all_gather | solution.py:83
  941.7 38.7 %all-reduce.2 = (f32[1024]{0:T(1024)S(1)}, f32[1024]{0:T(1024)S(1)}) all-reduce(f32[1024]{0:T(1024)S(1)} %get-tuple-element.33, f32[1024]{0:T(1024)S(1)} %get-tuple-element.32), channel_id=1, replica_groups=mesh['dp'=8,'fsdp'=4] {'dp','fsdp'}, use_global_device_ids=true, to_apply=%region_26.27 | all-reduce | flops 2048 | bytes 16384 | tf_op jit(solution)/shard_map/psum | solution.py:276
  1024.6 16.1 fusion.60
  1040.7 18.0 fusion.63
  1176.6 104.5 %reduce-scatter.25.cloned.1.call-done = bf16[256,3072]{1,0:T(8,128)(2,1)} async-done(((bf16[1024,3072]{1,0:T(8,128)(2,1)}), bf16[256,3072]{1,0:T(8,128)(2,1)}) %reduce-scatter.25.cloned.1.call-update) | async-done | bytes 1572880 | tf_op jit(solution)/shard_map/reduce_scatter | solution.py:98
  1281.1 147.5 %reduce-scatter.21.cloned.1.call-done = bf16[256,4096]{1,0:T(8,128)(2,1)} async-done(((bf16[1024,4096]{1,0:T(8,128)(2,1)}), bf16[256,4096]{1,0:T(8,128)(2,1)}) %reduce-scatter.21.cloned.1.call-update) | async-done | bytes 2097168 | tf_op jit(solution)/shard_map/reduce_scatter | solution.py:98
  1428.6 147.6 %reduce-scatter.23.cloned.1.call-done = bf16[1024,1024]{1,0:T(8,128)(2,1)} async-done(((bf16[4096,1024]{1,0:T(8,128)(2,1)}), bf16[1024,1024]{1,0:T(8,128)(2,1)}) %reduce-scatter.23.cloned.1.call-update) | async-done | bytes 2097168 | tf_op jit(solution)/shard_map/reduce_scatter | solution.py:101
  1576.2 147.5 %reduce-scatter.33.cloned.1.call-done = bf16[256,4096]{1,0:T(8,128)(2,1)} async-done(((bf16[1024,4096]{1,0:T(8,128)(2,1)}), bf16[256,4096]{1,0:T(8,128)(2,1)}) %reduce-scatter.33.cloned.1.call-update) | async-done | bytes 2097168 | tf_op jit(solution)/shard_map/reduce_scatter | solution.py:98
  1723.7 147.5 %reduce-scatter.35.cloned.1.call-done = bf16[1024,1024]{1,0:T(8,128)(2,1)} async-done(((bf16[4096,1024]{1,0:T(8,128)(2,1)}), bf16[1024,1024]{1,0:T(8,128)(2,1)}) %reduce-scatter.35.cloned.1.call-update) | async-done | bytes 2097168 | tf_op jit(solution)/shard_map/reduce_scatter | solution.py:101
  1874.0 20.4 reduce-scatter.39.cloned.1.call-done
  1895.4 19.6 reduce-scatter.37.cloned.1.call-done
  1915.9 20.0 reduce-scatter.41.cloned.1.call-done
  1936.8 18.9 reduce-scatter.19.cloned.1.call-done
  1969.8 158.8 %all-reduce.8.cloned.1.call-done = (bf16[256,4096]{1,0:T(8,128)(2,1)}, bf16[1024,1024]{1,0:T(8,128)(2,1)}, bf16[256,3072]{1,0:T(8,128)(2,1)}, bf16[256,1024]{1,0...) async-done(((bf16[256,4096]{1,0:T(8,128)(2,1)}, bf16[1024,1024]{1,0:T(8,128)(2,1)}, ...) | async-done | bytes 12058640 | tf_op jit(solution)/shard_map/psum | solution.py:109
  (346 shorter events, 342.6 us)
Async XLA Ops:
  7.2 155.0 %all-gather.9.cloned.1.call-start = ((), (), s32[]{:S(2)}) async-start(), calls=%async_computation.12 | async-start | bytes 10485760 | tf_op jit(solution)/shard_map/all_gather | solution.py:82
  7.9 303.7 %all-gather.11.cloned.1.call-start = ((), (), s32[]{:S(2)}) async-start(), calls=%async_computation.13 | async-start | bytes 10485760 | tf_op jit(solution)/shard_map/all_gather | solution.py:83
  8.7 418.1 %all-gather.13.cloned.1.call-start = ((), (), s32[]{:S(2)}) async-start(), calls=%async_computation.14 | async-start | bytes 7864320 | tf_op jit(solution)/shard_map/all_gather | solution.py:82
  9.4 463.0 %all-gather.15.cloned.1.call-start = ((), (), s32[]{:S(2)}) async-start(), calls=%async_computation.15 | async-start | bytes 2621440 | tf_op jit(solution)/shard_map/all_gather | solution.py:83
  10.0 543.4 %all-gather.17.cloned.1.call-start = ((), (), s32[]{:S(2)}) async-start(), calls=%async_computation.16 | async-start | bytes 5242880 | tf_op jit(solution)/shard_map/all_gather | solution.py:82
  10.6 643.8 %all-gather.19.cloned.1.call-start = ((), (), s32[]{:S(2)}) async-start(), calls=%async_computation.17 | async-start | bytes 2621440 | tf_op jit(solution)/shard_map/all_gather | solution.py:83
  11.2 740.0 %all-gather.21.cloned.1.call-start = ((), (), s32[]{:S(2)}) async-start(), calls=%async_computation.18 | async-start | bytes 10485760 | tf_op jit(solution)/shard_map/all_gather | solution.py:82
  11.9 888.7 %all-gather.23.cloned.1.call-start = ((), (), s32[]{:S(2)}) async-start(), calls=%async_computation.19 | async-start | bytes 10485760 | tf_op jit(solution)/shard_map/all_gather | solution.py:83
  12.7 1163.9 %reduce-scatter.27.cloned.1.call-start = ((), (), s32[]{:S(2)}) async-start(), calls=%async_computation.24 | async-start | bytes 2621440 | tf_op jit(solution)/shard_map/reduce_scatter | solution.py:101
  40.4 271.2 %copy-start.44 = (f32[1,1024]{1,0:T(1,128)}, f32[1,1024]{1,0:T(1,128)S(1)}, u32[]{:S(2)}) copy-start(f32[1,1024]{1,0:T(1,128)S(1)} %get-tuple-element.97) | copy-start | bytes 12292
  41.7 269.9 %copy-start.58 = (pred[512]{0:T(512)(128)(4,1)}, pred[512]{0:T(512)(128)(4,1)S(1)}, u32[]{:S(2)}) copy-start(pred[512]{0:T(512)(128)(4,1)S(1)} %get-tuple-element.56) | copy-start | bytes 1540
  51.1 375.7 %copy-start.52 = (f32[1,1024]{1,0:T(1,128)}, f32[1,1024]{1,0:T(1,128)S(1)}, u32[]{:S(2)}) copy-start(f32[1,1024]{1,0:T(1,128)S(1)} %mul.953) | copy-start | bytes 12292
  999.1 177.4 %reduce-scatter.31.cloned.1.call-start = ((), (), s32[]{:S(2)}) async-start(), calls=%async_computation.26 | async-start | bytes 2621440 | tf_op jit(solution)/shard_map/reduce_scatter | solution.py:101
  1004.3 172.3 %reduce-scatter.29.cloned.1.call-start = ((), (), s32[]{:S(2)}) async-start(), calls=%async_computation.25 | async-start | bytes 5242880 | tf_op jit(solution)/shard_map/reduce_scatter | solution.py:98
  1011.1 270.0 %reduce-scatter.25.cloned.1.call-start = ((), (), s32[]{:S(2)}) async-start(), calls=%async_computation.23 | async-start | bytes 7864320 | tf_op jit(solution)/shard_map/reduce_scatter | solution.py:98
  1089.6 339.0 %reduce-scatter.21.cloned.1.call-start = ((), (), s32[]{:S(2)}) async-start(), calls=%async_computation.21 | async-start | bytes 10485760 | tf_op jit(solution)/shard_map/reduce_scatter | solution.py:98
  1120.6 455.6 %reduce-scatter.23.cloned.1.call-start = ((), (), s32[]{:S(2)}) async-start(), calls=%async_computation.22 | async-start | bytes 10485760 | tf_op jit(solution)/shard_map/reduce_scatter | solution.py:101
  1132.8 591.0 %reduce-scatter.33.cloned.1.call-start = ((), (), s32[]{:S(2)}) async-start(), calls=%async_computation.27 | async-start | bytes 10485760 | tf_op jit(solution)/shard_map/reduce_scatter | solution.py:98
  1143.8 727.4 %reduce-scatter.35.cloned.1.call-start = ((), (), s32[]{:S(2)}) async-start(), calls=%async_computation.28 | async-start | bytes 10485760 | tf_op jit(solution)/shard_map/reduce_scatter | solution.py:101
  1156.1 738.3 %reduce-scatter.39.cloned.1.call-start = ((), (), s32[]{:S(2)}) async-start(), calls=%async_computation.30 | async-start | bytes 327680
  1168.6 746.4 %reduce-scatter.37.cloned.1.call-start = ((), (), s32[]{:S(2)}) async-start(), calls=%async_computation.29 | async-start | bytes 327680
  1169.6 766.3 %reduce-scatter.41.cloned.1.call-start = ((), (), s32[]{:S(2)}) async-start(), calls=%async_computation.31 | async-start | bytes 327680
  1170.6 785.1 %reduce-scatter.19.cloned.1.call-start = ((), (), s32[]{:S(2)}) async-start(), calls=%async_computation.20 | async-start | bytes 20480 | tf_op jit(solution)/shard_map/reduce_scatter | solution.py:104
  1176.5 952.1 %all-reduce.8.cloned.1.call-start = ((), (), s32[]{:S(2)}) async-start(), calls=%async_computation.32 | async-start | bytes 24117248 | tf_op jit(solution)/shard_map/psum | solution.py:109
  (77 other events, 1298.5 us)
Sparse Core Ops, SparseCore 0:
  9.6 152.5 all-gather.8
  163.8 147.7 all-gather.10
  313.2 113.5 all-gather.12
  428.2 44.1 all-gather.14
  473.8 79.4 all-gather.16
  554.8 45.4 all-gather.18
  601.8 149.3 all-gather.20
  752.8 147.8 all-gather.22
  999.3 43.7 reduce-scatter.26
  1045.3 43.1 reduce-scatter.30
  1091.4 76.0 reduce-scatter.28
  1169.8 111.2 reduce-scatter.24
  1283.6 144.9 reduce-scatter.20
  1431.0 145.1 reduce-scatter.22
  1578.5 145.1 reduce-scatter.32
  1726.1 145.1 reduce-scatter.34
  1874.0 20.3 reduce-scatter.38
  1897.1 17.8 reduce-scatter.36
  1917.9 17.9 reduce-scatter.40
  1938.6 17.1 reduce-scatter.18
  1961.2 167.3 all-reduce.7
where the time goes:
time: 2160 us; the launch traced here: 2150 us
  waiting for transfers between devices  1600 us (74%)
  matrix products  239 us (11%)
  blocking collectives  197 us (9%)
  other arithmetic  65.6 us (3%)
  local copies, waits for them, and re-layouts  32.1 us (1%)
    reduce_scatter x4, waiting for transfers between devices, reduce_grads(): lax.psum_scatter(grad_in.astype(jnp.bfloat16), 'fsdp', scatter_dimension=...  400 us
    all_gather x4, waiting for transfers between devices, fetch(): lax.all_gather(weight_in, 'fsdp', axis=0, tiled=True)  361 us
    all_gather x4, waiting for transfers between devices, fetch(): lax.all_gather(weight_out, 'fsdp', axis=0, tiled=True)  302 us
    reduce_scatter x4, waiting for transfers between devices, reduce_grads(): lax.psum_scatter(grad_out.astype(jnp.bfloat16), 'fsdp', scatter_dimension...  295 us
    psum x1, waiting for transfers between devices, reduce_grads(): lax.psum(shards[0].astype(jnp.bfloat16), 'dp').astype(jnp.float32)  159 us
    dot_general x8, matrix products, product_tn(): lax.dot_general(left_side, right_side, (((0,), (0,)), ((), ())), preferre...  65.8 us
    unnamed x24, waiting for transfers between devices  65.3 us
    dot_general x8, matrix products, product(): return jnp.dot(left_side, right_side, preferred_element_type=jnp.float32)  61.3 us
  transfers between devices with their start and end apart: 21, of which 17 were waited for; matrix products, arithmetic and copies ran while one was open for 12% of the time, Pallas kernels for 0%

commit v1 on v0

--- a/solution.py
+++ b/solution.py
@@ -1,6 +1,10 @@
+import functools
+
 import jax
 import jax.numpy as jnp
 from jax import lax
+from jax.experimental import pallas as pl
+from jax.experimental.pallas import tpu as pltpu
 from jax.sharding import PartitionSpec as P
 
 HEAD = 128
@@ -77,20 +81,268 @@
     )
 
 
-def fetch(weight_in, weight_out, small_part):
-    return (
-        lax.all_gather(weight_in, "fsdp", axis=0, tiled=True),
-        lax.all_gather(weight_out, "fsdp", axis=0, tiled=True),
-        lax.all_gather(small_part, "fsdp", axis=1, tiled=True),
-    )
-
-
-def fetch_again(weight_in, weight_out, small_part):
-    return (
-        lax.all_gather(weight_in, "fsdp", axis=0, tiled=True),
-        lax.all_gather(weight_out, "fsdp", axis=0, tiled=True),
-        lax.all_gather(small_part, "fsdp", axis=1, tiled=True),
-    )
+MESH = pl.DeviceIdType.MESH
+WAYS = 8
+
+
+def coordinates():
+    dp = lax.axis_index("dp")
+    z = lax.axis_index("fsdp")
+    core_bit = lax.rem(dp, 2)
+    x_bit = lax.rem(dp // 2, 2)
+    y_bit = lax.rem(dp // 4, 2)
+    return dp, z, core_bit, x_bit, y_bit
+
+
+def signal(sem, device):
+    pl.semaphore_signal(sem, inc=1, device_id=device, device_id_type=MESH)
+
+
+def greet(depth, dp, z, flat_peers):
+    barrier = pltpu.get_barrier_semaphore()
+    signal(barrier, (dp, lax.rem(z + 1, depth)))
+    signal(barrier, (dp, lax.rem(z + depth - 1, depth)))
+    for peer in flat_peers:
+        signal(barrier, (peer, z))
+    pl.semaphore_wait(barrier, 2 + len(flat_peers))
+
+
+def gather_kernel(depth, count, chunks, lead, *refs):
+    shards, small = refs[:count], refs[count]
+    fulls, small_full = refs[count + 1 : 2 * count + 1], refs[2 * count + 1]
+    send_sems, recv_sems, own_sems, small_sems = refs[2 * count + 2 :]
+    dp, z, core_bit, x_bit, y_bit = coordinates()
+    mine = lax.rem(dp, WAYS)
+    step_c, step_x, step_y = 1 - 2 * core_bit, 2 - 4 * x_bit, 4 - 8 * y_bit
+    peer_c, peer_x, peer_y = dp + step_c, dp + step_x, dp + step_y
+    greet(depth, dp, z, (peer_c, peer_x, peer_y))
+
+    def remote(source, target, send_sem, recv_sem, device):
+        return pltpu.make_async_remote_copy(
+            source, target, send_sem, recv_sem, device_id=device, device_id_type=MESH
+        )
+
+    def slot(chunk, owner, piece, half):
+        index, first, width = chunks[chunk]
+        rows = shards[index].shape[0]
+        part = rows // WAYS
+        if half is not None:
+            width = width // 2
+            first = first + half * width
+        start = pl.multiple_of(owner * rows + piece * part, part)
+        return fulls[index].at[pl.ds(start, part), pl.ds(first, width)]
+
+    def place(chunk, index, message, owner, piece, device, half=None):
+        where = slot(chunk, owner, piece, half)
+        return remote(
+            where,
+            where,
+            send_sems.at[chunk, index, message],
+            recv_sems.at[chunk, index, message],
+            device,
+        )
+
+    def each(action):
+        for hop in range(depth - 1):
+
+            @pl.when(z - 1 - hop >= 0)
+            def _():
+                action(2 * hop, z - 1 - hop, hop, 1)
+
+            @pl.when(z + 1 + hop < depth)
+            def _():
+                action(2 * hop + 1, z + 1 + hop, hop, -1)
+
+    here = (dp, z)
+    core_dev, x_dev, y_dev = (peer_c, z), (peer_x, z), (peer_y, z)
+    piece_x, piece_y, piece_xy = mine + step_x, mine + step_y, mine + step_x + step_y
+    other = mine + step_c
+    other_x, other_y, other_xy = other + step_x, other + step_y, other + step_x + step_y
+
+    small_local = pltpu.make_async_copy(small, small_full.at[z], own_sems.at[count, 0])
+    small_local.start()
+
+    def small_out(index, source, owner, device):
+        return remote(
+            source, small_full.at[owner], small_sems.at[index, 0], small_sems.at[index, 1], device
+        )
+
+    @pl.when(z + 1 < depth)
+    def _():
+        small_out(0, small, z, (dp, z + 1)).start()
+
+    @pl.when(z > 0)
+    def _():
+        small_out(1, small, z, (dp, z - 1)).start()
+
+    def line_start(chunk):
+        index, first, width = chunks[chunk]
+        part = shards[index].shape[0] // WAYS
+        source = shards[index].at[
+            pl.ds(pl.multiple_of(mine * part, part), part), pl.ds(first, width)
+        ]
+        target = slot(chunk, z, mine, None)
+
+        @pl.when(z + 1 < depth)
+        def _():
+            remote(
+                source, target, send_sems.at[chunk, 0, 0], recv_sems.at[chunk, 0, 0], (dp, z + 1)
+            ).start()
+
+        @pl.when(z > 0)
+        def _():
+            remote(
+                source, target, send_sems.at[chunk, 1, 0], recv_sems.at[chunk, 1, 0], (dp, z - 1)
+            ).start()
+
+    def line_arrived(chunk):
+        def action(index, owner, hop, way):
+            place(chunk, index, 0, owner, mine, here).wait_recv()
+            if hop < depth - 2:
+                following = z + way
+
+                @pl.when((following >= 0) & (following < depth))
+                def _():
+                    place(chunk, index + 2, 0, owner, mine, (dp, following)).start()
+
+            place(chunk, index, 1, owner, mine, x_dev).start()
+            place(chunk, index, 2, owner, mine, y_dev).start()
+            place(chunk, index, 5, owner, mine, core_dev).start()
+
+        each(action)
+
+    def plane_arrived(chunk):
+        def action(index, owner, hop, way):
+            place(chunk, index, 1, owner, piece_x, here).wait_recv()
+            place(chunk, index, 3, owner, piece_x, y_dev, 0).start()
+            place(chunk, index, 6, owner, piece_x, core_dev).start()
+            place(chunk, index, 2, owner, piece_y, here).wait_recv()
+            place(chunk, index, 4, owner, piece_y, x_dev, 1).start()
+            place(chunk, index, 7, owner, piece_y, core_dev).start()
+
+        each(action)
+
+    def corner_arrived(chunk):
+        def action(index, owner, hop, way):
+            for half in range(2):
+                place(chunk, index, 3 + half, owner, piece_xy, here, half).wait_recv()
+                place(chunk, index, 8 + half, owner, piece_xy, core_dev, half).start()
+
+        each(action)
+
+    def core_arrived(chunk):
+        def action(index, owner, hop, way):
+            place(chunk, index, 5, owner, other, here).wait_recv()
+            place(chunk, index, 6, owner, other_x, here).wait_recv()
+            place(chunk, index, 7, owner, other_y, here).wait_recv()
+            for half in range(2):
+                place(chunk, index, 8 + half, owner, other_xy, here, half).wait_recv()
+
+        each(action)
+
+    def small_action(index, owner, hop, way):
+        small_out(index, small, owner, here).wait_recv()
+        if hop < depth - 2:
+            following = z + way
+
+            @pl.when((following >= 0) & (following < depth))
+            def _():
+                small_out(index + 2, small_full.at[owner], owner, (dp, following)).start()
+
+    total = len(chunks)
+    for chunk in range(min(lead, total)):
+        line_start(chunk)
+    own_copies = []
+    for index in range(count):
+        rows = shards[index].shape[0]
+        target = fulls[index].at[pl.ds(pl.multiple_of(z * rows, rows), rows)]
+        copy = remote(
+            shards[index], target, own_sems.at[index, 0], own_sems.at[index, 1], core_dev
+        )
+        copy.start()
+        own_copies.append(copy)
+    for turn in range(total + 3):
+        if turn + lead < total:
+            line_start(turn + lead)
+        if turn < total:
+            line_arrived(turn)
+        if turn == 0:
+            each(small_action)
+        if 0 <= turn - 1 < total:
+            plane_arrived(turn - 1)
+        if 0 <= turn - 2 < total:
+            corner_arrived(turn - 2)
+        if 0 <= turn - 3 < total:
+            core_arrived(turn - 3)
+    for copy in own_copies:
+        copy.wait()
+    small_local.wait()
+
+    @pl.when(z + 1 < depth)
+    def _():
+        small_out(0, small, z, here).wait_send()
+
+    @pl.when(z > 0)
+    def _():
+        small_out(1, small, z, here).wait_send()
+
+    def small_drain(index, owner, hop, way):
+        if hop < depth - 2:
+            following = z + way
+
+            @pl.when((following >= 0) & (following < depth))
+            def _():
+                small_out(index + 2, small, owner, here).wait_send()
+
+    each(small_drain)
+    for chunk in range(total):
+
+        @pl.when(z + 1 < depth)
+        def _():
+            place(chunk, 0, 0, z, mine, here).wait_send()
+
+        @pl.when(z > 0)
+        def _():
+            place(chunk, 1, 0, z, mine, here).wait_send()
+
+        def drain(index, owner, hop, way):
+            if hop < depth - 2:
+                following = z + way
+
+                @pl.when((following >= 0) & (following < depth))
+                def _():
+                    place(chunk, index + 2, 0, owner, mine, here).wait_send()
+
+            for message in (1, 2, 5, 6, 7):
+                place(chunk, index, message, owner, mine, here).wait_send()
+            for message in (3, 4, 8, 9):
+                place(chunk, index, message, owner, mine, here, 0).wait_send()
+
+        each(drain)
+
+
+def gather_all(depth, weights, small):
+    count = len(weights)
+    chunks = [(index, 0, weight.shape[1]) for index, weight in enumerate(weights)]
+    shape = (len(chunks), 2 * (depth - 1), 10)
+    outs = [
+        jax.ShapeDtypeStruct((weight.shape[0] * depth, weight.shape[1]), weight.dtype)
+        for weight in weights
+    ]
+    outs.append(jax.ShapeDtypeStruct((depth,) + small.shape, small.dtype))
+    return pl.pallas_call(
+        functools.partial(gather_kernel, depth, count, chunks, 2),
+        out_shape=outs,
+        in_specs=[pl.BlockSpec(memory_space=pl.ANY)] * (count + 1),
+        out_specs=[pl.BlockSpec(memory_space=pl.ANY)] * (count + 1),
+        scratch_shapes=[
+            pltpu.SemaphoreType.DMA(shape),
+            pltpu.SemaphoreType.DMA(shape),
+            pltpu.SemaphoreType.DMA((count + 1, 2)),
+            pltpu.SemaphoreType.DMA((2 * (depth - 1), 2)),
+        ],
+        compiler_params=pltpu.CompilerParams(collective_id=0, has_side_effects=True),
+    )(*weights, small)
 
 
 def reduce_grads(grad_in, grad_out, small_grad):
@@ -314,6 +566,7 @@
 
 
 def local(
+    depth_devices,
     tokens,
     lengths,
     span_starts,
@@ -342,29 +595,40 @@
     live = valid.reshape(row_count, 1).astype(jnp.float32)
     masked_col = masked.reshape(row_count, 1)
     tables = rotation(frame_count)
-    first_small = jnp.concatenate([norm_gains[0:1], mask_embed[None, :]], axis=0)
-    second_small = norm_gains[1:2]
-    third_small = jnp.concatenate([norm_gains[2:3], depth, bn_affine], axis=0)
-    fourth_small = norm_gains[3:5]
-    first_weights = fetch(ffn1_in, ffn1_out, first_small)
+    small = jnp.concatenate([norm_gains, mask_embed[None, :], depth, bn_affine], axis=0)
+    small = jnp.pad(small, ((0, 16 - small.shape[0]), (0, 0)))
+    gathered = gather_all(
+        depth_devices,
+        [ffn1_in, ffn1_out, attn_in, attn_out, conv_in, conv_out, ffn2_in, ffn2_out],
+        small,
+    )
+    small_all = gathered[8].transpose(1, 0, 2).reshape(16, model_width)
+    third_small = jnp.concatenate([small_all[2:3], small_all[6:13]], axis=0)
+    first_weights = (gathered[0], gathered[1], small_all[jnp.array([0, 5])])
+    second_weights = (gathered[2], gathered[3], small_all[1:2])
+    third_weights = (gathered[4], gathered[5], third_small)
+    fourth_weights = (gathered[6], gathered[7], small_all[3:5])
+    first_back, second_back, third_back, fourth_back = (
+        first_weights,
+        second_weights,
+        third_weights,
+        fourth_weights,
+    )
     gain_one = first_weights[2][0].astype(jnp.float32)
     embed = first_weights[2][1].astype(jnp.float32)
     start = jnp.where(masked_col, embed, tokens.reshape(row_count, model_width).astype(jnp.float32))
     branch, first_stored = ffn_forward(start, gain_one, first_weights[0], first_weights[1])
     first = start + 0.5 * branch
-    second_weights = fetch(attn_in, attn_out, second_small)
     gain_two = second_weights[2][0].astype(jnp.float32)
     branch, second_stored = attention_forward(
         first, gain_two, second_weights[0], second_weights[1], valid, tables, units
     )
     second = first + branch
-    third_weights = fetch(conv_in, conv_out, third_small)
     gain_three = third_weights[2][0].astype(jnp.float32)
     branch, third_stored = conv_forward(
         second, gain_three, third_weights[0], third_weights[1], third_weights[2], live, units
     )
     third = second + branch
-    fourth_weights = fetch(ffn2_in, ffn2_out, fourth_small)
     gain_four = fourth_weights[2][0].astype(jnp.float32)
     gain_five = fourth_weights[2][1].astype(jnp.float32)
     branch, fourth_stored = ffn_forward(third, gain_four, fourth_weights[0], fourth_weights[1])
@@ -373,12 +637,10 @@
     output = out_norm.astype(jnp.bfloat16).reshape(units, frame_count, model_width)
     upstream = cotangent.reshape(row_count, model_width).astype(jnp.float32)
     grad_four, gain_five_grad = norm_back(upstream, gain_five, final_normed, final_inverse)
-    fourth_back = fetch_again(ffn2_in, ffn2_out, fourth_small)
     grad_three, grad_in, grad_out, gain_four_grad = ffn_backward(
         grad_four, fourth_stored, gain_four, fourth_back[0], fourth_back[1]
     )
     fourth_red = reduce_grads(grad_in, grad_out, jnp.stack([gain_four_grad, gain_five_grad]))
-    third_back = fetch_again(conv_in, conv_out, third_small)
     grad_two, grad_in, grad_out, gain_three_grad, kernel_grad, affine_full = conv_backward(
         grad_three,
         third_stored,
@@ -392,12 +654,10 @@
     third_red = reduce_grads(
         grad_in, grad_out, jnp.concatenate([gain_three_grad[None, :], kernel_grad], axis=0)
     )
-    second_back = fetch_again(attn_in, attn_out, second_small)
     grad_one, grad_in, grad_out, gain_two_grad = attention_backward(
         grad_two, second_stored, gain_two, second_back[0], second_back[1], valid, tables
     )
     second_red = reduce_grads(grad_in, grad_out, gain_two_grad[None, :])
-    first_back = fetch_again(ffn1_in, ffn1_out, first_small)
     grad_zero, grad_in, grad_out, gain_one_grad = ffn_backward(
         grad_one, first_stored, gain_one, first_back[0], first_back[1]
     )
@@ -469,4 +729,4 @@
         P("fsdp", None),
         P("fsdp", None),
     )
-    return jax.shard_map(local, mesh=mesh, in_specs=in_specs, out_specs=out_specs, check_vma=False)
+    return jax.shard_map(functools.partial(local, mesh.shape["fsdp"]), mesh=mesh, in_specs=in_specs, out_specs=out_specs, check_vma=False)

time: 2160 us -> 1560 us (0.72)
  waiting for transfers between devices: 1600 us -> 892 us
  Pallas kernels: 0 us -> 179 us
  blocking collectives: 197 us -> 136 us
    all_gather x8 -> x0, waiting for transfers between devices: 664 us -> none  [the longest x4 361 us: fetch(): lax.all_gather(weight_in, 'fsdp', axis=0, tiled=True)]
    pallas_call x0 -> x1, Pallas kernels: none -> 179 us  [gather_all(): pl.pallas_call(functools.partial(gather_kernel, depth, count, chunks, 2),...]
    all_gather x4 -> x0, blocking collectives: 56 us -> none  [fetch(): lax.all_gather(small_part, 'fsdp', axis=1, tiled=True)]
    reduce_scatter x4, waiting for transfers between devices: 400 us -> 359 us  [reduce_grads(): lax.psum_scatter(grad_in.astype(jnp.bfloat16), 'fsdp', scatter_dimension=...]
    unnamed x24 -> x16, waiting for transfers between devices: 65.3 us -> 60.4 us
  transfers between devices with their start and end apart: 21 -> 13, of which waited for: 17 -> 10; matrix products, arithmetic and copies ran while one was open for 12% -> 12% of each run, Pallas kernels for 0% -> 0%
where the time goes in v1:
time: 1560 us; the launch traced here: 1550 us
  waiting for transfers between devices  892 us (57%)
  matrix products  218 us (14%)
  Pallas kernels  179 us (11%)
  blocking collectives  136 us (9%)
  other arithmetic  68.9 us (4%)
  local copies, waits for them, and re-layouts  39.4 us (3%)
  between operations  16 us (1%)
    reduce_scatter x4, waiting for transfers between devices, reduce_grads(): lax.psum_scatter(grad_in.astype(jnp.bfloat16), 'fsdp', scatter_dimension=...  359 us
    reduce_scatter x4, waiting for transfers between devices, reduce_grads(): lax.psum_scatter(grad_out.astype(jnp.bfloat16), 'fsdp', scatter_dimension...  295 us
    pallas_call x1, Pallas kernels, gather_all(): pl.pallas_call(functools.partial(gather_kernel, depth, count, chunks, 2),...  179 us
    psum x1, waiting for transfers between devices, reduce_grads(): lax.psum(shards[0].astype(jnp.bfloat16), 'dp').astype(jnp.float32)  159 us
    dot_general x8, matrix products, product_nt(): lax.dot_general(left_side, right_side, (((1,), (1,)), ((), ())), preferre...  62.7 us
    dot_general x8, matrix products, product_tn(): lax.dot_general(left_side, right_side, (((0,), (0,)), ((), ())), preferre...  60.8 us
    unnamed x16, waiting for transfers between devices  60.4 us
    dot_general x8, matrix products, product(): return jnp.dot(left_side, right_side, preferred_element_type=jnp.float32)  44.6 us
  transfers between devices with their start and end apart: 13, of which 10 were waited for; matrix products, arithmetic and copies ran while one was open for 12% of the time, Pallas kernels for 0%

profile of v1, /device:TPU:0, one launch (start us, length us, event | category | flops | bytes accessed | tf_op | source)
XLA Modules:
  0.0 1550.7 jit_solution(43416479170964358)
XLA Ops:
  9.2 179.5 %shard_map.275 = (bf16[1024,4096]{1,0:T(8,128)(2,1)}, bf16[4096,1024]{1,0:T(8,128)(2,1)}, bf16[1024,3072]{1,0:T(8,128)(2,1)}, bf16[1024,1024]{1,0:T(8,128)(2,1)}...) custom-call(bf16[256,4096]{1,0:T(8,128)(2,1)} %refs_0_.1, ...), custom_call_target="tpu_custom_call" | custom-call | tf_op jit(solution)/shard_map/pallas_call | solution.py:333
  194.1 11.1 fusion.125
  241.9 37.4 %all-reduce.4 = (f32[1024]{0:T(1024)S(1)}, f32[]{:T(128)}) all-reduce(f32[1024]{0:T(1024)S(1)} %get-tuple-element.77, f32[]{:T(128)} %fusion.96), channel_id=1, replica_groups=mesh['dp'=8,'fsdp'=4] {'dp','fsdp'}, use_global_device_ids=true, to_apply=%region_10.11 | all-reduce | flops 1025 | bytes 8200 | tf_op jit(solution)/shard_map/psum | solution.py:481
  280.3 42.4 %psum.121 = f32[1024]{0:T(1024)S(1)} all-reduce(f32[1024]{0:T(1024)S(1)} %multiply_reduce_fusion.16), channel_id=1, replica_groups=mesh['dp'=8,'fsdp'=4] {'dp','fsdp'}, use_global_device_ids=true, to_apply=%region_14.15 | all-reduce | flops 1024 | bytes 8192 | tf_op jit(solution)/shard_map/psum | solution.py:484
  345.2 11.9 multiply_convert_fusion.2
  357.1 9.6 multiply_reduce_fusion.1
  379.4 43.3 %all-reduce.3 = (f32[1024]{0:T(1024)S(1)}, f32[1024]{0:T(1024)S(1)}) all-reduce(f32[1024]{0:T(1024)S(1)} %get-tuple-element.51, f32[1024]{0:T(1024)S(1)} %get-tuple-element.50), channel_id=1, replica_groups=mesh['dp'=8,'fsdp'=4] {'dp','fsdp'}, use_global_device_ids=true, to_apply=%region_26.27 | all-reduce | flops 2048 | bytes 16384 | tf_op jit(solution)/shard_map/psum | solution.py:528
  461.9 16.0 %fusion.60 = f32[1,512,8,128]{3,1,2,0:T(8,128)} fusion(f32[8,512,512]{1,2,0:T(8,128)} %fusion.76, f32[8,512,512]{1,2,0:T(8,128)} %copy-done.4, f32[8,512]{1,0:T(8,128)S(1)} %log_add_fusion, pred[512]{0:T(512)(128)(4,1)S(1)} %get-tuple-element.133, bf16[512,8,64]{2,0,1:T(8,128)(2,1)} %copy-done.27, bf16[512,8,64]{2,0,1:T(8,128)(2,1)} %copy-done.28), kind=kOutput, calls=%fused_computation.133 | convolution fusion | flops 562041344 | bytes 19939840 | tf_op jit(solution)/shard_map/uhqk,ukhd->uqhd/dot_general | solution.py:439
  477.9 17.7 %fusion.63 = f32[1,512,8,128]{3,1,2,0:T(8,128)} fusion(f32[8,512,512]{1,2,0:T(8,128)} %fusion.76, f32[8,512,512]{1,2,0:T(8,128)} %copy-done.4, f32[8,512]{1,0:T(8,128)S(1)} %log_add_fusion, pred[512]{0:T(512)(128)(4,1)S(1)} %get-tuple-element.133, bf16[512,8,64]{2,0,1:T(8,128)(2,1)} %copy-done.26, bf16[512,8,64]{2,0,1:T(8,128)(2,1)S(1)} %get-tuple-element.81), kind=kOutput, calls=%fused_computation.134 | convolution fusion | flops 562041344 | bytes 19939840 | tf_op jit(solution)/shard_map/uhqk,uqhd->ukhd/dot_general | solution.py:444
  527.7 12.1 convolution_convert_fusion
  541.4 9.1 convolution_convert_fusion.1
  562.3 11.0 convolution_convert_fusion.2
  575.4 10.1 multiply_convert_fusion
  615.3 63.3 %reduce-scatter.25.cloned.1.call-done = bf16[256,3072]{1,0:T(8,128)(2,1)} async-done(((bf16[1024,3072]{1,0:T(8,128)(2,1)}), bf16[256,3072]{1,0:T(8,128)(2,1)}) %reduce-scatter.25.cloned.1.call-update) | async-done | bytes 1572880 | tf_op jit(solution)/shard_map/reduce_scatter | solution.py:350
  678.6 147.4 %reduce-scatter.35.cloned.1.call-done = bf16[1024,1024]{1,0:T(8,128)(2,1)} async-done(((bf16[4096,1024]{1,0:T(8,128)(2,1)}), bf16[1024,1024]{1,0:T(8,128)(2,1)}) %reduce-scatter.35.cloned.1.call-update) | async-done | bytes 2097168 | tf_op jit(solution)/shard_map/reduce_scatter | solution.py:353
  826.0 147.6 %reduce-scatter.33.cloned.1.call-done = bf16[256,4096]{1,0:T(8,128)(2,1)} async-done(((bf16[1024,4096]{1,0:T(8,128)(2,1)}), bf16[256,4096]{1,0:T(8,128)(2,1)}) %reduce-scatter.33.cloned.1.call-update) | async-done | bytes 2097168 | tf_op jit(solution)/shard_map/reduce_scatter | solution.py:350
  973.5 147.7 %reduce-scatter.23.cloned.1.call-done = bf16[1024,1024]{1,0:T(8,128)(2,1)} async-done(((bf16[4096,1024]{1,0:T(8,128)(2,1)}), bf16[1024,1024]{1,0:T(8,128)(2,1)}) %reduce-scatter.23.cloned.1.call-update) | async-done | bytes 2097168 | tf_op jit(solution)/shard_map/reduce_scatter | solution.py:353
  1121.2 147.7 %reduce-scatter.21.cloned.1.call-done = bf16[256,4096]{1,0:T(8,128)(2,1)} async-done(((bf16[1024,4096]{1,0:T(8,128)(2,1)}), bf16[256,4096]{1,0:T(8,128)(2,1)}) %reduce-scatter.21.cloned.1.call-update) | async-done | bytes 2097168 | tf_op jit(solution)/shard_map/reduce_scatter | solution.py:350
  1271.7 20.5 %reduce-scatter.39.cloned.1.call-done = bf16[256,1]{1,0:T(8,128)(2,1)} async-done(((bf16[1024,1]{1,0:T(8,128)(2,1)}), bf16[256,1]{1,0:T(8,128)(2,1)}) %reduce-scatter.39.cloned.1.call-update) | async-done | bytes 528
  1293.1 19.8 %reduce-scatter.41.cloned.1.call-done = bf16[256,2]{1,0:T(8,128)(2,1)} async-done(((bf16[1024,2]{1,0:T(8,128)(2,1)}), bf16[256,2]{1,0:T(8,128)(2,1)}) %reduce-scatter.41.cloned.1.call-update) | async-done | bytes 1040
  1313.8 19.8 %reduce-scatter.37.cloned.1.call-done = bf16[256,2]{1,0:T(8,128)(2,1)} async-done(((bf16[1024,2]{1,0:T(8,128)(2,1)}), bf16[256,2]{1,0:T(8,128)(2,1)}) %reduce-scatter.37.cloned.1.call-update) | async-done | bytes 1040
  1334.6 19.0 %reduce-scatter.19.cloned.1.call-done = bf16[6,256]{1,0:T(8,128)(2,1)} async-done(((bf16[6,1024]{1,0:T(8,128)(2,1)}), bf16[6,256]{1,0:T(8,128)(2,1)}) %reduce-scatter.19.cloned.1.call-update) | async-done | bytes 3088 | tf_op jit(solution)/shard_map/reduce_scatter | solution.py:356
  1353.6 12.3 all-reduce.5
  1367.7 158.7 %all-reduce.9.cloned.1.call-done = (bf16[256,4096]{1,0:T(8,128)(2,1)}, bf16[1024,1024]{1,0:T(8,128)(2,1)}, bf16[256,3072]{1,0:T(8,128)(2,1)}, bf16[256,1024]{1,0...) async-done(((bf16[256,4096]{1,0:T(8,128)(2,1)}, bf16[1024,1024]{1,0:T(8,128)(2,1)}, ...) | async-done | bytes 12058640 | tf_op jit(solution)/shard_map/psum | solution.py:361
  (331 shorter events, 219.6 us)
Async XLA Ops:
  7.2 608.1 %reduce-scatter.31.cloned.1.call-start = ((), (), s32[]{:S(2)}) async-start(), calls=%async_computation.18 | async-start | bytes 2621440 | tf_op jit(solution)/shard_map/reduce_scatter | solution.py:353
  9.2 183.2 %copy-start.72 = (s32[1,5]{1,0:T(1,128)S(1)}, s32[1,5]{1,0:T(1,128)}, u32[]{:S(2)}) copy-start(s32[1,5]{1,0:T(1,128)} %param.19) | copy-start | bytes 64
  9.2 183.9 %copy-start.8 = (bf16[1,512,1024]{2,1,0:T(8,128)(2,1)S(1)}, bf16[1,512,1024]{2,1,0:T(8,128)(2,1)}, u32[]{:S(2)}) copy-start(bf16[1,512,1024]{2,1,0:T(8,128)(2,1)} %param.17) | copy-start | bytes 3145732
  189.6 23.7 %copy-start.52 = (f32[1,4,256]{2,0,1:T(1,128)}, f32[1,4,256]{2,0,1:T(1,128)S(1)}, u32[]{:S(2)}) copy-start(f32[1,4,256]{2,0,1:T(1,128)S(1)} %get-tuple-element.104) | copy-start | bytes 12292
  213.0 19.3 %copy-start.15 = (f32[512,1024]{1,0:T(8,128)}, f32[512,1024]{1,0:T(8,128)S(1)}, u32[]{:S(2)}) copy-start(f32[512,1024]{1,0:T(8,128)S(1)} %get-tuple-element.119) | copy-start | bytes 6291460
  241.9 85.5 %copy-start.6 = (f32[1,512,1024]{2,1,0:T(8,128)}, f32[1,512,1024]{2,1,0:T(8,128)S(1)}, u32[]{:S(2)}) copy-start(f32[1,512,1024]{2,1,0:T(8,128)S(1)} %get-tuple-element.78) | copy-start | bytes 6291460
  327.4 39.3 %copy-start.23 = (f32[512,1024]{1,0:T(8,128)}, f32[512,1024]{1,0:T(8,128)S(1)}, u32[]{:S(2)}) copy-start(f32[512,1024]{1,0:T(8,128)S(1)} %get-tuple-element.125) | copy-start | bytes 6291460
  373.1 242.1 %reduce-scatter.27.cloned.1.call-start = ((), (), s32[]{:S(2)}) async-start(), calls=%async_computation.16 | async-start | bytes 2621440 | tf_op jit(solution)/shard_map/reduce_scatter | solution.py:353
  441.8 173.5 %reduce-scatter.29.cloned.1.call-start = ((), (), s32[]{:S(2)}) async-start(), calls=%async_computation.17 | async-start | bytes 5242880 | tf_op jit(solution)/shard_map/reduce_scatter | solution.py:350
  448.6 230.0 %reduce-scatter.25.cloned.1.call-start = ((), (), s32[]{:S(2)}) async-start(), calls=%async_computation.15 | async-start | bytes 7864320 | tf_op jit(solution)/shard_map/reduce_scatter | solution.py:350
  526.5 299.5 %reduce-scatter.35.cloned.1.call-start = ((), (), s32[]{:S(2)}) async-start(), calls=%async_computation.20 | async-start | bytes 10485760 | tf_op jit(solution)/shard_map/reduce_scatter | solution.py:353
  539.8 433.7 %reduce-scatter.33.cloned.1.call-start = ((), (), s32[]{:S(2)}) async-start(), calls=%async_computation.19 | async-start | bytes 10485760 | tf_op jit(solution)/shard_map/reduce_scatter | solution.py:350
  550.6 570.6 %reduce-scatter.23.cloned.1.call-start = ((), (), s32[]{:S(2)}) async-start(), calls=%async_computation.14 | async-start | bytes 10485760 | tf_op jit(solution)/shard_map/reduce_scatter | solution.py:353
  573.3 14.3 copy-start.9
  573.3 14.3 copy-start.45
  573.3 14.3 copy-start.47
  573.3 14.3 copy-start.51
  573.3 14.3 copy-start.59
  573.3 695.6 %reduce-scatter.21.cloned.1.call-start = ((), (), s32[]{:S(2)}) async-start(), calls=%async_computation.13 | async-start | bytes 10485760 | tf_op jit(solution)/shard_map/reduce_scatter | solution.py:350
  595.0 697.2 %reduce-scatter.39.cloned.1.call-start = ((), (), s32[]{:S(2)}) async-start(), calls=%async_computation.22 | async-start | bytes 327680
  596.0 716.9 %reduce-scatter.41.cloned.1.call-start = ((), (), s32[]{:S(2)}) async-start(), calls=%async_computation.23 | async-start | bytes 327680
  597.0 736.6 %reduce-scatter.37.cloned.1.call-start = ((), (), s32[]{:S(2)}) async-start(), calls=%async_computation.21 | async-start | bytes 327680
  609.2 744.4 %reduce-scatter.19.cloned.1.call-start = ((), (), s32[]{:S(2)}) async-start(), calls=%async_computation.12 | async-start | bytes 20480 | tf_op jit(solution)/shard_map/reduce_scatter | solution.py:356
  615.2 911.3 %all-reduce.9.cloned.1.call-start = ((), (), s32[]{:S(2)}) async-start(), calls=%async_computation.24 | async-start | bytes 24117248 | tf_op jit(solution)/shard_map/psum | solution.py:361
  (74 other events, 362.1 us)
Sparse Core Ops, SparseCore 0:
  373.3 44.1 reduce-scatter.30
  441.9 44.0 reduce-scatter.26
  488.9 76.1 reduce-scatter.28
  567.4 111.2 reduce-scatter.24
  681.0 144.9 reduce-scatter.34
  828.3 145.1 reduce-scatter.32
  976.0 145.1 reduce-scatter.22
  1123.7 145.1 reduce-scatter.20
  1271.9 20.2 reduce-scatter.38
  1294.9 17.9 reduce-scatter.40
  1315.9 17.7 reduce-scatter.36
  1336.3 17.1 reduce-scatter.18
  1359.1 167.3 all-reduce.8

commit v2 on v1

--- a/solution.py
+++ b/solution.py
@@ -18,12 +18,6 @@
 
 def product(left_side, right_side):
     return jnp.dot(left_side, right_side, preferred_element_type=jnp.float32)
-
-
-def product_tn(left_side, right_side):
-    return lax.dot_general(
-        left_side, right_side, (((0,), (0,)), ((), ())), preferred_element_type=jnp.float32
-    )
 
 
 def product_nt(left_side, right_side):
@@ -345,23 +339,585 @@
     )(*weights, small)
 
 
-def reduce_grads(grad_in, grad_out, small_grad):
-    shards = (
-        lax.psum_scatter(
-            grad_in.astype(jnp.bfloat16), "fsdp", scatter_dimension=0, tiled=True
-        ).astype(jnp.float32),
-        lax.psum_scatter(
-            grad_out.astype(jnp.bfloat16), "fsdp", scatter_dimension=0, tiled=True
-        ).astype(jnp.float32),
-        lax.psum_scatter(
-            small_grad.astype(jnp.bfloat16), "fsdp", scatter_dimension=1, tiled=True
-        ).astype(jnp.float32),
-    )
-    return (
-        lax.psum(shards[0].astype(jnp.bfloat16), "dp").astype(jnp.float32),
-        lax.psum(shards[1].astype(jnp.bfloat16), "dp").astype(jnp.float32),
-        lax.psum(shards[2].astype(jnp.bfloat16), "dp").astype(jnp.float32),
-    )
+def add_pair(left, right):
+    return left + right
+
+
+def join_moments(left, right):
+    count = left[0:1] + right[0:1]
+    mean = (left[0:1] * left[1:2] + right[0:1] * right[1:2]) / count
+    gap = right[1:2] - left[1:2]
+    spread = left[2:3] + right[2:3] + gap * gap * (left[0:1] * right[0:1] / count)
+    return jnp.concatenate([count, mean, spread, left[3:]], axis=0)
+
+
+def exchange_kernel(depth, groups, combine, value, result, work, inbox, line, send_sems, recv_sems):
+    dp, z, core_bit, x_bit, y_bit = coordinates()
+    peers = [dp + 1 - 2 * core_bit, dp + 2 - 4 * x_bit, dp + 4 - 8 * y_bit]
+    group = dp // WAYS
+    barrier = pltpu.get_barrier_semaphore()
+    far = [lax.rem(group + step, groups) * WAYS + lax.rem(dp, WAYS) for step in range(1, groups)]
+    for peer in peers + far:
+        signal(barrier, (peer, z))
+    for step in range(1, depth):
+        signal(barrier, (dp, lax.rem(z + step, depth)))
+    pl.semaphore_wait(barrier, len(peers) + len(far) + depth - 1)
+    work[0] = value[...]
+    for turn, peer in enumerate(peers):
+        copy = pltpu.make_async_remote_copy(
+            work.at[turn],
+            inbox.at[turn],
+            send_sems.at[turn],
+            recv_sems.at[turn],
+            device_id=(peer, z),
+            device_id_type=MESH,
+        )
+        copy.start()
+        copy.wait()
+        work[turn + 1] = combine(work[turn], inbox[turn])
+
+    def spread(source, slots, first, targets, own):
+        copies = []
+        for step, target in enumerate(targets):
+            copy = pltpu.make_async_remote_copy(
+                source,
+                slots.at[own],
+                send_sems.at[first + step],
+                recv_sems.at[first + step],
+                device_id=target,
+                device_id_type=MESH,
+            )
+            copy.start()
+            copies.append(copy)
+        local = pltpu.make_async_copy(source, slots.at[own], send_sems.at[first + len(targets)])
+        local.start()
+        for copy in copies:
+            copy.wait()
+        local.wait()
+
+    last = len(peers)
+    if groups > 1:
+        spread(work.at[last], inbox.at[pl.ds(last, groups)], last, [(peer, z) for peer in far], group)
+        total = inbox[last]
+        for step in range(1, groups):
+            total = combine(total, inbox[last + step])
+        work[last] = total
+    first = last + groups
+    spread(
+        work.at[last],
+        line,
+        first,
+        [(dp, lax.rem(z + step, depth)) for step in range(1, depth)],
+        z,
+    )
+    total = line[0]
+    for step in range(1, depth):
+        total = combine(total, line[step])
+    result[...] = total
+
+
+def exchange(depth, groups, combine, value, collective):
+    shape = value.shape
+    sems = 3 + groups + depth
+    return pl.pallas_call(
+        functools.partial(exchange_kernel, depth, groups, combine),
+        out_shape=jax.ShapeDtypeStruct(shape, value.dtype),
+        in_specs=[pl.BlockSpec(memory_space=pltpu.VMEM)],
+        out_specs=pl.BlockSpec(memory_space=pltpu.VMEM),
+        scratch_shapes=[
+            pltpu.VMEM((4,) + shape, value.dtype),
+            pltpu.VMEM((3 + groups,) + shape, value.dtype),
+            pltpu.VMEM((depth,) + shape, value.dtype),
+            pltpu.SemaphoreType.DMA((sems,)),
+            pltpu.SemaphoreType.DMA((sems,)),
+        ],
+        compiler_params=pltpu.CompilerParams(collective_id=collective, has_side_effects=True),
+    )(value)
+
+
+LANES = 128
+HELD = 4
+
+
+def reduce_kernel(depth, groups, count, chunks, *refs):
+    lefts, rights, small = refs[0 : 2 * count : 2], refs[1 : 2 * count : 2], refs[2 * count]
+    at = 2 * count + 1
+    outs, small_out = refs[at : at + count], refs[at + count]
+    at += count + 1
+    left_peers, right_peers = refs[at : at + count], refs[at + count : at + 2 * count]
+    at += 2 * count
+    (
+        left_buf,
+        right_buf,
+        held,
+        first_in,
+        second_in,
+        line_in,
+        far_in,
+        final,
+        small_work,
+        small_in,
+        small_line,
+        pair_send,
+        pair_recv,
+        load_sems,
+        send_sems,
+        recv_sems,
+        store_sems,
+        small_send,
+        small_recv,
+    ) = refs[at:]
+    dp, z, core_bit, x_bit, y_bit = coordinates()
+    group = dp // WAYS
+    peer_c, peer_x, peer_y = (
+        dp + 1 - 2 * core_bit,
+        dp + 2 - 4 * x_bit,
+        dp + 4 - 8 * y_bit,
+    )
+    far = [lax.rem(group + step, groups) * WAYS + lax.rem(dp, WAYS) for step in range(1, groups)]
+    barrier = pltpu.get_barrier_semaphore()
+    for peer in [peer_c, peer_x, peer_y] + far:
+        signal(barrier, (peer, z))
+    for step in range(1, depth):
+        signal(barrier, (dp, lax.rem(z + step, depth)))
+    pl.semaphore_wait(barrier, 3 + len(far) + depth - 1)
+    tokens = lefts[0].shape[0]
+    block = left_buf.shape[2] // depth
+    here = (dp, z)
+
+    def remote(source, target, send_sem, recv_sem, device):
+        return pltpu.make_async_remote_copy(
+            source, target, send_sem, recv_sem, device_id=device, device_id_type=MESH
+        )
+
+    pair_copies = []
+    for index in range(count):
+        half = rights[index].shape[1] // 2
+        columns = pl.ds(pl.multiple_of((1 - core_bit) * half, half), half)
+        pair_copies.append(
+            (
+                remote(
+                    lefts[index],
+                    left_peers[index],
+                    pair_send.at[index, 0],
+                    pair_recv.at[index, 0],
+                    (peer_c, z),
+                ),
+                remote(
+                    rights[index].at[:, columns],
+                    right_peers[index],
+                    pair_send.at[index, 1],
+                    pair_recv.at[index, 1],
+                    (peer_c, z),
+                ),
+            )
+        )
+        for copy in pair_copies[index]:
+            copy.start()
+
+    def loads(chunk):
+        index, row, part, left_slot, right_slot, new_left, new_right = chunks[chunk]
+        rows = lefts[index].shape[1] // depth
+        half = rights[index].shape[1] // 2
+        piece = half // 4
+        copies = []
+        if new_left:
+            for side, source in enumerate((lefts[index], left_peers[index])):
+                for owner in range(depth):
+                    copies.append(
+                        pltpu.make_async_copy(
+                            source.at[:, pl.ds(owner * rows + row, block)],
+                            left_buf.at[
+                                left_slot, pl.ds(side * tokens, tokens), pl.ds(owner * block, block)
+                            ],
+                            load_sems.at[left_slot, side * depth + owner],
+                        )
+                    )
+        if new_right:
+            for quarter in range(4):
+                start = quarter * piece + part * LANES
+                own_start = pl.multiple_of(core_bit * half + start, LANES)
+                target = pl.ds(quarter * LANES, LANES)
+                copies.append(
+                    pltpu.make_async_copy(
+                        rights[index].at[:, pl.ds(own_start, LANES)],
+                        right_buf.at[right_slot, pl.ds(0, tokens), target],
+                        load_sems.at[2 + right_slot, quarter],
+                    )
+                )
+                copies.append(
+                    pltpu.make_async_copy(
+                        right_peers[index].at[:, pl.ds(start, LANES)],
+                        right_buf.at[right_slot, pl.ds(tokens, tokens), target],
+                        load_sems.at[2 + right_slot, 4 + quarter],
+                    )
+                )
+        return copies
+
+    arrived = set()
+
+    def load_start(chunk):
+        index = chunks[chunk][0]
+        if index not in arrived:
+            arrived.add(index)
+            for copy in pair_copies[index]:
+                copy.wait_recv()
+        for copy in loads(chunk):
+            copy.start()
+
+    def axes(chunk):
+        if chunk % 2 == 0:
+            return peer_x, peer_y, x_bit, y_bit
+        return peer_y, peer_x, y_bit, x_bit
+
+    def quarter_of(chunk, first_bit, second_bit):
+        if chunk % 2 == 0:
+            return 2 * first_bit + second_bit
+        return 2 * second_bit + first_bit
+
+    def first_copy(chunk, which, device):
+        _, _, first_bit, _ = axes(chunk)
+        return remote(
+            held.at[chunk % HELD, quarter_of(chunk, 1 - first_bit, which)],
+            first_in.at[chunk, which],
+            send_sems.at[chunk, which],
+            recv_sems.at[chunk, which],
+            device,
+        )
+
+    def second_copy(chunk, device):
+        _, _, _, second_bit = axes(chunk)
+        return remote(
+            first_in.at[chunk, 1 - second_bit],
+            second_in.at[chunk],
+            send_sems.at[chunk, 2],
+            recv_sems.at[chunk, 2],
+            device,
+        )
+
+    def line_copy(chunk, step, device):
+        return remote(
+            second_in.at[chunk, lax.rem(z + step, depth)],
+            line_in.at[chunk, step - 1],
+            send_sems.at[chunk, 2 + step],
+            recv_sems.at[chunk, 2 + step],
+            device,
+        )
+
+    def multiply(chunk):
+        index, row, part, left_slot, right_slot, new_left, new_right = chunks[chunk]
+        for copy in loads(chunk):
+            copy.wait()
+        if chunk + 1 < len(chunks):
+            load_start(chunk + 1)
+        if chunk >= HELD:
+            for which in range(2):
+                first_copy(chunk - HELD, which, here).wait_send()
+
+        def body(owner):
+            columns = pl.ds(pl.multiple_of(owner * block, block), block)
+            product = lax.dot_general(
+                left_buf[left_slot, :, columns],
+                right_buf[right_slot],
+                (((0,), (0,)), ((), ())),
+                preferred_element_type=jnp.float32,
+            ).astype(jnp.bfloat16)
+            for quarter in range(4):
+                held[chunk % HELD, quarter, owner] = product[
+                    :, quarter * LANES : (quarter + 1) * LANES
+                ]
+
+        pl.loop(0, depth)(body)
+        first_peer, _, _, _ = axes(chunk)
+        for which in range(2):
+            first_copy(chunk, which, (first_peer, z)).start()
+
+    def add_first(chunk):
+        _, second_peer, first_bit, second_bit = axes(chunk)
+        for which in range(2):
+            first_copy(chunk, which, here).wait_recv()
+
+        def add(which):
+            first_in[chunk, which] = (
+                first_in[chunk, which].astype(jnp.float32)
+                + held[chunk % HELD, quarter_of(chunk, first_bit, which)].astype(jnp.float32)
+            ).astype(jnp.bfloat16)
+
+        add(1 - second_bit)
+        second_copy(chunk, (second_peer, z)).start()
+        add(second_bit)
+
+    def add_second(chunk):
+        _, _, _, second_bit = axes(chunk)
+        second_copy(chunk, here).wait_recv()
+        second_in[chunk] = (
+            second_in[chunk].astype(jnp.float32) + first_in[chunk, second_bit].astype(jnp.float32)
+        ).astype(jnp.bfloat16)
+        for step in range(1, depth):
+            line_copy(chunk, step, (dp, lax.rem(z + step, depth))).start()
+
+    base = 2 + depth
+
+    def where(chunk, core, x_at, y_at, half=None):
+        index, row, part = chunks[chunk][:3]
+        width = outs[index].shape[1]
+        start = core * (width // 2) + (2 * x_at + y_at) * (width // 8) + part * LANES
+        size = block
+        if half is not None:
+            size = block // 2
+            row = row + half * size
+        return outs[index].at[pl.ds(row, size), pl.ds(pl.multiple_of(start, LANES), LANES)]
+
+    def from_final(chunk, message, device):
+        return remote(
+            final.at[chunk],
+            where(chunk, core_bit, x_bit, y_bit),
+            send_sems.at[chunk, base + message],
+            recv_sems.at[chunk, base + message],
+            device,
+        )
+
+    def passed(chunk, message, core, x_at, y_at, device, half=None):
+        place = where(chunk, core, x_at, y_at, half)
+        return remote(
+            place,
+            place,
+            send_sems.at[chunk, base + message],
+            recv_sems.at[chunk, base + message],
+            device,
+        )
+
+    def store(chunk):
+        return pltpu.make_async_copy(
+            final.at[chunk], where(chunk, core_bit, x_bit, y_bit), store_sems.at[chunk]
+        )
+
+    def far_copy(chunk, step, device):
+        return remote(
+            far_in.at[chunk, groups],
+            far_in.at[chunk, group],
+            send_sems.at[chunk, base + 9 + step],
+            recv_sems.at[chunk, base + 9 + step],
+            device,
+        )
+
+    def finish(chunk):
+        for step in range(1, depth):
+            line_copy(chunk, step, here).wait_recv()
+        total = second_in[chunk, z].astype(jnp.float32)
+        for step in range(1, depth):
+            total = total + line_in[chunk, step - 1].astype(jnp.float32)
+        if groups > 1:
+            own = total.astype(jnp.bfloat16)
+            far_in[chunk, groups] = own
+            far_in[chunk, group] = own
+            for step, peer in enumerate(far):
+                far_copy(chunk, step, (peer, z)).start()
+            for step in range(len(far)):
+                far_copy(chunk, step, here).wait()
+            total = far_in[chunk, 0].astype(jnp.float32)
+            for step in range(1, groups):
+                total = total + far_in[chunk, step].astype(jnp.float32)
+        final[chunk] = total.astype(jnp.bfloat16)
+        for message, peer in enumerate((peer_x, peer_y, peer_c)):
+            from_final(chunk, message, (peer, z)).start()
+        store(chunk).start()
+
+    def plane_arrived(chunk):
+        passed(chunk, 0, core_bit, 1 - x_bit, y_bit, here).wait_recv()
+        passed(chunk, 3, core_bit, 1 - x_bit, y_bit, (peer_y, z), 0).start()
+        passed(chunk, 5, core_bit, 1 - x_bit, y_bit, (peer_c, z)).start()
+        passed(chunk, 1, core_bit, x_bit, 1 - y_bit, here).wait_recv()
+        passed(chunk, 4, core_bit, x_bit, 1 - y_bit, (peer_x, z), 1).start()
+        passed(chunk, 6, core_bit, x_bit, 1 - y_bit, (peer_c, z)).start()
+
+    def corner_arrived(chunk):
+        for half in range(2):
+            passed(chunk, 3 + half, core_bit, 1 - x_bit, 1 - y_bit, here, half).wait_recv()
+            passed(chunk, 7 + half, core_bit, 1 - x_bit, 1 - y_bit, (peer_c, z), half).start()
+
+    def core_arrived(chunk):
+        other = 1 - core_bit
+        passed(chunk, 2, other, x_bit, y_bit, here).wait_recv()
+        passed(chunk, 5, other, 1 - x_bit, y_bit, here).wait_recv()
+        passed(chunk, 6, other, x_bit, 1 - y_bit, here).wait_recv()
+        for half in range(2):
+            passed(chunk, 7 + half, other, 1 - x_bit, 1 - y_bit, here, half).wait_recv()
+
+    def small_copy(turn, device):
+        return remote(
+            small_work.at[turn],
+            small_in.at[turn],
+            small_send.at[turn],
+            small_recv.at[turn],
+            device,
+        )
+
+    def small_far_copy(step, device):
+        return remote(
+            small_work.at[3],
+            small_in.at[3 + group],
+            small_send.at[3 + step],
+            small_recv.at[3 + step],
+            device,
+        )
+
+    slice_width = small_out.shape[1]
+
+    def small_line_copy(step, device):
+        columns = pl.ds(
+            pl.multiple_of(lax.rem(z + step, depth) * slice_width, slice_width), slice_width
+        )
+        return remote(
+            small_work.at[4, :, columns],
+            small_line.at[step - 1],
+            small_send.at[2 + groups + step],
+            small_recv.at[2 + groups + step],
+            device,
+        )
+
+    small_peers = (peer_c, peer_x, peer_y)
+
+    def small_turn(turn):
+        if turn == 0:
+            small_work[0] = small[...]
+        if 1 <= turn <= 3:
+            small_copy(turn - 1, here).wait_recv()
+            small_work[turn] = small_work[turn - 1] + small_in[turn - 1]
+        if turn < 3:
+            small_copy(turn, (small_peers[turn], z)).start()
+        if turn == 3:
+            if groups > 1:
+                small_in[3 + group] = small_work[3]
+                for step, peer in enumerate(far):
+                    small_far_copy(step, (peer, z)).start()
+                for step in range(len(far)):
+                    small_far_copy(step, here).wait()
+                total = small_in[3]
+                for step in range(1, groups):
+                    total = total + small_in[3 + step]
+                small_work[4] = total
+            else:
+                small_work[4] = small_work[3]
+            for step in range(1, depth):
+                small_line_copy(step, (dp, lax.rem(z + step, depth))).start()
+        if turn == 4:
+            columns = pl.ds(pl.multiple_of(z * slice_width, slice_width), slice_width)
+            total = small_work[4, :, columns]
+            for step in range(1, depth):
+                small_line_copy(step, here).wait_recv()
+                total = total + small_line[step - 1]
+            small_out[...] = total
+
+    total_chunks = len(chunks)
+    load_start(0)
+    for turn in range(total_chunks + 9):
+        if turn < 5:
+            small_turn(turn)
+        if turn < total_chunks:
+            multiply(turn)
+        for lag, action in (
+            (2, add_first),
+            (4, add_second),
+            (5, finish),
+            (6, plane_arrived),
+            (7, corner_arrived),
+            (8, core_arrived),
+        ):
+            if 0 <= turn - lag < total_chunks:
+                action(turn - lag)
+    for index in range(count):
+        for copy in pair_copies[index]:
+            copy.wait_send()
+    for turn in range(3):
+        small_copy(turn, here).wait_send()
+    for step in range(1, depth):
+        small_line_copy(step, here).wait_send()
+    for chunk in range(total_chunks):
+        if chunk >= total_chunks - HELD:
+            for which in range(2):
+                first_copy(chunk, which, here).wait_send()
+        second_copy(chunk, here).wait_send()
+        for step in range(1, depth):
+            line_copy(chunk, step, here).wait_send()
+        for message in range(3):
+            from_final(chunk, message, here).wait_send()
+        for message in (5, 6):
+            passed(chunk, message, core_bit, x_bit, y_bit, here).wait_send()
+        for message in (3, 4, 7, 8):
+            passed(chunk, message, core_bit, x_bit, y_bit, here, 0).wait_send()
+        store(chunk).wait()
+
+
+def reduce_chunks(depth, pairs, block):
+    chunks = []
+    left_slot, right_slot = 1, 1
+    last_left, last_right = None, None
+    for index, (left, right) in enumerate(pairs):
+        rows = left.shape[1] // depth
+        for row in range(0, rows, block):
+            for part in range(right.shape[1] // (WAYS * LANES)):
+                new_left = last_left != (index, row)
+                new_right = last_right != (index, part)
+                if new_left:
+                    left_slot = 1 - left_slot
+                if new_right:
+                    right_slot = 1 - right_slot
+                last_left, last_right = (index, row), (index, part)
+                chunks.append((index, row, part, left_slot, right_slot, new_left, new_right))
+    return chunks
+
+
+def reduce_all(depth, groups, pairs, small, collective):
+    count = len(pairs)
+    tokens = pairs[0][0].shape[0]
+    block = small.shape[1] // depth
+    chunks = reduce_chunks(depth, pairs, block)
+    total = len(chunks)
+    outs, left_peers, right_peers = [], [], []
+    for left, right in pairs:
+        outs.append(
+            jax.ShapeDtypeStruct((left.shape[1] // depth, right.shape[1]), jnp.bfloat16)
+        )
+        left_peers.append(jax.ShapeDtypeStruct(left.shape, jnp.bfloat16))
+        right_peers.append(jax.ShapeDtypeStruct((tokens, right.shape[1] // 2), jnp.bfloat16))
+    outs.append(jax.ShapeDtypeStruct((small.shape[0], block), jnp.float32))
+    low = jnp.bfloat16
+    messages = 2 + depth + 9 + groups
+    any_spec = pl.BlockSpec(memory_space=pl.ANY)
+    vmem_spec = pl.BlockSpec(memory_space=pltpu.VMEM)
+    operands = [array for pair in pairs for array in pair]
+    results = pl.pallas_call(
+        functools.partial(reduce_kernel, depth, groups, count, chunks),
+        out_shape=outs + left_peers + right_peers,
+        in_specs=[any_spec] * (2 * count) + [vmem_spec],
+        out_specs=[any_spec] * count + [vmem_spec] + [any_spec] * (2 * count),
+        scratch_shapes=[
+            pltpu.VMEM((2, 2 * tokens, depth * block), low),
+            pltpu.VMEM((2, 2 * tokens, 4 * LANES), low),
+            pltpu.VMEM((HELD, 4, depth, block, LANES), low),
+            pltpu.VMEM((total, 2, depth, block, LANES), low),
+            pltpu.VMEM((total, depth, block, LANES), low),
+            pltpu.VMEM((total, depth - 1, block, LANES), low),
+            pltpu.VMEM((total, groups + 1, block, LANES) if groups > 1 else (1, 1, 16, LANES), low),
+            pltpu.VMEM((total, block, LANES), low),
+            pltpu.VMEM((5,) + small.shape, jnp.float32),
+            pltpu.VMEM((3 + groups,) + small.shape, jnp.float32),
+            pltpu.VMEM((depth - 1, small.shape[0], block), jnp.float32),
+            pltpu.SemaphoreType.DMA((count, 2)),
+            pltpu.SemaphoreType.DMA((count, 2)),
+            pltpu.SemaphoreType.DMA((4, max(2 * depth, 8))),
+            pltpu.SemaphoreType.DMA((total, messages)),
+            pltpu.SemaphoreType.DMA((total, messages)),
+            pltpu.SemaphoreType.DMA((total,)),
+            pltpu.SemaphoreType.DMA((3 + groups + depth,)),
+            pltpu.SemaphoreType.DMA((3 + groups + depth,)),
+        ],
+        compiler_params=pltpu.CompilerParams(
+            collective_id=collective, has_side_effects=True, vmem_limit_bytes=58 * 1024 * 1024
+        ),
+    )(*operands, small)
+    return results[:count], results[count]
 
 
 def ffn_forward(inputs, layer_gain, weight_in, weight_out):
@@ -375,12 +931,10 @@
 def ffn_backward(upstream, stored, layer_gain, weight_in, weight_out):
     hidden, normed, inverse, inner, active = stored
     branch_grad = (0.5 * upstream).astype(jnp.bfloat16)
-    grad_out = product_tn(active, branch_grad)
     active_grad = product_nt(branch_grad, weight_out)
     inner_grad = (active_grad * swish_slope(inner)).astype(jnp.bfloat16)
-    grad_in = product_tn(hidden, inner_grad)
     norm_grad, gain_grad = norm_back(product_nt(inner_grad, weight_in), layer_gain, normed, inverse)
-    return (upstream + norm_grad, grad_in, grad_out, gain_grad)
+    return (upstream + norm_grad, [(hidden, inner_grad), (active, branch_grad)], gain_grad)
 
 
 def attention_scores(queries, keys_rot, key_live):
@@ -421,7 +975,6 @@
     hidden, normed, inverse, queries, keys_rot, values_low, log_total, merged = stored
     row_count, model_width = upstream.shape
     branch_grad = upstream.astype(jnp.bfloat16)
-    grad_out = product_tn(merged, branch_grad)
     merged_grad = product_nt(branch_grad, weight_out).astype(jnp.bfloat16).reshape(queries.shape)
     probs = jnp.exp(attention_scores(queries, keys_rot, key_live) - log_total)
     prob_grad = jnp.einsum(
@@ -453,14 +1006,13 @@
         ],
         axis=1,
     ).astype(jnp.bfloat16)
-    grad_in = product_tn(hidden, joined_grad)
     norm_grad, gain_grad = norm_back(
         product_nt(joined_grad, weight_in), layer_gain, normed, inverse
     )
-    return (upstream + norm_grad, grad_in, grad_out, gain_grad)
-
-
-def conv_forward(inputs, layer_gain, weight_in, weight_out, small_low, live, units):
+    return (upstream + norm_grad, [(hidden, joined_grad), (merged, branch_grad)], gain_grad)
+
+
+def conv_forward(inputs, layer_gain, weight_in, weight_out, small_low, live, units, share):
     row_count, model_width = inputs.shape
     frame_count = row_count // units
     out_norm, normed, inverse = layer_norm(inputs, layer_gain)
@@ -476,12 +1028,13 @@
     for offset in range(1, KER):
         mixed = mixed + kernel[offset] * padded[:, offset : offset + frame_count]
     mixed = mixed.reshape(row_count, model_width)
-    local_sum = jnp.sum(mixed * live, axis=0)
     local_count = jnp.sum(live)
-    total_sum, count = lax.psum((local_sum, local_count), ("dp", "fsdp"))
-    bmean = total_sum / count
-    deviation = mixed - bmean
-    bvar = lax.psum(jnp.sum(deviation * deviation * live, axis=0), ("dp", "fsdp")) / count
+    local_mean = jnp.sum(mixed * live, axis=0) / local_count
+    local_spread = jnp.sum(jnp.square(mixed - local_mean) * live, axis=0)
+    moments = jnp.stack([jnp.full((model_width,), local_count), local_mean, local_spread])
+    moments = share(join_moments, jnp.pad(moments, ((0, 5), (0, 0))), 1)
+    count, bmean = moments[0, 0], moments[1]
+    bvar = moments[2] / count
     bn_inverse = lax.rsqrt(bvar + EPSILON)
     bn_normed = (mixed - bmean) * bn_inverse
     pre_act = small_low[KER + 1].astype(jnp.float32) * bn_normed + small_low[KER + 2].astype(
@@ -504,7 +1057,7 @@
     return (product(active, weight_out), stored)
 
 
-def conv_backward(upstream, stored, layer_gain, weight_in, weight_out, small_low, live, units):
+def conv_backward(upstream, stored, layer_gain, weight_in, weight_out, small_low, live, units, share):
     (
         hidden,
         normed,
@@ -523,11 +1076,10 @@
     kernel = small_low[1 : KER + 1].astype(jnp.float32)
     bn_scale = small_low[KER + 1].astype(jnp.float32)
     branch_grad = upstream.astype(jnp.bfloat16)
-    grad_out = product_tn(active, branch_grad)
     pre_grad = product_nt(branch_grad, weight_out) * swish_slope(pre_act)
-    shift_total, scale_total = lax.psum(
-        (jnp.sum(pre_grad, axis=0), jnp.sum(pre_grad * bn_normed, axis=0)), ("dp", "fsdp")
-    )
+    sums = jnp.stack([jnp.sum(pre_grad, axis=0), jnp.sum(pre_grad * bn_normed, axis=0)])
+    sums = share(add_pair, jnp.pad(sums, ((0, 6), (0, 0))), 2)
+    shift_total, scale_total = sums[0], sums[1]
     mixed_grad = bn_inverse * (
         bn_scale * pre_grad
         - live * (bn_scale * shift_total) / count
@@ -553,12 +1105,10 @@
     proj_grad = jnp.concatenate(
         [glu_grad * gate_part, glu_grad * linear_part * gate_part * (1.0 - gate_part)], axis=1
     ).astype(jnp.bfloat16)
-    grad_in = product_tn(hidden, proj_grad)
     norm_grad, gain_grad = norm_back(product_nt(proj_grad, weight_in), layer_gain, normed, inverse)
     return (
         upstream + norm_grad,
-        grad_in,
-        grad_out,
+        [(hidden, proj_grad), (active, branch_grad)],
         gain_grad,
         kernel_grad,
         jnp.stack([scale_total, shift_total]),
@@ -567,6 +1117,7 @@
 
 def local(
     depth_devices,
+    groups,
     tokens,
     lengths,
     span_starts,
@@ -608,12 +1159,6 @@
     second_weights = (gathered[2], gathered[3], small_all[1:2])
     third_weights = (gathered[4], gathered[5], third_small)
     fourth_weights = (gathered[6], gathered[7], small_all[3:5])
-    first_back, second_back, third_back, fourth_back = (
-        first_weights,
-        second_weights,
-        third_weights,
-        fourth_weights,
-    )
     gain_one = first_weights[2][0].astype(jnp.float32)
     embed = first_weights[2][1].astype(jnp.float32)
     start = jnp.where(masked_col, embed, tokens.reshape(row_count, model_width).astype(jnp.float32))
@@ -625,8 +1170,9 @@
     )
     second = first + branch
     gain_three = third_weights[2][0].astype(jnp.float32)
+    share = functools.partial(exchange, depth_devices, groups)
     branch, third_stored = conv_forward(
-        second, gain_three, third_weights[0], third_weights[1], third_weights[2], live, units
+        second, gain_three, third_weights[0], third_weights[1], third_weights[2], live, units, share
     )
     third = second + branch
     gain_four = fourth_weights[2][0].astype(jnp.float32)
@@ -637,29 +1183,25 @@
     output = out_norm.astype(jnp.bfloat16).reshape(units, frame_count, model_width)
     upstream = cotangent.reshape(row_count, model_width).astype(jnp.float32)
     grad_four, gain_five_grad = norm_back(upstream, gain_five, final_normed, final_inverse)
-    grad_three, grad_in, grad_out, gain_four_grad = ffn_backward(
-        grad_four, fourth_stored, gain_four, fourth_back[0], fourth_back[1]
-    )
-    fourth_red = reduce_grads(grad_in, grad_out, jnp.stack([gain_four_grad, gain_five_grad]))
-    grad_two, grad_in, grad_out, gain_three_grad, kernel_grad, affine_full = conv_backward(
+    grad_three, fourth_pairs, gain_four_grad = ffn_backward(
+        grad_four, fourth_stored, gain_four, fourth_weights[0], fourth_weights[1]
+    )
+    grad_two, third_pairs, gain_three_grad, kernel_grad, affine_full = conv_backward(
         grad_three,
         third_stored,
         gain_three,
-        third_back[0],
-        third_back[1],
+        third_weights[0],
+        third_weights[1],
         third_weights[2],
         live,
         units,
-    )
-    third_red = reduce_grads(
-        grad_in, grad_out, jnp.concatenate([gain_three_grad[None, :], kernel_grad], axis=0)
-    )
-    grad_one, grad_in, grad_out, gain_two_grad = attention_backward(
-        grad_two, second_stored, gain_two, second_back[0], second_back[1], valid, tables
-    )
-    second_red = reduce_grads(grad_in, grad_out, gain_two_grad[None, :])
-    grad_zero, grad_in, grad_out, gain_one_grad = ffn_backward(
-        grad_one, first_stored, gain_one, first_back[0], first_back[1]
+        share,
+    )
+    grad_one, second_pairs, gain_two_grad = attention_backward(
+        grad_two, second_stored, gain_two, second_weights[0], second_weights[1], valid, tables
+    )
+    grad_zero, first_pairs, gain_one_grad = ffn_backward(
+        grad_one, first_stored, gain_one, first_weights[0], first_weights[1]
     )
     masked_float = masked_col.astype(jnp.float32)
     embed_grad = jnp.sum(grad_zero * masked_float, axis=0)
@@ -668,29 +1210,55 @@
         .astype(jnp.bfloat16)
         .reshape(units, frame_count, model_width)
     )
-    first_red = reduce_grads(grad_in, grad_out, jnp.stack([gain_one_grad, embed_grad]))
+    small_grads = jnp.concatenate(
+        [
+            jnp.stack(
+                [
+                    gain_one_grad,
+                    gain_two_grad,
+                    gain_three_grad,
+                    gain_four_grad,
+                    gain_five_grad,
+                    embed_grad,
+                ]
+            ),
+            kernel_grad,
+            jnp.zeros((5, model_width), jnp.float32),
+        ],
+        axis=0,
+    )
+    reduced, small_sum = reduce_all(
+        depth_devices,
+        groups,
+        fourth_pairs + third_pairs + second_pairs + first_pairs,
+        small_grads,
+        3,
+    )
+    ffn2_in_grad, ffn2_out_grad, conv_in_grad, conv_out_grad = (
+        array.astype(jnp.float32) for array in reduced[:4]
+    )
+    attn_in_grad, attn_out_grad, ffn1_in_grad, ffn1_out_grad = (
+        array.astype(jnp.float32) for array in reduced[4:]
+    )
     column_width = norm_gains.shape[1]
     affine_grad = lax.dynamic_slice_in_dim(
         affine_full, lax.axis_index("fsdp") * column_width, column_width, 1
     )
-    gains_grad = jnp.concatenate(
-        [first_red[2][0:1], second_red[2], third_red[2][0:1], fourth_red[2]], axis=0
-    )
     return (
         output,
         input_grad,
-        first_red[2][1],
-        gains_grad,
-        first_red[0],
-        first_red[1],
-        second_red[0],
-        second_red[1],
-        third_red[0],
-        third_red[1],
-        third_red[2][1:],
+        small_sum[5],
+        small_sum[0:5],
+        ffn1_in_grad,
+        ffn1_out_grad,
+        attn_in_grad,
+        attn_out_grad,
+        conv_in_grad,
+        conv_out_grad,
+        small_sum[6 : 6 + KER],
         affine_grad,
-        fourth_red[0],
-        fourth_red[1],
+        ffn2_in_grad,
+        ffn2_out_grad,
     )
 
 
@@ -729,4 +1297,5 @@
         P("fsdp", None),
         P("fsdp", None),
     )
-    return jax.shard_map(functools.partial(local, mesh.shape["fsdp"]), mesh=mesh, in_specs=in_specs, out_specs=out_specs, check_vma=False)
+    body = functools.partial(local, mesh.shape["fsdp"], mesh.shape["dp"] // WAYS)
+    return jax.shard_map(body, mesh=mesh, in_specs=in_specs, out_specs=out_specs, check_vma=False)

time: 1560 us -> 741 us (0.47)
  waiting for transfers between devices: 892 us -> 0 us
  Pallas kernels: 179 us -> 491 us
  blocking collectives: 136 us -> 0 us
  matrix products: 218 us -> 145 us
    reduce_scatter x9 -> x0, waiting for transfers between devices: 673 us -> none  [the longest x4 359 us: reduce_grads(): lax.psum_scatter(grad_in.astype(jnp.bfloat16), 'fsdp', scatter_dimension=...]
    pallas_call x0 -> x3, Pallas kernels: none -> 311 us  [the longest x1 283 us: reduce_all(): pl.pallas_call(functools.partial(reduce_kernel, depth, groups, count, chu...]
    psum x1 -> x0, waiting for transfers between devices: 159 us -> none  [reduce_grads(): lax.psum(shards[0].astype(jnp.bfloat16), 'dp').astype(jnp.float32)]
    psum x4 -> x0, blocking collectives: 136 us -> none  [the longest x1 43.3 us: conv_backward(): lax.psum((jnp.sum(pre_grad, axis=0), jnp.sum(pre_grad * bn_normed, axis=0...]
    dot_general x8 -> x0, matrix products: 60.8 us -> none  [product_tn(): lax.dot_general(left_side, right_side, (((0,), (0,)), ((), ())), preferre...]
    unnamed x16 -> x0, waiting for transfers between devices: 60.4 us -> none
  transfers between devices with their start and end apart: 13 -> 0, of which waited for: 10 -> 0; matrix products, arithmetic and copies ran while one was open for 12% -> 0% of each run, Pallas kernels for 0% -> 0%
where the time goes in v2:
time: 741 us; the launch traced here: 733 us
  Pallas kernels  491 us (66%)
  matrix products  145 us (20%)
  other arithmetic  64.8 us (9%)
  local copies, waits for them, and re-layouts  29.3 us (4%)
    pallas_call x1, Pallas kernels, reduce_all(): pl.pallas_call(functools.partial(reduce_kernel, depth, groups, count, chu...  283 us
    pallas_call x1, Pallas kernels, gather_all(): pl.pallas_call(functools.partial(gather_kernel, depth, count, chunks, 2),...  179 us
    dot_general x8, matrix products, product_nt(): lax.dot_general(left_side, right_side, (((1,), (1,)), ((), ())), preferre...  50.4 us
    dot_general x8, matrix products, product(): return jnp.dot(left_side, right_side, preferred_element_type=jnp.float32)  48.4 us
    pallas_call x2, Pallas kernels, exchange(): pl.pallas_call(functools.partial(exchange_kernel, depth, groups, combine)...  28.5 us
    convert_element_type x8, other arithmetic, local(): array.astype(jnp.float32)  17.5 us
    dot_general x1, matrix products, attention_backward(): jnp.einsum('uhqk,uqhd->ukhd', score_grad, queries, preferred_element_type...  16.6 us
    dot_general x1, matrix products, attention_backward(): jnp.einsum('uhqk,ukhd->uqhd', score_grad, keys_rot, preferred_element_typ...  15.5 us

profile of v2, /device:TPU:0, one launch (start us, length us, event | category | flops | bytes accessed | tf_op | source)
XLA Modules:
  0.0 733.0 jit_solution(6200808640533845022)
XLA Ops:
  2.6 179.5 %shard_map.275 = (bf16[1024,4096]{1,0:T(8,128)(2,1)}, bf16[4096,1024]{1,0:T(8,128)(2,1)}, bf16[1024,3072]{1,0:T(8,128)(2,1)}, bf16[1024,1024]{1,0:T(8,128)(2,1)}...) custom-call(bf16[256,4096]{1,0:T(8,128)(2,1)} %refs_0_.1, ...), custom_call_target="tpu_custom_call" | custom-call | tf_op jit(solution)/shard_map/pallas_call | solution.py:327
  186.4 11.3 %multiply_convert_fusion.4 = (bf16[512,4096]{1,0:T(8,128)(2,1)S(1)}, f32[512,4096]{1,0:T(8,128)}) fusion(bf16[512,1024]{1,0:T(8,128)(2,1)S(1)} %fusion.47.refs_12_, bf16[1024,4096]{1,0:T(8,128)(2,1)} %get-tuple-element.33), kind=kOutput, calls=%fused_computation.12 | convolution fusion | flops 4305453056 | bytes 22020096 | tf_op jit(solution)/shard_map/dot_general | solution.py:20
  197.7 4.7 fusion.126
  203.6 6.2 fusion.130
  237.3 14.5 %shard_map.276 = f32[8,1024]{1,0:T(8,128)} custom-call(f32[8,1024]{1,0:T(8,128)} %pad.21.value), custom_call_target="tpu_custom_call" | custom-call | tf_op jit(solution)/shard_map/pallas_call | solution.py:422
  255.4 3.3 fusion.128
  259.5 10.6 %multiply_convert_fusion.3 = (bf16[512,4096]{1,0:T(8,128)(2,1)S(1)}, f32[512,4096]{1,0:T(8,128)}) fusion(bf16[512,1024]{1,0:T(8,128)(2,1)S(1)} %multiply_convert_fusion.11.refs_0_, bf16[1024,4096]{1,0:T(8,128)(2,1)} %get-tuple-element.39), kind=kOutput, calls=%fused_computation.7 | convolution fusion | flops 4305453056 | bytes 22020096 | tf_op jit(solution)/shard_map/dot_general | solution.py:20
  270.1 8.5 %fusion.129 = (f32[512]{0:T(512)S(1)}, f32[512,1024]{1,0:T(8,128)S(1)}) fusion(f32[512,1024]{1,0:T(8,128)S(1)} %get-tuple-element.138, bf16[512,4096]{1,0:T(8,128)(2,1)S(1)} %get-tuple-element.139.refs_2_, bf16[4096,1024]{1,0:T(8,128)(2,1)} %get-tuple-element.40), kind=kOutput, calls=%fused_computation.242 | convolution fusion | flops 4296539648 | bytes 16779264 | tf_op jit(solution)/shard_map/dot_general | solution.py:20
  281.6 10.4 %multiply_convert_fusion.2.refs_1_ = bf16[512,4096]{1,0:T(8,128)(2,1)S(1)} fusion(f32[512,4096]{1,0:T(8,128)} %get-tuple-element.140, bf16[512,1024]{1,0:T(8,128)(2,1)S(1)} %multiply_convert_fusion.9.refs_3_, bf16[4096,1024]{1,0:T(8,128)(2,1)} %get-tuple-element.40), kind=kOutput, calls=%fused_computation.6 | convolution fusion | flops 4313841664 | bytes 22020096 | tf_op jit(solution)/shard_map/dot_general | solution.py:24
  292.1 9.0 %multiply_reduce_fusion.7 = (f32[1024]{0:T(1024)S(1)}, f32[512]{0:T(512)S(1)}, f32[512]{0:T(512)S(1)}, f32[512,1024]{1,0:T(8,128)S(1)}) fusion(f32[512,1024]{1,0:T(8,128)S(1)} %get-tuple-element.138, f32[512]{0:T(512)S(1)} %add_rsqrt_fusion.2, f32[512]{0:T(512)S(1)} %broadcast_multiply_fusion.11, f32[1024]{0:T(1024)S(1)} %bitcast.257, ...), kind=kOutput, calls=%fused_computation.82 | convolution fusion | flops 4299159552 | bytes 16793600 | tf_op jit(solution)/shard_map/dot_general | solution.py:24
  304.1 3.4 fusion.114
  308.1 14.0 %shard_map.277 = f32[8,1024]{1,0:T(8,128)} custom-call(f32[8,1024]{1,0:T(8,128)} %select_maximum_fusion.value), custom_call_target="tpu_custom_call" | custom-call | tf_op jit(solution)/shard_map/pallas_call | solution.py:422
  323.6 4.4 multiply_reduce_fusion.3
  344.3 6.0 fusion.77
  350.4 16.6 %fusion.66 = f32[1,512,8,128]{3,1,2,0:T(8,128)S(1)} fusion(f32[8,512,512]{1,2,0:T(8,128)} %fusion.77, f32[8,512,512]{1,2,0:T(8,128)} %copy-done.2, f32[8,512]{1,0:T(8,128)S(1)} %log_add_fusion, pred[512]{0:T(512)(128)(4,1)S(1)} %get-tuple-element.148, bf16[512,8,64]{2,0,1:T(8,128)(2,1)} %copy-done.26, bf16[512,8,64]{2,0,1:T(8,128)(2,1)} %copy-done.25), kind=kOutput, calls=%fused_computation.129 | convolution fusion | flops 562041344 | bytes 19939840 | tf_op jit(solution)/shard_map/uhqk,uqhd->ukhd/dot_general | solution.py:997
  367.0 15.5 %fusion.63 = f32[1,512,8,128]{3,1,2,0:T(8,128)} fusion(f32[8,512,512]{1,2,0:T(8,128)} %fusion.77, f32[8,512,512]{1,2,0:T(8,128)} %copy-done.2, f32[8,512]{1,0:T(8,128)S(1)} %log_add_fusion, pred[512]{0:T(512)(128)(4,1)S(1)} %get-tuple-element.148, bf16[512,8,64]{2,0,1:T(8,128)(2,1)S(1)} %copy-done.23, bf16[512,8,64]{2,0,1:T(8,128)(2,1)} %copy-done.24), kind=kOutput, calls=%fused_computation.128 | convolution fusion | flops 562041344 | bytes 19939840 | tf_op jit(solution)/shard_map/uhqk,ukhd->uqhd/dot_general | solution.py:992
  382.5 3.8 add_convert_fusion.1
  390.5 3.3 convolution_convert_fusion
  396.4 7.4 %multiply_reduce_fusion.9 = (f32[1024]{0:T(1024)S(1)}, f32[512]{0:T(512)S(1)}, f32[512]{0:T(512)S(1)}, f32[512,1024]{1,0:T(8,128)S(1)}) fusion(f32[512,1024]{1,0:T(8,128)S(1)} %copy-done.4, f32[512]{0:T(512)S(1)} %copy-done.67, f32[512]{0:T(512)S(1)} %copy-done.60, f32[1024]{0:T(1024)S(1)} %bitcast.241, bf16[1024,3072]{1,0:T(8,128)(2,1)} %get-tuple-element.35, ...), kind=kOutput, calls=%fused_computation.84 | convolution fusion | flops 3234854912 | bytes 13647872 | tf_op jit(solution)/shard_map/dot_general | solution.py:24
  404.8 10.9 %multiply_convert_fusion.refs_13_ = bf16[512,4096]{1,0:T(8,128)(2,1)S(1)} fusion(f32[512,4096]{1,0:T(8,128)} %get-tuple-element.130, bf16[512,1024]{1,0:T(8,128)(2,1)S(1)} %get-tuple-element.77.refs_15_, bf16[4096,1024]{1,0:T(8,128)(2,1)} %get-tuple-element.34), kind=kOutput, calls=%fused_computation.2 | convolution fusion | flops 4313841664 | bytes 22020096 | tf_op jit(solution)/shard_map/dot_general | solution.py:24
  415.8 5.1 fusion.52
  423.5 3.3 pad_maximum_fusion.refs_9_
  429.7 283.0 %shard_map.278 = (bf16[256,4096]{1,0:T(8,128)(2,1)}, bf16[1024,1024]{1,0:T(8,128)(2,1)}, bf16[256,2048]{1,0:T(8,128)(2,1)}, bf16[256,1024]{1,0:T(8,128)(2,1)}, b...) custom-call(bf16[512,1024]{1,0:T(8,128)(2,1)} %copy-done.19, ...), custom_call_target="tpu_custom_call" | custom-call | tf_op jit(solution)/shard_map/pallas_call | solution.py:890
  712.7 4.2 convert_element_type.288
  (274 shorter events, 90.7 us)
Async XLA Ops:
  2.6 181.5 %copy-start.76 = (s32[1,5]{1,0:T(1,128)S(1)}, s32[1,5]{1,0:T(1,128)}, u32[]{:S(2)}) copy-start(s32[1,5]{1,0:T(1,128)} %param.19) | copy-start | bytes 64
  2.6 182.2 %copy-start.10 = (bf16[1,512,1024]{2,1,0:T(8,128)(2,1)S(1)}, bf16[1,512,1024]{2,1,0:T(8,128)(2,1)}, u32[]{:S(2)}) copy-start(bf16[1,512,1024]{2,1,0:T(8,128)(2,1)} %param.17) | copy-start | bytes 3145732
  183.5 14.2 %copy-start.53 = (f32[1,1024]{1,0:T(1,128)}, f32[1,1024]{1,0:T(1,128)S(1)}, u32[]{:S(2)}) copy-start(f32[1,1024]{1,0:T(1,128)S(1)} %get-tuple-element.125) | copy-start | bytes 12292
  184.9 12.8 %copy-start.64 = (pred[512]{0:T(512)(128)(4,1)}, pred[512]{0:T(512)(128)(4,1)S(1)}, u32[]{:S(2)}) copy-start(pred[512]{0:T(512)(128)(4,1)S(1)} %get-tuple-element.76) | copy-start | bytes 1540
  185.8 11.9 %slice-start.4 = ((s8[8388608]{0:T(1024)(128)(4,1)}), s8[4194304]{0:T(1024)(128)(4,1)S(1)}, s32[]{:S(2)}) async-start(s8[8388608]{0:T(1024)(128)(4,1)} %bitcast.290), calls=%async_computation.4 | async-start | bytes 8388608
  186.4 11.3 %copy-start.29 = (bf16[512,1024]{1,0:T(8,128)(2,1)}, bf16[512,1024]{1,0:T(8,128)(2,1)S(1)}, u32[]{:S(2)}) copy-start(bf16[512,1024]{1,0:T(8,128)(2,1)S(1)} %fusion.47.refs_12_) | copy-start | bytes 3145732
  186.4 11.3 %slice-start.5 = ((s8[8388608]{0:T(1024)(128)(4,1)}), s8[4194304]{0:T(1024)(128)(4,1)S(1)}, s32[]{:S(2)}) async-start(s8[8388608]{0:T(1024)(128)(4,1)} %bitcast.290), calls=%async_computation.5 | async-start | bytes 8388608
  202.4 20.8 %copy-start.3 = (f32[512,1024]{1,0:T(8,128)}, f32[512,1024]{1,0:T(8,128)S(1)}, u32[]{:S(2)}) copy-start(f32[512,1024]{1,0:T(8,128)S(1)} %get-tuple-element.132) | copy-start | bytes 6291460
  209.8 10.7 %copy-start.15 = (f32[512,3072]{1,0:T(8,128)}, f32[512,3072]{1,0:T(8,128)S(1)}, u32[]{:S(2)}) copy-start(f32[512,3072]{1,0:T(8,128)S(1)} %fusion.130) | copy-start | bytes 18874372
  259.4 10.7 %copy-start.19 = (bf16[512,1024]{1,0:T(8,128)(2,1)}, bf16[512,1024]{1,0:T(8,128)(2,1)S(1)}, u32[]{:S(2)}) copy-start(bf16[512,1024]{1,0:T(8,128)(2,1)S(1)} %multiply_convert_fusion.11.refs_0_) | copy-start | bytes 3145732
  270.1 8.5 %copy-start.39 = (bf16[512,4096]{1,0:T(8,128)(2,1)}, bf16[512,4096]{1,0:T(8,128)(2,1)S(1)}, u32[]{:S(2)}) copy-start(bf16[512,4096]{1,0:T(8,128)(2,1)S(1)} %get-tuple-element.139.refs_2_) | copy-start | bytes 12582916
  281.6 10.5 %copy-start.20 = (bf16[512,1024]{1,0:T(8,128)(2,1)}, bf16[512,1024]{1,0:T(8,128)(2,1)S(1)}, u32[]{:S(2)}) copy-start(bf16[512,1024]{1,0:T(8,128)(2,1)S(1)} %multiply_convert_fusion.9.refs_3_) | copy-start | bytes 3145732
  292.0 9.0 %copy-start.40 = (bf16[512,4096]{1,0:T(8,128)(2,1)}, bf16[512,4096]{1,0:T(8,128)(2,1)S(1)}, u32[]{:S(2)}) copy-start(bf16[512,4096]{1,0:T(8,128)(2,1)S(1)} %multiply_convert_fusion.2.refs_1_) | copy-start | bytes 12582916
  350.4 16.6 %copy-start.23 = (bf16[512,8,64]{2,0,1:T(8,128)(2,1)S(1)}, bf16[512,8,64]{2,0,1:T(8,128)(2,1)}, u32[]{:S(2)}) copy-start(bf16[512,8,64]{2,0,1:T(8,128)(2,1)} %copy-done.22) | copy-start | bytes 1572868
  387.9 8.4 %copy-start.34 = (bf16[64,8,8,128]{3,1,2,0:T(8,128)(2,1)}, bf16[64,8,8,128]{3,1,2,0:T(8,128)(2,1)S(1)}, u32[]{:S(2)}) copy-start(bf16[64,8,8,128]{3,1,2,0:T(8,128)(2,1)S(1)} %copy.149) | copy-start | bytes 3145732
  403.8 11.8 %slice-start.2 = ((s8[8388608]{0:T(1024)(128)(4,1)}), s8[4194304]{0:T(1024)(128)(4,1)S(1)}, s32[]{:S(2)}) async-start(s8[8388608]{0:T(1024)(128)(4,1)} %bitcast.288), calls=%async_computation.2 | async-start | bytes 8388608
  404.7 11.0 %copy-start.28 = (bf16[512,1024]{1,0:T(8,128)(2,1)}, bf16[512,1024]{1,0:T(8,128)(2,1)S(1)}, u32[]{:S(2)}) copy-start(bf16[512,1024]{1,0:T(8,128)(2,1)S(1)} %get-tuple-element.77.refs_15_) | copy-start | bytes 3145732
  404.7 11.0 %copy-start.11 = (bf16[1,512,1024]{2,1,0:T(8,128)(2,1)S(1)}, bf16[1,512,1024]{2,1,0:T(8,128)(2,1)}, u32[]{:S(2)}) copy-start(bf16[1,512,1024]{2,1,0:T(8,128)(2,1)} %param.17) | copy-start | bytes 3145732
  404.7 11.0 %copy-start.54 = (f32[1,1024]{1,0:T(1,128)S(1)}, f32[1,1024]{1,0:T(1,128)}, u32[]{:S(2)}) copy-start(f32[1,1024]{1,0:T(1,128)} %copy-done.53) | copy-start | bytes 12292
  404.7 11.0 %copy-start.58 = (f32[1,1024]{1,0:T(1,128)S(1)}, f32[1,1024]{1,0:T(1,128)}, u32[]{:S(2)}) copy-start(f32[1,1024]{1,0:T(1,128)} %copy-done.57) | copy-start | bytes 12292
  404.7 11.0 %copy-start.62 = (f32[512]{0:T(512)S(1)}, f32[512]{0:T(512)}, u32[]{:S(2)}) copy-start(f32[512]{0:T(512)} %copy-done.61) | copy-start | bytes 6148
  404.8 11.0 %copy-start.65 = (pred[512]{0:T(512)(128)(4,1)S(1)}, pred[512]{0:T(512)(128)(4,1)}, u32[]{:S(2)}) copy-start(pred[512]{0:T(512)(128)(4,1)} %copy-done.64) | copy-start | bytes 1540
  404.8 11.0 %copy-start.69 = (f32[512]{0:T(512)S(1)}, f32[512]{0:T(512)}, u32[]{:S(2)}) copy-start(f32[512]{0:T(512)} %copy-done.68) | copy-start | bytes 6148
  404.8 11.0 %slice-start.3 = ((s8[8388608]{0:T(1024)(128)(4,1)}), s8[4194304]{0:T(1024)(128)(4,1)S(1)}, s32[]{:S(2)}) async-start(s8[8388608]{0:T(1024)(128)(4,1)} %bitcast.288), calls=%async_computation.3 | async-start | bytes 8388608
  (59 other events, 188.1 us)

commit v3 on v2

--- a/solution.py
+++ b/solution.py
@@ -63,15 +63,6 @@
     back_half = inputs[..., half_size:]
     return jnp.concatenate(
         [front * cosine - back_half * sine, front * sine + back_half * cosine], axis=-1
-    )
-
-
-def unrotate(inputs, cosine, sine):
-    half_size = HEAD // 2
-    front = inputs[..., :half_size]
-    back_half = inputs[..., half_size:]
-    return jnp.concatenate(
-        [front * cosine + back_half * sine, back_half * cosine - front * sine], axis=-1
     )
 
 
@@ -436,16 +427,307 @@
 
 
 LANES = 128
-HELD = 4
-
-
-def reduce_kernel(depth, groups, count, chunks, *refs):
-    lefts, rights, small = refs[0 : 2 * count : 2], refs[1 : 2 * count : 2], refs[2 * count]
-    at = 2 * count + 1
-    outs, small_out = refs[at : at + count], refs[at + count]
-    at += count + 1
+HELD = 3
+TILE = 512
+ROWS = 256
+
+
+def column_tile(index):
+    return pl.ds(index * TILE, TILE)
+
+
+def row_blocks(rows, body):
+    def step(block):
+        body(pl.ds(pl.multiple_of(block * ROWS, ROWS), ROWS))
+
+    pl.loop(0, rows // ROWS)(step)
+
+
+def nt(left_side, right_side):
+    return lax.dot_general(
+        left_side, right_side, (((1,), (1,)), ((), ())), preferred_element_type=jnp.float32
+    )
+
+
+def backward_units(inputs, made, results, scratch, small_first, pair_start):
+    (
+        grad_in,
+        branch_in,
+        queries_in,
+        keys_in,
+        values_in,
+        attn_in_w,
+        attn_out_w,
+        ffn_in_w,
+        ffn_out_w,
+        inner_in,
+        first_in,
+        start_in,
+        log_total,
+        live,
+        masked,
+        cosine,
+        sine,
+        gains,
+        small,
+    ) = inputs
+    joined_out, fresh_out, inner_out = made
+    (input_grad,) = results
+    (
+        heads,
+        joined,
+        row_tiles,
+        column_tiles,
+        inner_tiles,
+        grad,
+        resid,
+        total,
+        gain_rows,
+        sems,
+        row_sems,
+        column_sems,
+        inner_sems,
+        put_sems,
+    ) = scratch
+    frames, width = grad.shape
+    ff_tiles = inner_in.shape[1] // TILE
+    joined_tiles = joined_out.shape[1] // TILE
+    row_plan = [(attn_out_w, index) for index in range(width // TILE)]
+    row_plan += [(ffn_out_w, index) for index in range(ff_tiles)]
+    column_plan = [(attn_in_w, index) for index in range(joined_tiles)]
+    column_plan += [(ffn_in_w, index) for index in range(ff_tiles)]
+
+    def row_copy(at):
+        source, index = row_plan[at]
+        return pltpu.make_async_copy(
+            source.at[pl.ds(index * TILE, TILE)], row_tiles.at[at % 2], row_sems.at[at % 2]
+        )
+
+    def column_copy(at):
+        source, index = column_plan[at]
+        return pltpu.make_async_copy(
+            source.at[:, column_tile(index)], column_tiles.at[at % 2], column_sems.at[at % 2]
+        )
+
+    def inner_copy(at):
+        return pltpu.make_async_copy(
+            inner_in.at[:, column_tile(at)], inner_tiles.at[at % 2], inner_sems.at[at % 2]
+        )
+
+    first_loads = [
+        pltpu.make_async_copy(source, target, sems.at[index])
+        for index, (source, target) in enumerate(
+            (
+                (branch_in, joined.at[:, pl.ds(0, width)]),
+                (queries_in, heads.at[0]),
+                (keys_in, heads.at[1]),
+                (values_in, heads.at[2]),
+                (grad_in, grad),
+                (first_in, resid),
+            )
+        )
+    ]
+
+    def start_loads():
+        for copy in first_loads[:1]:
+            copy.start()
+        for at in range(2):
+            row_copy(at).start()
+        for copy in first_loads[1:]:
+            copy.start()
+        for at in range(2):
+            column_copy(at).start()
+            inner_copy(at).start()
+
+    def merged_grad():
+        first_loads[0].wait()
+        for at in range(width // TILE):
+            row_copy(at).wait()
+
+            def body(rows, at=at):
+                heads[3, rows, column_tile(at)] = nt(
+                    joined[rows, pl.ds(0, width)], row_tiles[at % 2]
+                ).astype(jnp.bfloat16)
+
+            row_blocks(frames, body)
+            row_copy(at + 2).start()
+        for copy in first_loads[1:4]:
+            copy.wait()
+
+    def turned(gradient):
+        return gradient * cosine[...] + pltpu.roll(gradient, HEAD // 2, 1) * sine[...]
+
+    def head_step(head):
+        columns = pl.ds(pl.multiple_of(head * HEAD, HEAD), HEAD)
+        query, key, value = heads[0, :, columns], heads[1, :, columns], heads[2, :, columns]
+        upstream = heads[3, :, columns]
+        scale = HEAD ** (-0.5)
+        scores = jnp.where(live[...] > 0.0, nt(key, query) * scale, NEGATIVE)
+        probs = jnp.exp(scores - log_total[head])
+        value_grad = product(probs.astype(jnp.bfloat16), upstream)
+        prob_grad = nt(value, upstream)
+        row_term = jnp.sum(probs * prob_grad, axis=0, keepdims=True)
+        score_grad = (probs * (prob_grad - row_term) * scale).astype(jnp.bfloat16)
+        key_grad = turned(product(score_grad, query))
+        query_grad = turned(
+            lax.dot_general(
+                score_grad, key, (((0,), (0,)), ((), ())), preferred_element_type=jnp.float32
+            )
+        )
+        for part, value_of in enumerate((query_grad, key_grad, value_grad)):
+            target = pl.ds(pl.multiple_of(part * width + head * HEAD, HEAD), HEAD)
+            joined[:, target] = value_of.astype(jnp.bfloat16)
+
+    def some_heads(low_head, high_head):
+        def unit():
+            pl.loop(low_head, high_head)(head_step)
+
+        return unit
+
+    joined_store = pltpu.make_async_copy(joined, joined_out, sems.at[6])
+    fresh_store = pltpu.make_async_copy(heads.at[0], fresh_out, sems.at[7])
+    start_load = pltpu.make_async_copy(start_in, resid, sems.at[5])
+    grad_store = pltpu.make_async_copy(heads.at[1], input_grad, sems.at[8])
+
+    def add_tile(at, source_of, first):
+        column_copy(at).wait()
+
+        def body(rows):
+            product_part = nt(source_of(rows), column_tiles[at % 2])
+            total[rows] = product_part if first else total[rows] + product_part
+
+        row_blocks(frames, body)
+        if at + 2 < len(column_plan):
+            column_copy(at + 2).start()
+
+    def project(low_tile, high_tile):
+        def unit():
+            if low_tile == 0:
+                joined_store.start()
+            for at in range(low_tile, high_tile):
+                add_tile(at, lambda rows, at=at: joined[rows, column_tile(at)], at == 0)
+
+        return unit
+
+    def norm_step(row, rows, gain):
+        value = resid[rows]
+        centered = value - jnp.mean(value, axis=-1, keepdims=True)
+        inverse = lax.rsqrt(jnp.mean(centered * centered, axis=-1, keepdims=True) + EPSILON)
+        normed = centered * inverse
+        upstream = total[rows]
+        scaled = upstream * gain
+        first_mean = jnp.mean(scaled, axis=-1, keepdims=True)
+        second_mean = jnp.mean(scaled * normed, axis=-1, keepdims=True)
+        gain_rows[row] = gain_rows[row] + jnp.sum(upstream * normed, axis=0, keepdims=True)
+        grad[rows] = grad[rows] + inverse * (scaled - first_mean - normed * second_mean)
+
+    def attention_done():
+        joined_store.wait()
+        pair_start(0)
+        for copy in first_loads[4:]:
+            copy.wait()
+        gain_rows[...] = jnp.zeros_like(gain_rows)
+        gain = gains[1:2]
+
+        def body(rows):
+            norm_step(1, rows, gain)
+            heads[0, rows] = (0.5 * grad[rows]).astype(jnp.bfloat16)
+
+        row_blocks(frames, body)
+        start_load.start()
+        fresh_store.start()
+
+    def inner_put(at):
+        return pltpu.make_async_copy(
+            joined.at[:, column_tile(at % 2)], inner_out.at[:, column_tile(at)], put_sems.at[at % 2]
+        )
+
+    def feed_tiles(low_tile, high_tile):
+        def unit():
+            for at in range(low_tile, high_tile):
+                if at == 0:
+                    fresh_store.wait()
+                    pair_start(1)
+                row_at = width // TILE + at
+                row_copy(row_at).wait()
+                inner_copy(at).wait()
+                if at >= 2:
+                    inner_put(at - 2).wait()
+
+                def body(rows, at=at, row_at=row_at):
+                    active_grad = nt(heads[0, rows], row_tiles[row_at % 2])
+                    inner = inner_tiles[at % 2, rows]
+                    gate = jax.nn.sigmoid(inner)
+                    joined[rows, column_tile(at % 2)] = (
+                        active_grad * (gate * (1.0 + inner * (1.0 - gate)))
+                    ).astype(jnp.bfloat16)
+
+                row_blocks(frames, body)
+                inner_put(at).start()
+                if row_at + 2 < len(row_plan):
+                    row_copy(row_at + 2).start()
+                if at + 2 < ff_tiles:
+                    inner_copy(at + 2).start()
+                add_tile(
+                    joined_tiles + at, lambda rows, at=at: joined[rows, column_tile(at % 2)], at == 0
+                )
+            if high_tile == ff_tiles:
+                for at in range(ff_tiles - 2, ff_tiles):
+                    inner_put(at).wait()
+                pair_start(2)
+
+        return unit
+
+    def feed_done():
+        start_load.wait()
+        gain = gains[0:1]
+
+        def body(rows):
+            norm_step(0, rows, gain)
+            hidden = masked[rows]
+            final = grad[rows]
+            gain_rows[2] = gain_rows[2] + jnp.sum(final * hidden, axis=0, keepdims=True)
+            heads[1, rows] = (final * (1.0 - hidden)).astype(jnp.bfloat16)
+
+        row_blocks(frames, body)
+        grad_store.start()
+        small_first[...] = small[...]
+        small_first[0:1] = gain_rows[0]
+        small_first[1:2] = gain_rows[1]
+        small_first[5:6] = gain_rows[2]
+        grad_store.wait()
+
+    head_count = width // HEAD
+    units = [merged_grad]
+    for at in range(0, head_count, 2):
+        units.append(some_heads(at, at + 2))
+    for at in range(0, joined_tiles, 3):
+        units.append(project(at, at + 3))
+    units.append(attention_done)
+    for at in range(0, ff_tiles, 2):
+        units.append(feed_tiles(at, at + 2))
+    units.append(feed_done)
+    return start_loads, units
+
+
+INPUTS = 19
+
+
+def reduce_kernel(depth, groups, count, chunks, given, late, *refs):
+    extra, refs = refs[:INPUTS], refs[INPUTS:]
+    given_refs, refs = refs[: len(given)], refs[len(given) :]
+    outs, small_out = refs[:count], refs[count]
+    input_grad, made = refs[count + 1], refs[count + 2 : count + 2 + len(late)]
+    at = count + 2 + len(late)
     left_peers, right_peers = refs[at : at + count], refs[at + count : at + 2 * count]
     at += 2 * count
+    slots = dict(zip(given, given_refs))
+    for name, ref in zip(late, made):
+        slots[(name, 1)] = ref
+    lefts = [slots[(index, 0)] for index in range(count)]
+    rights = [slots[(index, 1)] for index in range(count)]
+    unit_scratch, refs = refs[at : at + 14], refs[at + 14 :]
+    at = 0
     (
         left_buf,
         right_buf,
@@ -512,8 +794,23 @@
                 ),
             )
         )
+
+    def pair_start(index):
         for copy in pair_copies[index]:
             copy.start()
+
+    for index in range(count):
+        if index not in late:
+            pair_start(index)
+    start_loads, units = backward_units(
+        extra,
+        made,
+        (input_grad,),
+        unit_scratch,
+        small_work.at[0],
+        lambda number: pair_start(late[number]),
+    )
+    start_loads()
 
     def loads(chunk):
         index, row, part, left_slot, right_slot, new_left, new_right = chunks[chunk]
@@ -779,8 +1076,6 @@
     small_peers = (peer_c, peer_x, peer_y)
 
     def small_turn(turn):
-        if turn == 0:
-            small_work[0] = small[...]
         if 1 <= turn <= 3:
             small_copy(turn - 1, here).wait_recv()
             small_work[turn] = small_work[turn - 1] + small_in[turn - 1]
@@ -812,10 +1107,12 @@
     total_chunks = len(chunks)
     load_start(0)
     for turn in range(total_chunks + 9):
-        if turn < 5:
-            small_turn(turn)
         if turn < total_chunks:
             multiply(turn)
+        if turn < len(units):
+            units[turn]()
+        if 0 <= turn - len(units) < 5:
+            small_turn(turn - len(units))
         for lag, action in (
             (2, add_first),
             (4, add_second),
@@ -868,31 +1165,61 @@
     return chunks
 
 
-def reduce_all(depth, groups, pairs, small, collective):
+def reduce_all(depth, groups, pairs, extra, small, collective):
     count = len(pairs)
     tokens = pairs[0][0].shape[0]
-    block = small.shape[1] // depth
-    chunks = reduce_chunks(depth, pairs, block)
+    width = small.shape[1]
+    block = width // depth
+    shapes = [
+        (left, right if not isinstance(right, int) else jax.ShapeDtypeStruct((tokens, right), left.dtype))
+        for left, right in pairs
+    ]
+    chunks = reduce_chunks(depth, shapes, block)
     total = len(chunks)
-    outs, left_peers, right_peers = [], [], []
-    for left, right in pairs:
-        outs.append(
-            jax.ShapeDtypeStruct((left.shape[1] // depth, right.shape[1]), jnp.bfloat16)
-        )
-        left_peers.append(jax.ShapeDtypeStruct(left.shape, jnp.bfloat16))
-        right_peers.append(jax.ShapeDtypeStruct((tokens, right.shape[1] // 2), jnp.bfloat16))
+    low = jnp.bfloat16
+    given, operands, late = [], [], []
+    for index, (left, right) in enumerate(pairs):
+        given.append((index, 0))
+        operands.append(left)
+        if isinstance(right, int):
+            late.append(index)
+        else:
+            given.append((index, 1))
+            operands.append(right)
+    outs, made, left_peers, right_peers = [], [], [], []
+    for index, (left, right) in enumerate(shapes):
+        outs.append(jax.ShapeDtypeStruct((left.shape[1] // depth, right.shape[1]), low))
+        left_peers.append(jax.ShapeDtypeStruct(left.shape, low))
+        right_peers.append(jax.ShapeDtypeStruct((tokens, right.shape[1] // 2), low))
+        if index in late:
+            made.append(jax.ShapeDtypeStruct(right.shape, low))
     outs.append(jax.ShapeDtypeStruct((small.shape[0], block), jnp.float32))
-    low = jnp.bfloat16
+    outs.append(jax.ShapeDtypeStruct((tokens, width), low))
     messages = 2 + depth + 9 + groups
     any_spec = pl.BlockSpec(memory_space=pl.ANY)
     vmem_spec = pl.BlockSpec(memory_space=pltpu.VMEM)
-    operands = [array for pair in pairs for array in pair]
     results = pl.pallas_call(
-        functools.partial(reduce_kernel, depth, groups, count, chunks),
-        out_shape=outs + left_peers + right_peers,
-        in_specs=[any_spec] * (2 * count) + [vmem_spec],
-        out_specs=[any_spec] * count + [vmem_spec] + [any_spec] * (2 * count),
+        functools.partial(reduce_kernel, depth, groups, count, chunks, given, late),
+        out_shape=outs + made + left_peers + right_peers,
+        in_specs=[any_spec] * 12 + [vmem_spec] * 7 + [any_spec] * len(operands),
+        out_specs=[any_spec] * count
+        + [vmem_spec]
+        + [any_spec] * (1 + len(made) + 2 * count),
         scratch_shapes=[
+            pltpu.VMEM((4, tokens, width), low),
+            pltpu.VMEM((tokens, 3 * width), low),
+            pltpu.VMEM((2, TILE, width), low),
+            pltpu.VMEM((2, width, TILE), low),
+            pltpu.VMEM((2, tokens, TILE), jnp.float32),
+            pltpu.VMEM((tokens, width), jnp.float32),
+            pltpu.VMEM((tokens, width), jnp.float32),
+            pltpu.VMEM((tokens, width), jnp.float32),
+            pltpu.VMEM((3, 1, width), jnp.float32),
+            pltpu.SemaphoreType.DMA((9,)),
+            pltpu.SemaphoreType.DMA((2,)),
+            pltpu.SemaphoreType.DMA((2,)),
+            pltpu.SemaphoreType.DMA((2,)),
+            pltpu.SemaphoreType.DMA((2,)),
             pltpu.VMEM((2, 2 * tokens, depth * block), low),
             pltpu.VMEM((2, 2 * tokens, 4 * LANES), low),
             pltpu.VMEM((HELD, 4, depth, block, LANES), low),
@@ -914,10 +1241,10 @@
             pltpu.SemaphoreType.DMA((3 + groups + depth,)),
         ],
         compiler_params=pltpu.CompilerParams(
-            collective_id=collective, has_side_effects=True, vmem_limit_bytes=58 * 1024 * 1024
+            collective_id=collective, has_side_effects=True, vmem_limit_bytes=62 * 1024 * 1024
         ),
-    )(*operands, small)
-    return results[:count], results[count]
+    )(*extra, small, *operands)
+    return results[:count], results[count], results[count + 1]
 
 
 def ffn_forward(inputs, layer_gain, weight_in, weight_out):
@@ -969,47 +1296,6 @@
         product(merged, weight_out),
         (hidden, normed, inverse, queries, keys_rot, values_low, log_total, merged),
     )
-
-
-def attention_backward(upstream, stored, layer_gain, weight_in, weight_out, key_live, tables):
-    hidden, normed, inverse, queries, keys_rot, values_low, log_total, merged = stored
-    row_count, model_width = upstream.shape
-    branch_grad = upstream.astype(jnp.bfloat16)
-    merged_grad = product_nt(branch_grad, weight_out).astype(jnp.bfloat16).reshape(queries.shape)
-    probs = jnp.exp(attention_scores(queries, keys_rot, key_live) - log_total)
-    prob_grad = jnp.einsum(
-        "uqhd,ukhd->uhqk", merged_grad, values_low, preferred_element_type=jnp.float32
-    )
-    value_grad = jnp.einsum(
-        "uhqk,uqhd->ukhd",
-        probs.astype(jnp.bfloat16),
-        merged_grad,
-        preferred_element_type=jnp.float32,
-    )
-    row_term = jnp.sum(probs * prob_grad, axis=-1, keepdims=True)
-    score_grad = (probs * (prob_grad - row_term) * HEAD ** (-0.5)).astype(jnp.bfloat16)
-    query_grad = unrotate(
-        jnp.einsum("uhqk,ukhd->uqhd", score_grad, keys_rot, preferred_element_type=jnp.float32),
-        tables[0],
-        tables[1],
-    )
-    key_grad = unrotate(
-        jnp.einsum("uhqk,uqhd->ukhd", score_grad, queries, preferred_element_type=jnp.float32),
-        tables[0],
-        tables[1],
-    )
-    joined_grad = jnp.concatenate(
-        [
-            query_grad.reshape(row_count, model_width),
-            key_grad.reshape(row_count, model_width),
-            value_grad.reshape(row_count, model_width),
-        ],
-        axis=1,
-    ).astype(jnp.bfloat16)
-    norm_grad, gain_grad = norm_back(
-        product_nt(joined_grad, weight_in), layer_gain, normed, inverse
-    )
-    return (upstream + norm_grad, [(hidden, joined_grad), (merged, branch_grad)], gain_grad)
 
 
 def conv_forward(inputs, layer_gain, weight_in, weight_out, small_low, live, units, share):
@@ -1197,47 +1483,56 @@
         units,
         share,
     )
-    grad_one, second_pairs, gain_two_grad = attention_backward(
-        grad_two, second_stored, gain_two, second_weights[0], second_weights[1], valid, tables
-    )
-    grad_zero, first_pairs, gain_one_grad = ffn_backward(
-        grad_one, first_stored, gain_one, first_weights[0], first_weights[1]
-    )
-    masked_float = masked_col.astype(jnp.float32)
-    embed_grad = jnp.sum(grad_zero * masked_float, axis=0)
-    input_grad = (
-        (grad_zero * (1.0 - masked_float))
-        .astype(jnp.bfloat16)
-        .reshape(units, frame_count, model_width)
-    )
+    hidden_one, _, _, inner_one, active_one = first_stored
+    hidden_two, _, _, queries, keys_rot, values_low, log_total, merged = second_stored
+    zero_row = jnp.zeros((1, model_width), jnp.float32)
     small_grads = jnp.concatenate(
         [
-            jnp.stack(
-                [
-                    gain_one_grad,
-                    gain_two_grad,
-                    gain_three_grad,
-                    gain_four_grad,
-                    gain_five_grad,
-                    embed_grad,
-                ]
-            ),
+            zero_row,
+            zero_row,
+            gain_three_grad[None, :],
+            gain_four_grad[None, :],
+            gain_five_grad[None, :],
+            zero_row,
             kernel_grad,
             jnp.zeros((5, model_width), jnp.float32),
         ],
         axis=0,
     )
-    reduced, small_sum = reduce_all(
-        depth_devices,
-        groups,
-        fourth_pairs + third_pairs + second_pairs + first_pairs,
-        small_grads,
-        3,
-    )
+    branch_grad = grad_two.astype(jnp.bfloat16)
+    flat = (row_count, model_width)
+    cosine, sine = tables[0][:, 0], tables[1][:, 0]
+    extra = [
+        grad_two,
+        branch_grad,
+        queries.reshape(flat),
+        keys_rot.reshape(flat),
+        values_low.reshape(flat),
+        second_weights[0],
+        second_weights[1],
+        first_weights[0],
+        first_weights[1],
+        inner_one,
+        first,
+        start,
+        log_total.reshape(model_width // HEAD, 1, row_count),
+        live,
+        masked_col.astype(jnp.float32),
+        jnp.concatenate([cosine, cosine], axis=1),
+        jnp.concatenate([sine, -sine], axis=1),
+        small_all[0:8].astype(jnp.float32),
+    ]
+    pairs = fourth_pairs + third_pairs
+    pairs += [(merged, branch_grad), (hidden_two, attn_in.shape[1])]
+    pairs += [(active_one, model_width), (hidden_one, ffn1_in.shape[1])]
+    reduced, small_sum, input_grad = reduce_all(
+        depth_devices, groups, pairs, extra, small_grads, 3
+    )
+    input_grad = input_grad.reshape(units, frame_count, model_width)
     ffn2_in_grad, ffn2_out_grad, conv_in_grad, conv_out_grad = (
         array.astype(jnp.float32) for array in reduced[:4]
     )
-    attn_in_grad, attn_out_grad, ffn1_in_grad, ffn1_out_grad = (
+    attn_out_grad, attn_in_grad, ffn1_out_grad, ffn1_in_grad = (
         array.astype(jnp.float32) for array in reduced[4:]
     )
     column_width = norm_gains.shape[1]

time: 741 us -> 674 us (0.910)
  matrix products: 145 us -> 76.1 us
    dot_general x4 -> x0, matrix products: 41.4 us -> none  [the longest x1 16.6 us: attention_backward(): jnp.einsum('uhqk,uqhd->ukhd', score_grad, queries, preferred_element_type...]
    dot_general x8 -> x4, matrix products: 50.4 us -> 26.8 us  [product_nt(): lax.dot_general(left_side, right_side, (((1,), (1,)), ((), ())), preferre...]
    unnamed x171 -> x92, local copies, waits for them, and re-layouts: 15.1 us -> 14.8 us
where the time goes in v3:
time: 674 us; the launch traced here: 666 us
  Pallas kernels  489 us (73%)
  matrix products  76.1 us (11%)
  other arithmetic  63.8 us (9%)
  local copies, waits for them, and re-layouts  34.2 us (5%)
    pallas_call x1, Pallas kernels, reduce_all(): pl.pallas_call(functools.partial(reduce_kernel, depth, groups, count, chu...  281 us
    pallas_call x1, Pallas kernels, gather_all(): pl.pallas_call(functools.partial(gather_kernel, depth, count, chunks, 2),...  179 us
    dot_general x8, matrix products, product(): return jnp.dot(left_side, right_side, preferred_element_type=jnp.float32)  44.5 us
    pallas_call x2, Pallas kernels, exchange(): pl.pallas_call(functools.partial(exchange_kernel, depth, groups, combine)...  28.4 us
    dot_general x4, matrix products, product_nt(): lax.dot_general(left_side, right_side, (((1,), (1,)), ((), ())), preferre...  26.8 us
    convert_element_type x8, other arithmetic, local(): array.astype(jnp.float32)  17.9 us
    unnamed x92, local copies, waits for them, and re-layouts  14.8 us

profile of v3, /device:TPU:0, one launch (start us, length us, event | category | flops | bytes accessed | tf_op | source)
XLA Modules:
  0.0 665.6 jit_solution(14844345499181039485)
XLA Ops:
  9.0 179.5 %shard_map.275 = (bf16[1024,4096]{1,0:T(8,128)(2,1)}, bf16[4096,1024]{1,0:T(8,128)(2,1)}, bf16[1024,3072]{1,0:T(8,128)(2,1)}, bf16[1024,1024]{1,0:T(8,128)(2,1)}...) custom-call(bf16[256,4096]{1,0:T(8,128)(2,1)} %refs_0_.1, ...), custom_call_target="tpu_custom_call" | custom-call | tf_op jit(solution)/shard_map/pallas_call | solution.py:318
  193.5 11.3 %multiply_convert_fusion.2 = (bf16[512,4096]{1,0:T(8,128)(2,1)S(1)}, f32[512,4096]{1,0:T(8,128)}) fusion(bf16[512,1024]{1,0:T(8,128)(2,1)S(1)} %fusion.34.refs_31_, bf16[1024,4096]{1,0:T(8,128)(2,1)} %get-tuple-element.34.refs_7_), kind=kOutput, calls=%fused_computation.7 | convolution fusion | flops 4305453056 | bytes 22020096 | tf_op jit(solution)/shard_map/dot_general | solution.py:20
  204.8 5.9 convert_select_fusion
  213.9 3.5 fusion.79
  220.6 2.7 copy.75
  233.7 2.5 fusion
  242.2 3.0 copy.76.refs_27_
  256.4 14.5 %shard_map.276 = f32[8,1024]{1,0:T(8,128)} custom-call(f32[8,1024]{1,0:T(8,128)} %pad.21.value), custom_call_target="tpu_custom_call" | custom-call | tf_op jit(solution)/shard_map/pallas_call | solution.py:413
  274.5 3.7 fusion.77
  278.9 7.8 %multiply_convert_fusion.1 = (bf16[512,4096]{1,0:T(8,128)(2,1)S(1)}, f32[512,4096]{1,0:T(8,128)}) fusion(bf16[512,1024]{1,0:T(8,128)(2,1)S(1)} %multiply_convert_fusion.7.refs_19_, bf16[1024,4096]{1,0:T(8,128)(2,1)S(1)} %bitcast.252), kind=kOutput, calls=%fused_computation.2 | convolution fusion | flops 4305453056 | bytes 22020096 | tf_op jit(solution)/shard_map/dot_general | solution.py:20
  286.7 8.5 %fusion.78 = (f32[512]{0:T(512)S(1)}, f32[512,1024]{1,0:T(8,128)S(1)}) fusion(f32[512,1024]{1,0:T(8,128)S(1)} %get-tuple-element.126, bf16[512,4096]{1,0:T(8,128)(2,1)S(1)} %get-tuple-element.127.refs_21_, bf16[4096,1024]{1,0:T(8,128)(2,1)} %get-tuple-element.41), kind=kOutput, calls=%fused_computation.191 | convolution fusion | flops 4296539648 | bytes 16779264 | tf_op jit(solution)/shard_map/dot_general | solution.py:20
  298.2 10.4 %multiply_convert_fusion.refs_20_ = bf16[512,4096]{1,0:T(8,128)(2,1)S(1)} fusion(f32[512,4096]{1,0:T(8,128)} %get-tuple-element.128, bf16[512,1024]{1,0:T(8,128)(2,1)S(1)} %multiply_convert_fusion.5.refs_22_, bf16[4096,1024]{1,0:T(8,128)(2,1)} %get-tuple-element.41), kind=kOutput, calls=%fused_computation.1 | convolution fusion | flops 4313841664 | bytes 22020096 | tf_op jit(solution)/shard_map/dot_general | solution.py:24
  308.7 9.0 %multiply_reduce_fusion.5 = (f32[1024]{0:T(1024)S(1)}, f32[512]{0:T(512)S(1)}, f32[512]{0:T(512)S(1)}, f32[512,1024]{1,0:T(8,128)S(1)}) fusion(f32[512,1024]{1,0:T(8,128)S(1)} %get-tuple-element.126, f32[512]{0:T(512)S(1)} %add_rsqrt_fusion.2, f32[512]{0:T(512)S(1)} %broadcast_multiply_fusion.7, f32[1024]{0:T(1024)S(1)} %bitcast.224, ...), kind=kOutput, calls=%fused_computation.52 | convolution fusion | flops 4299159552 | bytes 16793600 | tf_op jit(solution)/shard_map/dot_general | solution.py:24
  317.7 3.1 fusion.69
  320.9 3.4 fusion.67
  324.9 14.0 %shard_map.277 = f32[8,1024]{1,0:T(8,128)} custom-call(f32[8,1024]{1,0:T(8,128)} %select_maximum_fusion.value), custom_call_target="tpu_custom_call" | custom-call | tf_op jit(solution)/shard_map/pallas_call | solution.py:413
  339.7 4.4 multiply_reduce_fusion.2
  351.0 4.0 multiply_reduce_fusion.6
  357.8 4.6 fusion.68
  362.4 280.9 %shard_map.278 = (bf16[256,4096]{1,0:T(8,128)(2,1)}, bf16[1024,1024]{1,0:T(8,128)(2,1)}, bf16[256,2048]{1,0:T(8,128)(2,1)}, bf16[256,1024]{1,0:T(8,128)(2,1)}, b...) custom-call(f32[512,1024]{1,0:T(8,128)} %get-tuple-element.70.refs_0, ...), custom_call_target="tpu_custom_call" | custom-call | tf_op jit(solution)/shard_map/pallas_call | solution.py:1201
  654.2 2.5 convert_element_type.266
  656.7 2.5 convert_element_type.267
  659.2 2.5 convert_element_type.272
  661.7 2.5 convert_element_type.273
  (184 shorter events, 76.5 us)
Async XLA Ops:
  8.9 183.1 %copy-start.2 = (bf16[1,512,1024]{2,1,0:T(8,128)(2,1)S(1)}, bf16[1,512,1024]{2,1,0:T(8,128)(2,1)}, u32[]{:S(2)}) copy-start(bf16[1,512,1024]{2,1,0:T(8,128)(2,1)} %param.17) | copy-start | bytes 3145732
  188.4 4.5 copy-start.33
  193.0 11.8 %slice-start = ((s8[8388608]{0:T(1024)(128)(4,1)}), s8[4194304]{0:T(1024)(128)(4,1)S(1)}, s32[]{:S(2)}) async-start(s8[8388608]{0:T(1024)(128)(4,1)} %bitcast.178), calls=%async_computation | async-start | bytes 8388608
  193.0 20.8 %slice-start.2 = ((s8[6291456]{0:T(1024)(128)(4,1)}), s8[4194304]{0:T(1024)(128)(4,1)S(1)}, s32[]{:S(2)}) async-start(s8[6291456]{0:T(1024)(128)(4,1)} %bitcast.180), calls=%async_computation.2 | async-start | bytes 8388608
  193.5 11.3 %copy-start.16 = (bf16[512,1024]{1,0:T(8,128)(2,1)}, bf16[512,1024]{1,0:T(8,128)(2,1)S(1)}, u32[]{:S(2)}) copy-start(bf16[512,1024]{1,0:T(8,128)(2,1)S(1)} %fusion.34.refs_31_) | copy-start | bytes 3145732
  193.5 11.3 %slice-start.1 = ((s8[8388608]{0:T(1024)(128)(4,1)}), s8[4194304]{0:T(1024)(128)(4,1)S(1)}, s32[]{:S(2)}) async-start(s8[8388608]{0:T(1024)(128)(4,1)} %bitcast.178), calls=%async_computation.1 | async-start | bytes 8388608
  193.5 20.3 %slice-start.3 = ((s8[6291456]{0:T(1024)(128)(4,1)}), s8[2097152]{0:T(1024)(128)(4,1)S(1)}, s32[]{:S(2)}) async-start(s8[6291456]{0:T(1024)(128)(4,1)} %bitcast.180), calls=%async_computation.3 | async-start | bytes 4194304
  204.8 5.9 copy-start.18
  210.7 3.1 copy-start.9
  213.9 3.5 copy-start.17
  242.2 4.0 copy-start.3
  270.9 3.5 copy-start.4
  273.8 5.1 slice-start.4
  274.5 3.7 copy-start.12
  274.5 4.4 slice-start.5
  278.9 7.8 %copy-start.13 = (bf16[512,1024]{1,0:T(8,128)(2,1)}, bf16[512,1024]{1,0:T(8,128)(2,1)S(1)}, u32[]{:S(2)}) copy-start(bf16[512,1024]{1,0:T(8,128)(2,1)S(1)} %multiply_convert_fusion.7.refs_19_) | copy-start | bytes 3145732
  286.7 8.5 %copy-start.19 = (bf16[512,4096]{1,0:T(8,128)(2,1)}, bf16[512,4096]{1,0:T(8,128)(2,1)S(1)}, u32[]{:S(2)}) copy-start(bf16[512,4096]{1,0:T(8,128)(2,1)S(1)} %get-tuple-element.127.refs_21_) | copy-start | bytes 12582916
  298.2 10.5 %copy-start.14 = (bf16[512,1024]{1,0:T(8,128)(2,1)}, bf16[512,1024]{1,0:T(8,128)(2,1)S(1)}, u32[]{:S(2)}) copy-start(bf16[512,1024]{1,0:T(8,128)(2,1)S(1)} %multiply_convert_fusion.5.refs_22_) | copy-start | bytes 3145732
  308.7 9.0 %copy-start.20 = (bf16[512,4096]{1,0:T(8,128)(2,1)}, bf16[512,4096]{1,0:T(8,128)(2,1)S(1)}, u32[]{:S(2)}) copy-start(bf16[512,4096]{1,0:T(8,128)(2,1)S(1)} %multiply_convert_fusion.refs_20_) | copy-start | bytes 12582916
  317.7 3.1 copy-start.36
  320.8 3.4 copy-start.15
  339.7 4.4 copy-start.7
  643.3 7.1 %copy-start.29 = (bf16[256,2048]{1,0:T(8,128)(2,1)S(1)}, bf16[256,2048]{1,0:T(8,128)(2,1)}, u32[]{:S(2)}) copy-start(bf16[256,2048]{1,0:T(8,128)(2,1)} %get-tuple-element.48) | copy-start | bytes 3145732
  648.2 3.8 copy-start.28
  (19 other events, 37.9 us)

commit v4 on v3

--- a/solution.py
+++ b/solution.py
@@ -57,15 +57,6 @@
     return (jnp.cos(angles)[:, None, :], jnp.sin(angles)[:, None, :])
 
 
-def rotate(inputs, cosine, sine):
-    half_size = HEAD // 2
-    front = inputs[..., :half_size]
-    back_half = inputs[..., half_size:]
-    return jnp.concatenate(
-        [front * cosine - back_half * sine, front * sine + back_half * cosine], axis=-1
-    )
-
-
 MESH = pl.DeviceIdType.MESH
 WAYS = 8
 
@@ -92,10 +83,266 @@
     pl.semaphore_wait(barrier, 2 + len(flat_peers))
 
 
+TILE = 512
+ROWS = 256
+ALONG_LINE = ()
+GATHER_LAGS = (2, 4, 6)
+GATHER_LEAD = 3
+PER_TURN = 3
+
+
+def column_tile(index):
+    return pl.ds(index * TILE, TILE)
+
+
+def row_blocks(rows, body):
+    def step(block):
+        body(pl.ds(pl.multiple_of(block * ROWS, ROWS), ROWS))
+
+    pl.loop(0, rows // ROWS)(step)
+
+
+def nt(left_side, right_side):
+    return lax.dot_general(
+        left_side, right_side, (((1,), (1,)), ((), ())), preferred_element_type=jnp.float32
+    )
+
+
+def forward_units(inputs, weights, results, scratch, small_full):
+    tokens, masked, live, cosine, sine = inputs
+    ffn_in_w, ffn_out_w, attn_in_w, attn_out_w = weights
+    (
+        start_out,
+        hidden_one_out,
+        inner_out,
+        active_out,
+        first_out,
+        hidden_two_out,
+        queries_out,
+        keys_out,
+        values_out,
+        log_out,
+        merged_out,
+        second_out,
+    ) = results
+    (
+        resid,
+        total,
+        hidden,
+        active,
+        heads,
+        merged,
+        row_tiles,
+        column_tiles,
+        inner_tiles,
+        gains,
+        sems,
+        row_sems,
+        column_sems,
+        inner_sems,
+    ) = scratch
+    frames, width = resid.shape
+    ff_tiles = active.shape[1] // TILE
+    head_tiles = width // TILE
+
+    def row_copy(source):
+        return lambda at: pltpu.make_async_copy(
+            source.at[pl.ds(at * TILE, TILE)], row_tiles.at[at % 2], row_sems.at[at % 2]
+        )
+
+    def column_copy(source):
+        return lambda at: pltpu.make_async_copy(
+            source.at[:, column_tile(at)], column_tiles.at[at % 2], column_sems.at[at % 2]
+        )
+
+    def stream(copy_of, low_tile, high_tile, count, body):
+        if low_tile == 0:
+            for at in range(min(2, count)):
+                copy_of(at).start()
+        for at in range(low_tile, high_tile):
+            copy_of(at).wait()
+            body(at)
+            if at + 2 < count:
+                copy_of(at + 2).start()
+
+    def put(source, target, index):
+        return pltpu.make_async_copy(source, target, sems.at[index])
+
+    start_put = put(resid, start_out, 0)
+    hidden_one_put = put(hidden, hidden_one_out, 1)
+    active_put = put(active, active_out, 2)
+    first_put = put(resid, first_out, 3)
+    hidden_two_put = put(hidden, hidden_two_out, 4)
+    head_puts = [
+        put(heads.at[part], target, 5 + part)
+        for part, target in enumerate((queries_out, keys_out, values_out))
+    ]
+    merged_put = put(merged, merged_out, 8)
+    second_put = put(total, second_out, 9)
+
+    def normed(value, gain):
+        centered = value - jnp.mean(value, axis=-1, keepdims=True)
+        inverse = lax.rsqrt(jnp.mean(centered * centered, axis=-1, keepdims=True) + EPSILON)
+        return (centered * inverse * gain).astype(jnp.bfloat16)
+
+    def prepare():
+        depth, _, piece = small_full.shape
+        for owner in range(depth):
+            gains[:, owner * piece : (owner + 1) * piece] = small_full[owner].astype(jnp.float32)
+        gain, embed = gains[0:1], gains[5:6]
+
+        def body(rows):
+            value = jnp.where(masked[rows] > 0.0, embed, tokens[rows].astype(jnp.float32))
+            resid[rows] = value
+            hidden[rows] = normed(value, gain)
+
+        row_blocks(frames, body)
+        start_put.start()
+        hidden_one_put.start()
+
+    def inner_put(at):
+        return pltpu.make_async_copy(
+            inner_tiles.at[at % 2], inner_out.at[:, column_tile(at)], inner_sems.at[at % 2]
+        )
+
+    def widen(low_tile, high_tile):
+        def unit():
+            def body(at):
+                if at >= 2:
+                    inner_put(at - 2).wait()
+
+                def step(rows):
+                    inner = product(hidden[rows], column_tiles[at % 2])
+                    inner_tiles[at % 2, rows] = inner
+                    active[rows, column_tile(at)] = (inner * jax.nn.sigmoid(inner)).astype(
+                        jnp.bfloat16
+                    )
+
+                row_blocks(frames, step)
+                inner_put(at).start()
+
+            stream(column_copy(ffn_in_w), low_tile, high_tile, ff_tiles, body)
+            if high_tile == ff_tiles:
+                active_put.start()
+                for at in range(ff_tiles - 2, ff_tiles):
+                    inner_put(at).wait()
+
+        return unit
+
+    def narrow(low_tile, high_tile):
+        def unit():
+            def body(at):
+                def step(rows):
+                    part = product(active[rows, column_tile(at)], row_tiles[at % 2])
+                    total[rows] = part if at == 0 else total[rows] + part
+
+                row_blocks(frames, step)
+
+            stream(row_copy(ffn_out_w), low_tile, high_tile, ff_tiles, body)
+
+        return unit
+
+    def first_done():
+        start_put.wait()
+        hidden_one_put.wait()
+        active_put.wait()
+        gain = gains[1:2]
+
+        def body(rows):
+            value = resid[rows] + 0.5 * total[rows]
+            resid[rows] = value
+            hidden[rows] = normed(value, gain)
+
+        row_blocks(frames, body)
+        first_put.start()
+        hidden_two_put.start()
+
+    def split_heads(low_tile, high_tile):
+        def unit():
+            def body(at):
+                part = at // head_tiles
+
+                def step(rows):
+                    value = product(hidden[rows], column_tiles[at % 2])
+                    for head in range(TILE // HEAD):
+                        piece = value[:, head * HEAD : (head + 1) * HEAD]
+                        if part < 2:
+                            piece = piece * cosine[rows] + pltpu.roll(piece, HEAD // 2, 1) * sine[rows]
+                        first = (at % head_tiles) * TILE + head * HEAD
+                        heads[part, rows, pl.ds(first, HEAD)] = piece.astype(jnp.bfloat16)
+
+                row_blocks(frames, step)
+
+            stream(column_copy(attn_in_w), low_tile, high_tile, 3 * head_tiles, body)
+            if high_tile == 3 * head_tiles:
+                for copy in head_puts:
+                    copy.start()
+
+        return unit
+
+    def head_step(head):
+        columns = pl.ds(pl.multiple_of(head * HEAD, HEAD), HEAD)
+        query, key, value = heads[0, :, columns], heads[1, :, columns], heads[2, :, columns]
+        scores = jnp.where(live[...] > 0.0, nt(key, query) * HEAD ** (-0.5), NEGATIVE)
+        top_score = jnp.max(scores, axis=0, keepdims=True)
+        raised = jnp.exp(scores - top_score)
+        amount = jnp.sum(raised, axis=0, keepdims=True)
+        log_out[head] = top_score + jnp.log(amount)
+        probs = (raised * (1.0 / amount)).astype(jnp.bfloat16)
+        merged[:, columns] = lax.dot_general(
+            probs, value, (((0,), (0,)), ((), ())), preferred_element_type=jnp.float32
+        ).astype(jnp.bfloat16)
+
+    def some_heads(low_head, high_head):
+        def unit():
+            pl.loop(low_head, high_head)(head_step)
+
+        return unit
+
+    def attention_done():
+        merged_put.start()
+
+        def body(at):
+            def step(rows):
+                part = product(merged[rows, column_tile(at)], row_tiles[at % 2])
+                total[rows] = (resid[rows] if at == 0 else total[rows]) + part
+
+            row_blocks(frames, step)
+
+        stream(row_copy(attn_out_w), 0, head_tiles, head_tiles, body)
+        second_put.start()
+
+    def finish():
+        for copy in [first_put, hidden_two_put, merged_put, second_put] + head_puts:
+            copy.wait()
+
+    units = [(None, prepare)]
+    for at in range(0, ff_tiles, 2):
+        units.append((0, widen(at, at + 2)))
+    for at in range(0, ff_tiles, 4):
+        units.append((1, narrow(at, at + 4)))
+    units.append((1, first_done))
+    for at in range(0, 3 * head_tiles, 3):
+        units.append((2, split_heads(at, at + 3)))
+    for at in range(0, width // HEAD, 2):
+        units.append((2, some_heads(at, at + 2)))
+    units.append((3, attention_done))
+    return units, finish
+
+
+FORWARD_INPUTS = 5
+FORWARD_RESULTS = 12
+FORWARD_SCRATCH = 14
+
+
 def gather_kernel(depth, count, chunks, lead, *refs):
+    extra, refs = refs[:FORWARD_INPUTS], refs[FORWARD_INPUTS:]
     shards, small = refs[:count], refs[count]
     fulls, small_full = refs[count + 1 : 2 * count + 1], refs[2 * count + 1]
-    send_sems, recv_sems, own_sems, small_sems = refs[2 * count + 2 :]
+    refs = refs[2 * count + 2 :]
+    results, refs = refs[:FORWARD_RESULTS], refs[FORWARD_RESULTS:]
+    unit_scratch, refs = refs[:FORWARD_SCRATCH], refs[FORWARD_SCRATCH:]
+    send_sems, recv_sems, own_sems, small_sems = refs
     dp, z, core_bit, x_bit, y_bit = coordinates()
     mine = lax.rem(dp, WAYS)
     step_c, step_x, step_y = 1 - 2 * core_bit, 2 - 4 * x_bit, 4 - 8 * y_bit
@@ -111,6 +358,8 @@
         index, first, width = chunks[chunk]
         rows = shards[index].shape[0]
         part = rows // WAYS
+        if index in ALONG_LINE:
+            part = rows // 2
         if half is not None:
             width = width // 2
             first = first + half * width
@@ -162,11 +411,13 @@
 
     def line_start(chunk):
         index, first, width = chunks[chunk]
-        part = shards[index].shape[0] // WAYS
+        whole_line = index in ALONG_LINE
+        part = shards[index].shape[0] // (2 if whole_line else WAYS)
+        piece = core_bit if whole_line else mine
         source = shards[index].at[
-            pl.ds(pl.multiple_of(mine * part, part), part), pl.ds(first, width)
+            pl.ds(pl.multiple_of(piece * part, part), part), pl.ds(first, width)
         ]
-        target = slot(chunk, z, mine, None)
+        target = slot(chunk, z, piece, None)
 
         @pl.when(z + 1 < depth)
         def _():
@@ -180,16 +431,24 @@
                 source, target, send_sems.at[chunk, 1, 0], recv_sems.at[chunk, 1, 0], (dp, z - 1)
             ).start()
 
+    def along_line(chunk):
+        return chunks[chunk][0] in ALONG_LINE
+
     def line_arrived(chunk):
+        piece = core_bit if along_line(chunk) else mine
+
         def action(index, owner, hop, way):
-            place(chunk, index, 0, owner, mine, here).wait_recv()
+            place(chunk, index, 0, owner, piece, here).wait_recv()
             if hop < depth - 2:
                 following = z + way
 
                 @pl.when((following >= 0) & (following < depth))
                 def _():
-                    place(chunk, index + 2, 0, owner, mine, (dp, following)).start()
-
+                    place(chunk, index + 2, 0, owner, piece, (dp, following)).start()
+
+            if along_line(chunk):
+                place(chunk, index, 5, owner, piece, core_dev).start()
+                return
             place(chunk, index, 1, owner, mine, x_dev).start()
             place(chunk, index, 2, owner, mine, y_dev).start()
             place(chunk, index, 5, owner, mine, core_dev).start()
@@ -217,6 +476,9 @@
 
     def core_arrived(chunk):
         def action(index, owner, hop, way):
+            if along_line(chunk):
+                place(chunk, index, 5, owner, 1 - core_bit, here).wait_recv()
+                return
             place(chunk, index, 5, owner, other, here).wait_recv()
             place(chunk, index, 6, owner, other_x, here).wait_recv()
             place(chunk, index, 7, owner, other_y, here).wait_recv()
@@ -246,22 +508,37 @@
         )
         copy.start()
         own_copies.append(copy)
-    for turn in range(total + 3):
+    last_chunk = {index: chunk for chunk, (index, _, _) in enumerate(chunks)}
+    seen = set()
+    units, finish = forward_units(extra, fulls[:4], results, unit_scratch, small_full)
+    plane_lag, corner_lag, core_lag = GATHER_LAGS
+    for turn in range(total + core_lag):
         if turn + lead < total:
             line_start(turn + lead)
         if turn < total:
             line_arrived(turn)
         if turn == 0:
             each(small_action)
-        if 0 <= turn - 1 < total:
-            plane_arrived(turn - 1)
-        if 0 <= turn - 2 < total:
-            corner_arrived(turn - 2)
-        if 0 <= turn - 3 < total:
-            core_arrived(turn - 3)
-    for copy in own_copies:
-        copy.wait()
-    small_local.wait()
+            small_local.wait()
+        if 0 <= turn - plane_lag < total and not along_line(turn - plane_lag):
+            plane_arrived(turn - plane_lag)
+        if 0 <= turn - corner_lag < total and not along_line(turn - corner_lag):
+            corner_arrived(turn - corner_lag)
+        if 0 <= turn - core_lag < total:
+            core_arrived(turn - core_lag)
+        for _ in range(PER_TURN):
+            if units and (units[0][0] is None or last_chunk[units[0][0]] <= turn - core_lag):
+                needed, unit = units.pop(0)
+                if needed is not None and needed not in seen:
+                    seen.add(needed)
+                    own_copies[needed].wait_recv()
+                unit()
+    assert not units
+    finish()
+    for index, copy in enumerate(own_copies):
+        if index not in seen:
+            copy.wait_recv()
+        copy.wait_send()
 
     @pl.when(z + 1 < depth)
     def _():
@@ -281,14 +558,15 @@
 
     each(small_drain)
     for chunk in range(total):
+        piece = core_bit if along_line(chunk) else mine
 
         @pl.when(z + 1 < depth)
         def _():
-            place(chunk, 0, 0, z, mine, here).wait_send()
+            place(chunk, 0, 0, z, piece, here).wait_send()
 
         @pl.when(z > 0)
         def _():
-            place(chunk, 1, 0, z, mine, here).wait_send()
+            place(chunk, 1, 0, z, piece, here).wait_send()
 
         def drain(index, owner, hop, way):
             if hop < depth - 2:
@@ -296,8 +574,11 @@
 
                 @pl.when((following >= 0) & (following < depth))
                 def _():
-                    place(chunk, index + 2, 0, owner, mine, here).wait_send()
-
+                    place(chunk, index + 2, 0, owner, piece, here).wait_send()
+
+            if along_line(chunk):
+                place(chunk, index, 5, owner, piece, here).wait_send()
+                return
             for message in (1, 2, 5, 6, 7):
                 place(chunk, index, message, owner, mine, here).wait_send()
             for message in (3, 4, 8, 9):
@@ -306,28 +587,73 @@
         each(drain)
 
 
-def gather_all(depth, weights, small):
+def gather_all(depth, weights, splits, small, tokens, masked, live, tables):
     count = len(weights)
-    chunks = [(index, 0, weight.shape[1]) for index, weight in enumerate(weights)]
+    chunks = []
+    for index, weight in enumerate(weights):
+        width = weight.shape[1] // splits[index]
+        chunks += [(index, part * width, width) for part in range(splits[index])]
     shape = (len(chunks), 2 * (depth - 1), 10)
-    outs = [
-        jax.ShapeDtypeStruct((weight.shape[0] * depth, weight.shape[1]), weight.dtype)
-        for weight in weights
+    frames, width = tokens.shape
+    wide = weights[0].shape[1]
+    heads = width // HEAD
+    low, full = jnp.bfloat16, jnp.float32
+
+    def array(shape, dtype):
+        return jax.ShapeDtypeStruct(shape, dtype)
+
+    outs = [array((weight.shape[0] * depth, weight.shape[1]), low) for weight in weights]
+    outs.append(array((depth,) + small.shape, small.dtype))
+    square = (frames, width)
+    outs += [
+        array(square, full),
+        array(square, low),
+        array((frames, wide), full),
+        array((frames, wide), low),
+        array(square, full),
+        array(square, low),
+        array(square, low),
+        array(square, low),
+        array(square, low),
+        array((heads, 1, frames), full),
+        array(square, low),
+        array(square, full),
     ]
-    outs.append(jax.ShapeDtypeStruct((depth,) + small.shape, small.dtype))
+    any_spec = pl.BlockSpec(memory_space=pl.ANY)
+    vmem_spec = pl.BlockSpec(memory_space=pltpu.VMEM)
     return pl.pallas_call(
-        functools.partial(gather_kernel, depth, count, chunks, 2),
+        functools.partial(gather_kernel, depth, count, chunks, GATHER_LEAD),
         out_shape=outs,
-        in_specs=[pl.BlockSpec(memory_space=pl.ANY)] * (count + 1),
-        out_specs=[pl.BlockSpec(memory_space=pl.ANY)] * (count + 1),
+        in_specs=[vmem_spec] * FORWARD_INPUTS + [any_spec] * (count + 1),
+        out_specs=[any_spec] * count
+        + [vmem_spec]
+        + [any_spec] * 9
+        + [vmem_spec]
+        + [any_spec] * 2,
         scratch_shapes=[
+            pltpu.VMEM(square, full),
+            pltpu.VMEM(square, full),
+            pltpu.VMEM(square, low),
+            pltpu.VMEM((frames, wide), low),
+            pltpu.VMEM((3,) + square, low),
+            pltpu.VMEM(square, low),
+            pltpu.VMEM((2, TILE, width), low),
+            pltpu.VMEM((2, width, TILE), low),
+            pltpu.VMEM((2, frames, TILE), full),
+            pltpu.VMEM((small.shape[0], width), full),
+            pltpu.SemaphoreType.DMA((10,)),
+            pltpu.SemaphoreType.DMA((2,)),
+            pltpu.SemaphoreType.DMA((2,)),
+            pltpu.SemaphoreType.DMA((2,)),
             pltpu.SemaphoreType.DMA(shape),
             pltpu.SemaphoreType.DMA(shape),
             pltpu.SemaphoreType.DMA((count + 1, 2)),
             pltpu.SemaphoreType.DMA((2 * (depth - 1), 2)),
         ],
-        compiler_params=pltpu.CompilerParams(collective_id=0, has_side_effects=True),
-    )(*weights, small)
+        compiler_params=pltpu.CompilerParams(
+            collective_id=0, has_side_effects=True, vmem_limit_bytes=58 * 1024 * 1024
+        ),
+    )(tokens, masked, live, *tables, *weights, small)
 
 
 def add_pair(left, right):
@@ -428,25 +754,9 @@
 
 LANES = 128
 HELD = 3
-TILE = 512
-ROWS = 256
-
-
-def column_tile(index):
-    return pl.ds(index * TILE, TILE)
-
-
-def row_blocks(rows, body):
-    def step(block):
-        body(pl.ds(pl.multiple_of(block * ROWS, ROWS), ROWS))
-
-    pl.loop(0, rows // ROWS)(step)
-
-
-def nt(left_side, right_side):
-    return lax.dot_general(
-        left_side, right_side, (((1,), (1,)), ((), ())), preferred_element_type=jnp.float32
-    )
+LINE_FIRST = ()
+PLANE_LAGS = (2, 5, 8, 11, 14, 16)
+LINE_LAGS = (5, 6, 7, 8, 9, 10)
 
 
 def backward_units(inputs, made, results, scratch, small_first, pair_start):
@@ -732,9 +1042,13 @@
         left_buf,
         right_buf,
         held,
+        line_held,
         first_in,
         second_in,
         line_in,
+        whole_in,
+        half_in,
+        quarter_in,
         far_in,
         final,
         small_work,
@@ -799,9 +1113,7 @@
         for copy in pair_copies[index]:
             copy.start()
 
-    for index in range(count):
-        if index not in late:
-            pair_start(index)
+    pair_start(0)
     start_loads, units = backward_units(
         extra,
         made,
@@ -859,6 +1171,8 @@
             arrived.add(index)
             for copy in pair_copies[index]:
                 copy.wait_recv()
+            if index + 1 < count and index + 1 not in late:
+                pair_start(index + 1)
         for copy in loads(chunk):
             copy.start()
 
@@ -872,11 +1186,23 @@
             return 2 * first_bit + second_bit
         return 2 * second_bit + first_bit
 
+    plane_at, line_at = {}, {}
+    for chunk in range(len(chunks)):
+        places = line_at if chunk in LINE_FIRST else plane_at
+        places[chunk] = len(places)
+
     def first_copy(chunk, which, device):
         _, _, first_bit, _ = axes(chunk)
+        quarter = quarter_of(chunk, 1 - first_bit, which)
+        if chunk in line_at:
+            source = whole_in.at[line_at[chunk], 0, quarter]
+            target = half_in.at[line_at[chunk], which]
+        else:
+            source = held.at[chunk % HELD, quarter]
+            target = first_in.at[plane_at[chunk], which]
         return remote(
-            held.at[chunk % HELD, quarter_of(chunk, 1 - first_bit, which)],
-            first_in.at[chunk, which],
+            source,
+            target,
             send_sems.at[chunk, which],
             recv_sems.at[chunk, which],
             device,
@@ -884,22 +1210,44 @@
 
     def second_copy(chunk, device):
         _, _, _, second_bit = axes(chunk)
+        if chunk in line_at:
+            source = half_in.at[line_at[chunk], 1 - second_bit]
+            target = quarter_in.at[line_at[chunk]]
+        else:
+            source = first_in.at[plane_at[chunk], 1 - second_bit]
+            target = second_in.at[plane_at[chunk]]
         return remote(
-            first_in.at[chunk, 1 - second_bit],
-            second_in.at[chunk],
+            source,
+            target,
             send_sems.at[chunk, 2],
             recv_sems.at[chunk, 2],
             device,
         )
 
     def line_copy(chunk, step, device):
+        owner = lax.rem(z + step, depth)
+        if chunk in line_at:
+            source = line_held.at[line_at[chunk], :, owner]
+            target = whole_in.at[line_at[chunk], step - 1]
+        else:
+            source = second_in.at[plane_at[chunk], owner]
+            target = line_in.at[plane_at[chunk], step - 1]
         return remote(
-            second_in.at[chunk, lax.rem(z + step, depth)],
-            line_in.at[chunk, step - 1],
+            source,
+            target,
             send_sems.at[chunk, 2 + step],
             recv_sems.at[chunk, 2 + step],
             device,
         )
+
+    def held_sent(chunk):
+        if chunk not in line_at:
+            for which in range(2):
+                first_copy(chunk, which, here).wait_send()
+
+    def line_start(chunk):
+        for step in range(1, depth):
+            line_copy(chunk, step, (dp, lax.rem(z + step, depth))).start()
 
     def multiply(chunk):
         index, row, part, left_slot, right_slot, new_left, new_right = chunks[chunk]
@@ -908,8 +1256,7 @@
         if chunk + 1 < len(chunks):
             load_start(chunk + 1)
         if chunk >= HELD:
-            for which in range(2):
-                first_copy(chunk - HELD, which, here).wait_send()
+            held_sent(chunk - HELD)
 
         def body(owner):
             columns = pl.ds(pl.multiple_of(owner * block, block), block)
@@ -920,38 +1267,79 @@
                 preferred_element_type=jnp.float32,
             ).astype(jnp.bfloat16)
             for quarter in range(4):
-                held[chunk % HELD, quarter, owner] = product[
-                    :, quarter * LANES : (quarter + 1) * LANES
-                ]
+                piece = product[:, quarter * LANES : (quarter + 1) * LANES]
+                if chunk in line_at:
+                    line_held[line_at[chunk], quarter, owner] = piece
+                else:
+                    held[chunk % HELD, quarter, owner] = piece
 
         pl.loop(0, depth)(body)
+        if chunk in line_at:
+            line_start(chunk)
+            return
         first_peer, _, _, _ = axes(chunk)
         for which in range(2):
             first_copy(chunk, which, (first_peer, z)).start()
 
-    def add_first(chunk):
+    def line_total(chunk):
+        place = line_at[chunk]
+        for step in range(1, depth):
+            line_copy(chunk, step, here).wait_recv()
+        for quarter in range(4):
+            total = line_held[place, quarter, z].astype(jnp.float32)
+            for step in range(1, depth):
+                total = total + whole_in[place, step - 1, quarter].astype(jnp.float32)
+            whole_in[place, 0, quarter] = total.astype(jnp.bfloat16)
+        first_peer, _, _, _ = axes(chunk)
+        for which in range(2):
+            first_copy(chunk, which, (first_peer, z)).start()
+
+    def line_first_sum(chunk):
+        place = line_at[chunk]
         _, second_peer, first_bit, second_bit = axes(chunk)
         for which in range(2):
             first_copy(chunk, which, here).wait_recv()
 
         def add(which):
-            first_in[chunk, which] = (
-                first_in[chunk, which].astype(jnp.float32)
-                + held[chunk % HELD, quarter_of(chunk, first_bit, which)].astype(jnp.float32)
+            half_in[place, which] = (
+                half_in[place, which].astype(jnp.float32)
+                + whole_in[place, 0, quarter_of(chunk, first_bit, which)].astype(jnp.float32)
             ).astype(jnp.bfloat16)
 
         add(1 - second_bit)
         second_copy(chunk, (second_peer, z)).start()
         add(second_bit)
 
+    def add_first(chunk):
+        if chunk in line_at:
+            line_total(chunk)
+            return
+        place = plane_at[chunk]
+        _, second_peer, first_bit, second_bit = axes(chunk)
+        for which in range(2):
+            first_copy(chunk, which, here).wait_recv()
+
+        def add(which):
+            first_in[place, which] = (
+                first_in[place, which].astype(jnp.float32)
+                + held[chunk % HELD, quarter_of(chunk, first_bit, which)].astype(jnp.float32)
+            ).astype(jnp.bfloat16)
+
+        add(1 - second_bit)
+        second_copy(chunk, (second_peer, z)).start()
+        add(second_bit)
+
     def add_second(chunk):
+        if chunk in line_at:
+            line_first_sum(chunk)
+            return
+        place = plane_at[chunk]
         _, _, _, second_bit = axes(chunk)
         second_copy(chunk, here).wait_recv()
-        second_in[chunk] = (
-            second_in[chunk].astype(jnp.float32) + first_in[chunk, second_bit].astype(jnp.float32)
+        second_in[place] = (
+            second_in[place].astype(jnp.float32) + first_in[place, second_bit].astype(jnp.float32)
         ).astype(jnp.bfloat16)
-        for step in range(1, depth):
-            line_copy(chunk, step, (dp, lax.rem(z + step, depth))).start()
+        line_start(chunk)
 
     base = 2 + depth
 
@@ -998,12 +1386,23 @@
             device,
         )
 
-    def finish(chunk):
+    def piece_total(chunk):
+        if chunk in line_at:
+            _, _, _, second_bit = axes(chunk)
+            second_copy(chunk, here).wait_recv()
+            place = line_at[chunk]
+            return half_in[place, second_bit].astype(jnp.float32) + quarter_in[place].astype(
+                jnp.float32
+            )
         for step in range(1, depth):
             line_copy(chunk, step, here).wait_recv()
-        total = second_in[chunk, z].astype(jnp.float32)
+        total = second_in[plane_at[chunk], z].astype(jnp.float32)
         for step in range(1, depth):
-            total = total + line_in[chunk, step - 1].astype(jnp.float32)
+            total = total + line_in[plane_at[chunk], step - 1].astype(jnp.float32)
+        return total
+
+    def finish(chunk):
+        total = piece_total(chunk)
         if groups > 1:
             own = total.astype(jnp.bfloat16)
             far_in[chunk, groups] = own
@@ -1106,23 +1505,20 @@
 
     total_chunks = len(chunks)
     load_start(0)
-    for turn in range(total_chunks + 9):
+    stages = (add_first, add_second, finish, plane_arrived, corner_arrived, core_arrived)
+    agenda = {}
+    for chunk in range(total_chunks):
+        for lag, action in zip(LINE_LAGS if chunk in line_at else PLANE_LAGS, stages):
+            agenda.setdefault(chunk + lag, []).append((chunk, action))
+    for turn in range(max(agenda) + 1):
         if turn < total_chunks:
             multiply(turn)
         if turn < len(units):
             units[turn]()
         if 0 <= turn - len(units) < 5:
             small_turn(turn - len(units))
-        for lag, action in (
-            (2, add_first),
-            (4, add_second),
-            (5, finish),
-            (6, plane_arrived),
-            (7, corner_arrived),
-            (8, core_arrived),
-        ):
-            if 0 <= turn - lag < total_chunks:
-                action(turn - lag)
+        for chunk, action in sorted(agenda.get(turn, []), key=lambda item: -item[0]):
+            action(chunk)
     for index in range(count):
         for copy in pair_copies[index]:
             copy.wait_send()
@@ -1132,11 +1528,13 @@
         small_line_copy(step, here).wait_send()
     for chunk in range(total_chunks):
         if chunk >= total_chunks - HELD:
+            held_sent(chunk)
+        if chunk in line_at:
             for which in range(2):
                 first_copy(chunk, which, here).wait_send()
-        second_copy(chunk, here).wait_send()
         for step in range(1, depth):
             line_copy(chunk, step, here).wait_send()
+        second_copy(chunk, here).wait_send()
         for message in range(3):
             from_final(chunk, message, here).wait_send()
         for message in (5, 6):
@@ -1176,6 +1574,7 @@
     ]
     chunks = reduce_chunks(depth, shapes, block)
     total = len(chunks)
+    lines = len([chunk for chunk in range(total) if chunk in LINE_FIRST])
     low = jnp.bfloat16
     given, operands, late = [], [], []
     for index, (left, right) in enumerate(pairs):
@@ -1223,9 +1622,13 @@
             pltpu.VMEM((2, 2 * tokens, depth * block), low),
             pltpu.VMEM((2, 2 * tokens, 4 * LANES), low),
             pltpu.VMEM((HELD, 4, depth, block, LANES), low),
-            pltpu.VMEM((total, 2, depth, block, LANES), low),
-            pltpu.VMEM((total, depth, block, LANES), low),
-            pltpu.VMEM((total, depth - 1, block, LANES), low),
+            pltpu.VMEM((max(lines, 1), 4, depth, block, LANES) if lines else (1, 1, 1, 16, LANES), low),
+            pltpu.VMEM((total - lines, 2, depth, block, LANES), low),
+            pltpu.VMEM((total - lines, depth, block, LANES), low),
+            pltpu.VMEM((total - lines, depth - 1, block, LANES), low),
+            pltpu.VMEM((max(lines, 1), depth - 1, 4, block, LANES), low),
+            pltpu.VMEM((max(lines, 1), 2, block, LANES), low),
+            pltpu.VMEM((max(lines, 1), block, LANES), low),
             pltpu.VMEM((total, groups + 1, block, LANES) if groups > 1 else (1, 1, 16, LANES), low),
             pltpu.VMEM((total, block, LANES), low),
             pltpu.VMEM((5,) + small.shape, jnp.float32),
@@ -1262,40 +1665,6 @@
     inner_grad = (active_grad * swish_slope(inner)).astype(jnp.bfloat16)
     norm_grad, gain_grad = norm_back(product_nt(inner_grad, weight_in), layer_gain, normed, inverse)
     return (upstream + norm_grad, [(hidden, inner_grad), (active, branch_grad)], gain_grad)
-
-
-def attention_scores(queries, keys_rot, key_live):
-    raw_scores = jnp.einsum(
-        "uqhd,ukhd->uhqk", queries, keys_rot, preferred_element_type=jnp.float32
-    )
-    return jnp.where(key_live[:, None, None, :], raw_scores * HEAD ** (-0.5), NEGATIVE)
-
-
-def attention_forward(inputs, layer_gain, weight_in, weight_out, key_live, tables, units):
-    row_count, model_width = inputs.shape
-    shape_heads = (units, row_count // units, model_width // HEAD, HEAD)
-    out_norm, normed, inverse = layer_norm(inputs, layer_gain)
-    hidden = out_norm.astype(jnp.bfloat16)
-    joined = product(hidden, weight_in)
-    queries = rotate(joined[:, :model_width].reshape(shape_heads), tables[0], tables[1]).astype(
-        jnp.bfloat16
-    )
-    keys_rot = rotate(
-        joined[:, model_width : 2 * model_width].reshape(shape_heads), tables[0], tables[1]
-    ).astype(jnp.bfloat16)
-    values_low = joined[:, 2 * model_width :].reshape(shape_heads).astype(jnp.bfloat16)
-    scores = attention_scores(queries, keys_rot, key_live)
-    top_score = jnp.max(scores, axis=-1, keepdims=True)
-    log_total = top_score + jnp.log(jnp.sum(jnp.exp(scores - top_score), axis=-1, keepdims=True))
-    probs_low = jnp.exp(scores - log_total).astype(jnp.bfloat16)
-    heads_out = jnp.einsum(
-        "uhqk,ukhd->uqhd", probs_low, values_low, preferred_element_type=jnp.float32
-    )
-    merged = heads_out.reshape(row_count, model_width).astype(jnp.bfloat16)
-    return (
-        product(merged, weight_out),
-        (hidden, normed, inverse, queries, keys_rot, values_low, log_total, merged),
-    )
 
 
 def conv_forward(inputs, layer_gain, weight_in, weight_out, small_low, live, units, share):
@@ -1431,30 +1800,42 @@
     masked = jnp.any(inside, axis=1) & valid
     live = valid.reshape(row_count, 1).astype(jnp.float32)
     masked_col = masked.reshape(row_count, 1)
-    tables = rotation(frame_count)
+    cosine, sine = rotation(frame_count)
+    cosine, sine = cosine[:, 0], sine[:, 0]
+    cosine_row = jnp.concatenate([cosine, cosine], axis=1)
+    sine_row = jnp.concatenate([-sine, sine], axis=1)
     small = jnp.concatenate([norm_gains, mask_embed[None, :], depth, bn_affine], axis=0)
     small = jnp.pad(small, ((0, 16 - small.shape[0]), (0, 0)))
     gathered = gather_all(
         depth_devices,
         [ffn1_in, ffn1_out, attn_in, attn_out, conv_in, conv_out, ffn2_in, ffn2_out],
+        (2, 2, 2, 1, 1, 1, 2, 2),
         small,
-    )
+        tokens.reshape(row_count, model_width),
+        masked_col.astype(jnp.float32),
+        live,
+        (cosine_row, sine_row),
+    )
+    (
+        start,
+        hidden_one,
+        inner_one,
+        active_one,
+        first,
+        hidden_two,
+        queries,
+        keys_rot,
+        values_low,
+        log_total,
+        merged,
+        second,
+    ) = gathered[9:]
     small_all = gathered[8].transpose(1, 0, 2).reshape(16, model_width)
     third_small = jnp.concatenate([small_all[2:3], small_all[6:13]], axis=0)
-    first_weights = (gathered[0], gathered[1], small_all[jnp.array([0, 5])])
-    second_weights = (gathered[2], gathered[3], small_all[1:2])
+    first_weights = (gathered[0], gathered[1])
+    second_weights = (gathered[2], gathered[3])
     third_weights = (gathered[4], gathered[5], third_small)
     fourth_weights = (gathered[6], gathered[7], small_all[3:5])
-    gain_one = first_weights[2][0].astype(jnp.float32)
-    embed = first_weights[2][1].astype(jnp.float32)
-    start = jnp.where(masked_col, embed, tokens.reshape(row_count, model_width).astype(jnp.float32))
-    branch, first_stored = ffn_forward(start, gain_one, first_weights[0], first_weights[1])
-    first = start + 0.5 * branch
-    gain_two = second_weights[2][0].astype(jnp.float32)
-    branch, second_stored = attention_forward(
-        first, gain_two, second_weights[0], second_weights[1], valid, tables, units
-    )
-    second = first + branch
     gain_three = third_weights[2][0].astype(jnp.float32)
     share = functools.partial(exchange, depth_devices, groups)
     branch, third_stored = conv_forward(
@@ -1483,8 +1864,6 @@
         units,
         share,
     )
-    hidden_one, _, _, inner_one, active_one = first_stored
-    hidden_two, _, _, queries, keys_rot, values_low, log_total, merged = second_stored
     zero_row = jnp.zeros((1, model_width), jnp.float32)
     small_grads = jnp.concatenate(
         [
@@ -1500,14 +1879,12 @@
         axis=0,
     )
     branch_grad = grad_two.astype(jnp.bfloat16)
-    flat = (row_count, model_width)
-    cosine, sine = tables[0][:, 0], tables[1][:, 0]
     extra = [
         grad_two,
         branch_grad,
-        queries.reshape(flat),
-        keys_rot.reshape(flat),
-        values_low.reshape(flat),
+        queries,
+        keys_rot,
+        values_low,
         second_weights[0],
         second_weights[1],
         first_weights[0],
@@ -1515,11 +1892,11 @@
         inner_one,
         first,
         start,
-        log_total.reshape(model_width // HEAD, 1, row_count),
+        log_total,
         live,
         masked_col.astype(jnp.float32),
-        jnp.concatenate([cosine, cosine], axis=1),
-        jnp.concatenate([sine, -sine], axis=1),
+        cosine_row,
+        -sine_row,
         small_all[0:8].astype(jnp.float32),
     ]
     pairs = fourth_pairs + third_pairs

time: 674 us -> 621 us (0.921)
  matrix products: 76.1 us -> 48.6 us
  local copies, waits for them, and re-layouts: 34.2 us -> 14.3 us
    dot_general x8 -> x4, matrix products: 44.5 us -> 19.9 us  [product(): return jnp.dot(left_side, right_side, preferred_element_type=jnp.float32)]
    unnamed x92 -> x53, local copies, waits for them, and re-layouts: 14.8 us -> 6.92 us
where the time goes in v4:
time: 621 us; the launch traced here: 613 us
  Pallas kernels  488 us (79%)
  other arithmetic  60.4 us (10%)
  matrix products  48.6 us (8%)
  local copies, waits for them, and re-layouts  14.3 us (2%)
    pallas_call x1, Pallas kernels, reduce_all(): pl.pallas_call(functools.partial(reduce_kernel, depth, groups, count, chu...  274 us
    pallas_call x1, Pallas kernels, gather_all(): pl.pallas_call(functools.partial(gather_kernel, depth, count, chunks, GAT...  184 us
    pallas_call x2, Pallas kernels, exchange(): pl.pallas_call(functools.partial(exchange_kernel, depth, groups, combine)...  29 us
    dot_general x4, matrix products, product_nt(): lax.dot_general(left_side, right_side, (((1,), (1,)), ((), ())), preferre...  28.8 us
    dot_general x4, matrix products, product(): return jnp.dot(left_side, right_side, preferred_element_type=jnp.float32)  19.9 us
    convert_element_type x8, other arithmetic, local(): array.astype(jnp.float32)  17.9 us

profile of v4, /device:TPU:0, one launch (start us, length us, event | category | flops | bytes accessed | tf_op | source)
XLA Modules:
  0.0 613.0 jit_solution(6093009848937343889)
XLA Ops:
  9.0 184.2 %shard_map.266 = (bf16[1024,4096]{1,0:T(8,128)(2,1)}, bf16[4096,1024]{1,0:T(8,128)(2,1)}, bf16[1024,3072]{1,0:T(8,128)(2,1)}, bf16[1024,1024]{1,0:T(8,128)(2,1)}...) custom-call(bf16[512,1024]{1,0:T(8,128)(2,1)} %bitcast.119, ...), custom_call_target="tpu_custom_call" | custom-call | tf_op jit(solution)/shard_map/pallas_call | solution.py:624
  197.7 2.4 fusion.49
  202.1 2.9 fusion.12
  208.3 15.1 %shard_map.267 = f32[8,1024]{1,0:T(8,128)} custom-call(f32[8,1024]{1,0:T(8,128)} %pad.21.value), custom_call_target="tpu_custom_call" | custom-call | tf_op jit(solution)/shard_map/pallas_call | solution.py:739
  226.2 2.4 multiply_convert_fusion.7.refs_25_
  231.3 7.6 %multiply_convert_fusion.1 = (bf16[512,4096]{1,0:T(8,128)(2,1)S(1)}, f32[512,4096]{1,0:T(8,128)}) fusion(bf16[512,1024]{1,0:T(8,128)(2,1)S(1)} %multiply_convert_fusion.6.refs_19_, bf16[1024,4096]{1,0:T(8,128)(2,1)S(1)} %bitcast.172), kind=kOutput, calls=%fused_computation.1 | convolution fusion | flops 4305453056 | bytes 22020096 | tf_op jit(solution)/shard_map/dot_general | solution.py:20
  238.9 8.5 %fusion.48 = (f32[512]{0:T(512)S(1)}, f32[512,1024]{1,0:T(8,128)S(1)}) fusion(f32[512,1024]{1,0:T(8,128)S(1)} %get-tuple-element.126, bf16[512,4096]{1,0:T(8,128)(2,1)S(1)} %get-tuple-element.127.refs_21_, bf16[4096,1024]{1,0:T(8,128)(2,1)} %get-tuple-element.50), kind=kOutput, calls=%fused_computation.131 | convolution fusion | flops 4296539648 | bytes 16779264 | tf_op jit(solution)/shard_map/dot_general | solution.py:20
  250.4 10.4 %multiply_convert_fusion.refs_20_ = bf16[512,4096]{1,0:T(8,128)(2,1)S(1)} fusion(f32[512,4096]{1,0:T(8,128)} %get-tuple-element.128, bf16[512,1024]{1,0:T(8,128)(2,1)S(1)} %multiply_convert_fusion.4.refs_22_, bf16[4096,1024]{1,0:T(8,128)(2,1)} %get-tuple-element.50), kind=kOutput, calls=%fused_computation | convolution fusion | flops 4313841664 | bytes 22020096 | tf_op jit(solution)/shard_map/dot_general | solution.py:24
  260.9 9.0 %multiply_reduce_fusion.5 = (f32[1024]{0:T(1024)S(1)}, f32[512]{0:T(512)S(1)}, f32[512]{0:T(512)S(1)}, f32[512,1024]{1,0:T(8,128)S(1)}) fusion(f32[512,1024]{1,0:T(8,128)S(1)} %get-tuple-element.126, f32[512]{0:T(512)S(1)} %add_rsqrt_fusion.2, f32[512]{0:T(512)S(1)} %broadcast_multiply_fusion.7, f32[1024]{0:T(1024)S(1)} %bitcast.146, ...), kind=kOutput, calls=%fused_computation.37 | convolution fusion | flops 4299159552 | bytes 16793600 | tf_op jit(solution)/shard_map/dot_general | solution.py:24
  269.9 2.7 fusion.42
  272.6 5.3 fusion.39
  278.6 13.9 %shard_map.268 = f32[8,1024]{1,0:T(8,128)} custom-call(f32[8,1024]{1,0:T(8,128)} %select_maximum_fusion.value), custom_call_target="tpu_custom_call" | custom-call | tf_op jit(solution)/shard_map/pallas_call | solution.py:739
  293.4 5.0 multiply_reduce_fusion.2
  300.5 2.3 multiply_convert_fusion.3
  305.0 4.0 multiply_reduce_fusion.6
  311.8 4.6 fusion.41
  316.4 274.3 %shard_map.269 = (bf16[256,4096]{1,0:T(8,128)(2,1)}, bf16[1024,1024]{1,0:T(8,128)(2,1)}, bf16[256,2048]{1,0:T(8,128)(2,1)}, bf16[256,1024]{1,0:T(8,128)(2,1)}, b...) custom-call(f32[512,1024]{1,0:T(8,128)} %get-tuple-element.96.refs_0, ...), custom_call_target="tpu_custom_call" | custom-call | tf_op jit(solution)/shard_map/pallas_call | solution.py:1600
  593.4 2.1 convert_element_type.180
  595.5 2.2 convert_element_type.182
  599.4 2.0 convert_element_type.179
  601.6 2.5 convert_element_type.177
  604.1 2.5 convert_element_type.178
  606.6 2.5 convert_element_type.183
  609.1 2.5 convert_element_type.184
  (111 shorter events, 39.7 us)
Async XLA Ops:
  193.3 2.2 copy-start.2
  193.3 2.6 copy-start.20
  195.5 2.2 copy-start.21
  197.7 2.4 copy-start.6
  200.1 2.0 copy-start
  202.1 2.9 copy-start.3
  223.3 5.3 copy-start.23
  226.2 4.5 slice-start
  228.6 2.7 slice-start.1
  231.3 7.6 %copy-start.8 = (bf16[512,1024]{1,0:T(8,128)(2,1)}, bf16[512,1024]{1,0:T(8,128)(2,1)S(1)}, u32[]{:S(2)}) copy-start(bf16[512,1024]{1,0:T(8,128)(2,1)S(1)} %multiply_convert_fusion.6.refs_19_) | copy-start | bytes 3145732
  238.9 8.5 %copy-start.11 = (bf16[512,4096]{1,0:T(8,128)(2,1)}, bf16[512,4096]{1,0:T(8,128)(2,1)S(1)}, u32[]{:S(2)}) copy-start(bf16[512,4096]{1,0:T(8,128)(2,1)S(1)} %get-tuple-element.127.refs_21_) | copy-start | bytes 12582916
  250.4 10.5 %copy-start.9 = (bf16[512,1024]{1,0:T(8,128)(2,1)}, bf16[512,1024]{1,0:T(8,128)(2,1)S(1)}, u32[]{:S(2)}) copy-start(bf16[512,1024]{1,0:T(8,128)(2,1)S(1)} %multiply_convert_fusion.4.refs_22_) | copy-start | bytes 3145732
  260.8 9.0 %copy-start.12 = (bf16[512,4096]{1,0:T(8,128)(2,1)}, bf16[512,4096]{1,0:T(8,128)(2,1)S(1)}, u32[]{:S(2)}) copy-start(bf16[512,4096]{1,0:T(8,128)(2,1)S(1)} %multiply_convert_fusion.refs_20_) | copy-start | bytes 12582916
  272.6 5.3 copy-start.10
  293.4 5.0 copy-start.4
  298.4 2.2 copy-start.1
  302.9 2.2 copy-start.22
  590.7 7.1 %copy-start.18 = (bf16[256,2048]{1,0:T(8,128)(2,1)S(1)}, bf16[256,2048]{1,0:T(8,128)(2,1)}, u32[]{:S(2)}) copy-start(bf16[256,2048]{1,0:T(8,128)(2,1)} %get-tuple-element.72) | copy-start | bytes 3145732
  595.5 3.8 copy-start.17
  599.4 2.2 copy-start.16
  601.6 2.5 copy-start.15
  604.1 2.5 copy-start.14
  606.6 2.5 copy-start.13
  609.1 2.5 copy-start.19
  (2 other events, 2.6 us)

commit v5 on v4

--- a/solution.py
+++ b/solution.py
@@ -85,7 +85,7 @@
 
 TILE = 512
 ROWS = 256
-ALONG_LINE = ()
+ALONG_LINE = (5,)
 GATHER_LAGS = (2, 4, 6)
 GATHER_LEAD = 3
 PER_TURN = 3
@@ -754,9 +754,9 @@
 
 LANES = 128
 HELD = 3
-LINE_FIRST = ()
-PLANE_LAGS = (2, 5, 8, 11, 14, 16)
-LINE_LAGS = (5, 6, 7, 8, 9, 10)
+LINE_FIRST = (3, 8, 13, 17)
+PLANE_LAGS = (2, 5, 9, 12, 15, 17)
+LINE_LAGS = (5, 8, 10, 13, 16, 18)
 
 
 def backward_units(inputs, made, results, scratch, small_first, pair_start):
@@ -1023,6 +1023,10 @@
 INPUTS = 19
 
 
+def line_chunks(groups):
+    return LINE_FIRST if groups == 1 else LINE_FIRST[:1]
+
+
 def reduce_kernel(depth, groups, count, chunks, given, late, *refs):
     extra, refs = refs[:INPUTS], refs[INPUTS:]
     given_refs, refs = refs[: len(given)], refs[len(given) :]
@@ -1188,7 +1192,7 @@
 
     plane_at, line_at = {}, {}
     for chunk in range(len(chunks)):
-        places = line_at if chunk in LINE_FIRST else plane_at
+        places = line_at if chunk in line_chunks(groups) else plane_at
         places[chunk] = len(places)
 
     def first_copy(chunk, which, device):
@@ -1574,7 +1578,7 @@
     ]
     chunks = reduce_chunks(depth, shapes, block)
     total = len(chunks)
-    lines = len([chunk for chunk in range(total) if chunk in LINE_FIRST])
+    lines = len([chunk for chunk in range(total) if chunk in line_chunks(groups)])
     low = jnp.bfloat16
     given, operands, late = [], [], []
     for index, (left, right) in enumerate(pairs):

time: 621 us -> 596 us (0.960)
  Pallas kernels: 488 us -> 463 us
    pallas_call x1, Pallas kernels: 274 us -> 254 us  [reduce_all(): pl.pallas_call(functools.partial(reduce_kernel, depth, groups, count, chu...]
where the time goes in v5:
time: 596 us; the launch traced here: 588 us
  Pallas kernels  463 us (78%)
  other arithmetic  60.2 us (10%)
  matrix products  48.6 us (8%)
  local copies, waits for them, and re-layouts  14.3 us (2%)
    pallas_call x1, Pallas kernels, reduce_all(): pl.pallas_call(functools.partial(reduce_kernel, depth, groups, count, chu...  254 us
    pallas_call x1, Pallas kernels, gather_all(): pl.pallas_call(functools.partial(gather_kernel, depth, count, chunks, GAT...  181 us
    pallas_call x2, Pallas kernels, exchange(): pl.pallas_call(functools.partial(exchange_kernel, depth, groups, combine)...  28.9 us
    dot_general x4, matrix products, product_nt(): lax.dot_general(left_side, right_side, (((1,), (1,)), ((), ())), preferre...  28.7 us
    dot_general x4, matrix products, product(): return jnp.dot(left_side, right_side, preferred_element_type=jnp.float32)  19.9 us
    convert_element_type x8, other arithmetic, local(): array.astype(jnp.float32)  17.9 us

profile of v5, /device:TPU:0, one launch (start us, length us, event | category | flops | bytes accessed | tf_op | source)
XLA Modules:
  0.0 588.0 jit_solution(16937368994547787693)
XLA Ops:
  9.0 180.6 %shard_map.266 = (bf16[1024,4096]{1,0:T(8,128)(2,1)}, bf16[4096,1024]{1,0:T(8,128)(2,1)}, bf16[1024,3072]{1,0:T(8,128)(2,1)}, bf16[1024,1024]{1,0:T(8,128)(2,1)}...) custom-call(bf16[512,1024]{1,0:T(8,128)(2,1)} %bitcast.119, ...), custom_call_target="tpu_custom_call" | custom-call | tf_op jit(solution)/shard_map/pallas_call | solution.py:624
  194.0 2.4 fusion.49
  198.4 2.9 fusion.12
  204.6 15.1 %shard_map.267 = f32[8,1024]{1,0:T(8,128)} custom-call(f32[8,1024]{1,0:T(8,128)} %pad.21.value), custom_call_target="tpu_custom_call" | custom-call | tf_op jit(solution)/shard_map/pallas_call | solution.py:739
  222.6 2.4 multiply_convert_fusion.7.refs_25_
  227.6 7.6 %multiply_convert_fusion.1 = (bf16[512,4096]{1,0:T(8,128)(2,1)S(1)}, f32[512,4096]{1,0:T(8,128)}) fusion(bf16[512,1024]{1,0:T(8,128)(2,1)S(1)} %multiply_convert_fusion.6.refs_19_, bf16[1024,4096]{1,0:T(8,128)(2,1)S(1)} %bitcast.172), kind=kOutput, calls=%fused_computation.1 | convolution fusion | flops 4305453056 | bytes 22020096 | tf_op jit(solution)/shard_map/dot_general | solution.py:20
  235.3 8.5 %fusion.48 = (f32[512]{0:T(512)S(1)}, f32[512,1024]{1,0:T(8,128)S(1)}) fusion(f32[512,1024]{1,0:T(8,128)S(1)} %get-tuple-element.126, bf16[512,4096]{1,0:T(8,128)(2,1)S(1)} %get-tuple-element.127.refs_21_, bf16[4096,1024]{1,0:T(8,128)(2,1)} %get-tuple-element.50), kind=kOutput, calls=%fused_computation.131 | convolution fusion | flops 4296539648 | bytes 16779264 | tf_op jit(solution)/shard_map/dot_general | solution.py:20
  246.7 10.4 %multiply_convert_fusion.refs_20_ = bf16[512,4096]{1,0:T(8,128)(2,1)S(1)} fusion(f32[512,4096]{1,0:T(8,128)} %get-tuple-element.128, bf16[512,1024]{1,0:T(8,128)(2,1)S(1)} %multiply_convert_fusion.4.refs_22_, bf16[4096,1024]{1,0:T(8,128)(2,1)} %get-tuple-element.50), kind=kOutput, calls=%fused_computation | convolution fusion | flops 4313841664 | bytes 22020096 | tf_op jit(solution)/shard_map/dot_general | solution.py:24
  257.2 9.0 %multiply_reduce_fusion.5 = (f32[1024]{0:T(1024)S(1)}, f32[512]{0:T(512)S(1)}, f32[512]{0:T(512)S(1)}, f32[512,1024]{1,0:T(8,128)S(1)}) fusion(f32[512,1024]{1,0:T(8,128)S(1)} %get-tuple-element.126, f32[512]{0:T(512)S(1)} %add_rsqrt_fusion.2, f32[512]{0:T(512)S(1)} %broadcast_multiply_fusion.7, f32[1024]{0:T(1024)S(1)} %bitcast.146, ...), kind=kOutput, calls=%fused_computation.37 | convolution fusion | flops 4299159552 | bytes 16793600 | tf_op jit(solution)/shard_map/dot_general | solution.py:24
  266.2 2.7 fusion.42
  268.9 5.3 fusion.39
  274.9 13.9 %shard_map.268 = f32[8,1024]{1,0:T(8,128)} custom-call(f32[8,1024]{1,0:T(8,128)} %select_maximum_fusion.value), custom_call_target="tpu_custom_call" | custom-call | tf_op jit(solution)/shard_map/pallas_call | solution.py:739
  289.6 5.0 multiply_reduce_fusion.2
  296.8 2.1 multiply_convert_fusion.3
  301.1 4.0 multiply_reduce_fusion.6
  307.9 4.6 fusion.41
  312.5 253.6 %shard_map.269 = (bf16[256,4096]{1,0:T(8,128)(2,1)}, bf16[1024,1024]{1,0:T(8,128)(2,1)}, bf16[256,2048]{1,0:T(8,128)(2,1)}, bf16[256,1024]{1,0:T(8,128)(2,1)}, b...) custom-call(f32[512,1024]{1,0:T(8,128)} %get-tuple-element.96.refs_0, ...), custom_call_target="tpu_custom_call" | custom-call | tf_op jit(solution)/shard_map/pallas_call | solution.py:1604
  568.7 2.1 convert_element_type.180
  570.9 2.2 convert_element_type.182
  574.7 2.0 convert_element_type.179
  576.9 2.5 convert_element_type.177
  579.4 2.5 convert_element_type.178
  581.9 2.5 convert_element_type.183
  584.4 2.5 convert_element_type.184
  (111 shorter events, 39.7 us)
Async XLA Ops:
  189.6 2.2 copy-start.2
  189.6 2.6 copy-start.20
  191.8 2.2 copy-start.21
  194.0 2.4 copy-start.6
  196.4 2.0 copy-start
  198.4 2.9 copy-start.3
  219.7 5.3 copy-start.23
  222.5 4.5 slice-start
  225.0 2.7 slice-start.1
  227.6 7.6 %copy-start.8 = (bf16[512,1024]{1,0:T(8,128)(2,1)}, bf16[512,1024]{1,0:T(8,128)(2,1)S(1)}, u32[]{:S(2)}) copy-start(bf16[512,1024]{1,0:T(8,128)(2,1)S(1)} %multiply_convert_fusion.6.refs_19_) | copy-start | bytes 3145732
  235.3 8.5 %copy-start.11 = (bf16[512,4096]{1,0:T(8,128)(2,1)}, bf16[512,4096]{1,0:T(8,128)(2,1)S(1)}, u32[]{:S(2)}) copy-start(bf16[512,4096]{1,0:T(8,128)(2,1)S(1)} %get-tuple-element.127.refs_21_) | copy-start | bytes 12582916
  246.7 10.5 %copy-start.9 = (bf16[512,1024]{1,0:T(8,128)(2,1)}, bf16[512,1024]{1,0:T(8,128)(2,1)S(1)}, u32[]{:S(2)}) copy-start(bf16[512,1024]{1,0:T(8,128)(2,1)S(1)} %multiply_convert_fusion.4.refs_22_) | copy-start | bytes 3145732
  257.2 9.0 %copy-start.12 = (bf16[512,4096]{1,0:T(8,128)(2,1)}, bf16[512,4096]{1,0:T(8,128)(2,1)S(1)}, u32[]{:S(2)}) copy-start(bf16[512,4096]{1,0:T(8,128)(2,1)S(1)} %multiply_convert_fusion.refs_20_) | copy-start | bytes 12582916
  268.9 5.3 copy-start.10
  289.6 5.0 copy-start.4
  294.6 2.2 copy-start.1
  298.9 2.2 copy-start.22
  566.0 7.1 %copy-start.18 = (bf16[256,2048]{1,0:T(8,128)(2,1)S(1)}, bf16[256,2048]{1,0:T(8,128)(2,1)}, u32[]{:S(2)}) copy-start(bf16[256,2048]{1,0:T(8,128)(2,1)} %get-tuple-element.72) | copy-start | bytes 3145732
  570.9 3.8 copy-start.17
  574.7 2.2 copy-start.16
  576.9 2.5 copy-start.15
  579.4 2.5 copy-start.14
  581.9 2.5 copy-start.13
  584.4 2.5 copy-start.19
  (2 other events, 2.6 us)
